TPU v7x, 768 devices: a whole 4x8x12 slice. The times are simulated.
768 devices in a mesh: row: 96 (over z, x, y_hi), col: 8 (over y_lo, core).
Axes of the slice: x: 4, y: 8 (y_hi: 2, y_lo: 4; y = y_hi * 4 + y_lo), z: 12, core: 2. Of those that a mesh axis runs over, the one named last changes fastest.
Arguments:
- values: float32 [768, 16, 64, 64], P('row', 'col'), as said below
- radius: int32 [768], replicated, may hold values from 3 to 7, as said below
- branch: int32 [2, 768], replicated, may hold values from 0 to 1
Outputs:
- purified: float32 [768, 16, 64, 64], P('row', 'col')
- traces: float32 [2], replicated
Inputs may be any that keep to these rules, and one draw needn't show every extreme that they name: values is symmetric: the block in slot k of block row I is the transpose of the block in slot 16 - k of block row I + k - 8, and every block outside the pattern is zero. Some block row has radius 3 and some has radius 7.
All inputs are finite; a program needn't handle non-finite values.
Results may differ from a plain program's by a relative error of at most 0.00017.
Values sent between devices are 32-bit elements; how exact they have to be, the bound alone decides.
No kernel may reach another device: no remote copies, remote signals or barrier semaphores. Data moves between devices by JAX's collectives and lax.ppermute only.
A program may use at most 128 MiB of HBM per device.

v0:
```python
import jax
import jax.numpy as jnp
from jax import lax
from jax.sharding import PartitionSpec as P


def with_halo(cells, sides, width):
    for axis, dim in sides:
        count = lax.axis_size(axis)
        ends = count - 1
        head = lax.slice_in_dim(cells, 0, width, axis=dim)
        tail = lax.slice_in_dim(cells, cells.shape[dim] - width, cells.shape[dim], axis=dim)
        cells = jnp.concatenate(
            [
                lax.ppermute(tail, axis, [(i, (i + 1) % count) for i in range(ends)]),
                cells,
                lax.ppermute(head, axis, [((i + 1) % count, i) for i in range(ends)]),
            ],
            axis=dim,
        )
    return cells


def lookup(table, indices):
    entries = jnp.arange(table.shape[0], dtype=jnp.int32)
    hits = indices[..., None] == entries
    return jnp.sum(jnp.where(hits, table, 0), axis=-1)


def pattern_mask(radius, row_ids, slot_ids):
    count = radius.shape[0]
    column = row_ids[:, None] + slot_ids[None, :] - 8
    inside = (column >= 0) & (column < count)
    partner = lookup(radius, jnp.clip(column, 0, count - 1))
    own_reach = lookup(radius, row_ids)[:, None]
    reach = jnp.minimum(own_reach, partner)
    keep = inside & (jnp.abs(slot_ids[None, :] - 8) <= reach)
    return keep.astype(jnp.float32)[:, :, None, None]


def accumulate_panels(stack, first_slot, slot_count, block_rows):
    all_slots = stack.shape[1]
    size = stack.shape[2]
    padded = jnp.pad(stack, ((0, 0), (8, 8), (0, 0), (0, 0)))

    def turn(offset, running):
        base = block_rows + 8 - offset
        upper_blocks = lax.dynamic_slice(stack, (base, offset, 0, 0), (block_rows, 1, size, size))[
            :, 0
        ]
        lower_blocks = lax.dynamic_slice(
            padded, (base, offset + first_slot, 0, 0), (block_rows, slot_count, size, size)
        )
        products = jnp.einsum(
            "qxy,qsxz->qsyz", upper_blocks, lower_blocks, precision=lax.Precision.HIGHEST
        )
        return running + products

    start = jnp.zeros((block_rows, slot_count, size, size), jnp.float32)
    return lax.fori_loop(0, all_slots, turn, start)


def per_device(values, radius, branch):
    block_rows = values.shape[0]
    own_slots = values.shape[1]
    row_index = lax.axis_index("row")
    col_index = lax.axis_index("col")
    first_slot = col_index * own_slots
    slot_ids = first_slot + jnp.arange(own_slots, dtype=jnp.int32)
    row_ids = row_index * block_rows + jnp.arange(block_rows, dtype=jnp.int32)
    pattern = pattern_mask(radius, row_ids, slot_ids)
    count = radius.shape[0]
    columns = jnp.clip(row_ids[:, None] + slot_ids[None, :] - 8, 0, count - 1)
    current = values
    traces = []
    for step_index in range(branch.shape[0]):
        nearby = with_halo(current, (("row", 0),), block_rows)
        whole = lax.all_gather(nearby, "col", axis=1, tiled=True)
        squared = accumulate_panels(whole, first_slot, own_slots, block_rows)
        squared = squared * pattern
        diagonal_part = (
            jnp.trace(squared, axis1=2, axis2=3) * (slot_ids == 8).astype(jnp.float32)[None, :]
        )
        traces.append(lax.psum(jnp.sum(diagonal_part), ("row", "col")))
        flags = branch[step_index]
        pick = lookup(flags, row_ids)[:, None] * lookup(flags, columns)
        current = jnp.where((pick == 1)[:, :, None, None], 2.0 * current - squared, squared)
    return (current, jnp.stack(traces))


def solution(mesh):
    in_specs = (P("row", "col", None, None), P(), P())
    out_specs = (P("row", "col", None, None), P())
    return jax.shard_map(
        per_device, mesh=mesh, in_specs=in_specs, out_specs=out_specs, check_vma=False
    )
```

profile of v0, /device:TPU:1, one launch (start us, length us, event | category | flops | bytes accessed | tf_op | source)
XLA Modules:
  0.0 630.2 jit_solution(13462763671997413565)
XLA Ops:
  8.3 8.3 %collective-permute-start = (f32[8,2,64,64]{3,2,0,1:T(8,128)S(1)}, f32[8,2,64,64]{3,2,0,1:T(8,128)S(1)}, u32[]{:S(2)}, u32[]{:S(2)}) collective-permute-start(f32[8,2,64,64]{3,2,0,1:T(8,128)S(1)} %copy.34), channel_id=1, source_target_pairs={{0,8},{8,16},{16,24},{24,32},{32,40},{40,48},{48,56},{56,64},{64,7... | collective-permute-start | bytes 786440 | tf_op jit(solution)/shard_map/ppermute | solution.py:15
  17.9 33.3 %collective-permute-done = f32[8,2,64,64]{3,2,0,1:T(8,128)S(1)} collective-permute-done((f32[8,2,64,64]{3,2,0,1:T(8,128)S(1)}, f32[8,2,64,64]{3,2,0,1:T(8,128)S(1)}, u32[]{:S(2)}, u32[]{:S(2)}) %collective-permute-start) | collective-permute-done | bytes 262176 | tf_op jit(solution)/shard_map/ppermute | solution.py:15
  51.2 5.6 collective-permute-done.1
  56.8 2.4 pad_maximum_fusion
  62.3 147.6 %all-gather.3.cloned.1.call-done = f32[24,16,64,64]{3,2,0,1:T(8,128)} async-done(((f32[24,2,64,64]{3,2,0,1:T(8,128)}), f32[24,16,64,64]{3,2,0,1:T(8,128)}) %all-gather.3.cloned.1.call-update) | async-done | bytes 6291472 | tf_op jit(solution)/shard_map/all_gather | solution.py:78
  210.0 14.5 %pad.7 = f32[24,32,64,64]{3,2,0,1:T(8,128)} pad(f32[24,16,64,64]{3,2,0,1:T(8,128)} %all-gather.3.cloned.1.call-done, f32[]{:T(128)} %constant.141.clone.1), padding=0_0x8_8x0_0x0_0 | pad | bytes 18874372 | tf_op jit(solution)/shard_map/jit(_pad)/pad | solution.py:44
  224.5 35.8 %while.32 = (s32[]{:T(128)}, f32[8,2,64,64]{2,3,1,0:T(8,128)S(1)}, s32[]{:T(128)}, f32[24,32,64,64]{3,2,0,1:T(8,128)}, f32[24,16,64,64]{3,2,0,1:T(8,128)}, /*ind...) while((s32[]{:T(128)}, f32[8,2,64,64]{2,3,1,0:T(8,128)S(1)}, s32[]{:T(128)}, ...), condition=%wide.region_5.6_spmd.clone, body=%wide.region_4.5_spmd.clone.sunk | while | flops 50462728 | bytes 1313482 | solution.py:60
  260.6 6.8 %collective-permute-start.2 = (f32[8,2,64,64]{3,2,1,0:T(8,128)S(1)}, f32[8,2,64,64]{3,2,1,0:T(8,128)S(1)}, u32[]{:S(2)}, u32[]{:S(2)}) collective-permute-start(f32[8,2,64,64]{3,2,1,0:T(8,128)S(1)} %subtract_select_fusion.1), channel_id=1, source_target_pairs={{0,8},{8,16},{16,24},{24,32},{32,40},{40,48},{48,56},{56,64},{64,7... | collective-permute-start | bytes 786440 | tf_op jit(solution)/shard_map/ppermute | solution.py:15
  268.7 37.4 %collective-permute-done.2 = f32[8,2,64,64]{3,2,1,0:T(8,128)S(1)} collective-permute-done((f32[8,2,64,64]{3,2,1,0:T(8,128)S(1)}, f32[8,2,64,64]{3,2,1,0:T(8,128)S(1)}, u32[]{:S(2)}, u32[]{:S(2)}) %collective-permute-start.2) | collective-permute-done | bytes 262176 | tf_op jit(solution)/shard_map/ppermute | solution.py:15
  308.3 146.8 %all-gather.5.cloned.1.call-done = f32[24,16,64,64]{3,2,1,0:T(8,128)} async-done(((f32[24,2,64,64]{3,2,1,0:T(8,128)}), f32[24,16,64,64]{3,2,1,0:T(8,128)}) %all-gather.5.cloned.1.call-update) | async-done | bytes 6291472 | tf_op jit(solution)/shard_map/all_gather | solution.py:78
  455.1 14.5 %pad.8 = f32[24,32,64,64]{3,2,1,0:T(8,128)} pad(f32[24,16,64,64]{3,2,1,0:T(8,128)} %all-gather.5.cloned.1.call-done, f32[]{:T(128)} %constant.141.clone.1), padding=0_0x8_8x0_0x0_0 | pad | bytes 18874372 | tf_op jit(solution)/shard_map/jit(_pad)/pad | solution.py:44
  469.6 35.8 %while.33 = (s32[]{:T(128)}, f32[8,2,64,64]{2,3,1,0:T(8,128)S(1)}, s32[]{:T(128)}, f32[24,32,64,64]{3,2,1,0:T(8,128)}, f32[24,16,64,64]{3,2,1,0:T(8,128)}, /*ind...) while((s32[]{:T(128)}, f32[8,2,64,64]{2,3,1,0:T(8,128)S(1)}, s32[]{:T(128)}, ...), condition=%wide.region_9.10_spmd.clone, body=%wide.region_8.9_spmd.clone.sunk | while | flops 50462728 | bytes 1313482 | solution.py:60
  471.8 2.2 fusion.23
  474.0 2.2 fusion.23
  476.3 2.2 fusion.23
  478.5 2.2 fusion.23
  480.8 2.2 fusion.23
  487.5 2.2 fusion.23
  489.7 2.2 fusion.23
  494.2 2.2 fusion.23
  496.5 2.2 fusion.23
  500.9 2.2 fusion.23
  503.2 2.2 fusion.23
  507.4 114.2 %all-reduce.2 = (f32[1]{0:T(128)}, f32[1]{0:T(128)}) all-reduce(f32[1]{0:T(128)} %bitcast.1, f32[1]{0:T(128)} %bitcast), channel_id=1, replica_groups=mesh['row'=96,'col'=8] {'row','col'}, use_global_device_ids=true, to_apply=%region_15.16 | all-reduce | flops 2 | bytes 16 | tf_op jit(solution)/shard_map/psum | solution.py:84
  (54 shorter events, 59.3 us)
Async XLA Ops:
  7.2 202.8 %all-gather.3.cloned.1.call-start = ((), (), s32[]{:S(2)}) async-start(), calls=%async_computation | async-start | bytes 14155776 | tf_op jit(solution)/shard_map/all_gather | solution.py:78
  8.3 42.9 %collective-permute-start = (f32[8,2,64,64]{3,2,0,1:T(8,128)S(1)}, f32[8,2,64,64]{3,2,0,1:T(8,128)S(1)}, u32[]{:S(2)}, u32[]{:S(2)}) collective-permute-start(f32[8,2,64,64]{3,2,0,1:T(8,128)S(1)} %copy.34), channel_id=1, source_target_pairs={{0,8},{8,16},{16,24},{24,32},{32,40},{40,48},{48,56},{56,64},{64,7... | collective-permute-start | bytes 786440 | tf_op jit(solution)/shard_map/ppermute | solution.py:15
  16.6 40.2 %collective-permute-start.1 = (f32[8,2,64,64]{3,2,0,1:T(8,128)S(1)}, f32[8,2,64,64]{3,2,0,1:T(8,128)S(1)}, u32[]{:S(2)}, u32[]{:S(2)}) collective-permute-start(f32[8,2,64,64]{3,2,0,1:T(8,128)S(1)} %copy.34), channel_id=1, source_target_pairs={{8,0},{16,8},{24,16},{32,24},{40,32},{48,40},{56,48},{64,56},{72,6... | collective-permute-start | bytes 786440 | tf_op jit(solution)/shard_map/ppermute | solution.py:17
  59.2 395.9 %all-gather.5.cloned.1.call-start = ((), (), s32[]{:S(2)}) async-start(), calls=%async_computation.1 | async-start | bytes 14155776 | tf_op jit(solution)/shard_map/all_gather | solution.py:78
  62.3 198.2 %copy-start = (f32[8,2,64,64]{3,2,1,0:T(8,128)S(1)}, f32[8,2,64,64]{3,2,1,0:T(8,128)}, u32[]{:S(2)}) copy-start(f32[8,2,64,64]{3,2,1,0:T(8,128)} %param.7) | copy-start | bytes 786436
  260.6 45.5 %collective-permute-start.2 = (f32[8,2,64,64]{3,2,1,0:T(8,128)S(1)}, f32[8,2,64,64]{3,2,1,0:T(8,128)S(1)}, u32[]{:S(2)}, u32[]{:S(2)}) collective-permute-start(f32[8,2,64,64]{3,2,1,0:T(8,128)S(1)} %subtract_select_fusion.1), channel_id=1, source_target_pairs={{0,8},{8,16},{16,24},{24,32},{32,40},{40,48},{48,56},{56,64},{64,7... | collective-permute-start | bytes 786440 | tf_op jit(solution)/shard_map/ppermute | solution.py:15
  267.4 39.4 %collective-permute-start.3 = (f32[8,2,64,64]{3,2,1,0:T(8,128)S(1)}, f32[8,2,64,64]{3,2,1,0:T(8,128)S(1)}, u32[]{:S(2)}, u32[]{:S(2)}) collective-permute-start(f32[8,2,64,64]{3,2,1,0:T(8,128)S(1)} %subtract_select_fusion.1), channel_id=1, source_target_pairs={{8,0},{16,8},{24,16},{32,24},{40,32},{48,40},{56,48},{64,56},{72,6... | collective-permute-start | bytes 786440 | tf_op jit(solution)/shard_map/ppermute | solution.py:17
Sparse Core Ops, SparseCore 0:
  59.3 150.5 all-gather.2
  308.3 146.7 all-gather.4
where the time goes:
time: 632 us; the launch traced here: 630 us
  waiting for transfers between devices  372 us (59%)
  blocking collectives  114 us (18%)
  matrix products  70.5 us (11%)
  local copies, waits for them, and re-layouts  31.5 us (5%)
  starting transfers between devices  17.7 us (3%)
  between operations  14.2 us (2%)
  other arithmetic  9.47 us (1%)
    all_gather x2, waiting for transfers between devices, per_device(): whole = lax.all_gather(nearby, 'col', axis=1, tiled=True)  294 us
    psum x1, blocking collectives, per_device(): traces.append(lax.psum(jnp.sum(diagonal_part), ('row', 'col')))  114 us
    ppermute x2, waiting for transfers between devices, with_halo(): lax.ppermute(tail, axis, [(i, (i + 1) % count) for i in range(ends)])  70.7 us
    dot_general x32, matrix products, turn(): jnp.einsum('qxy,qsxz->qsyz', upper_blocks, lower_blocks, precision=lax.Pr...  70.5 us
    pad x2, local copies, waits for them, and re-layouts, accumulate_panels(): padded = jnp.pad(stack, ((0, 0), (8, 8), (0, 0), (0, 0)))  29 us
    ppermute x2, starting transfers between devices, with_halo(): lax.ppermute(tail, axis, [(i, (i + 1) % count) for i in range(ends)])  15.1 us
  transfers between devices with their start and end apart: 6, of which 6 were waited for; matrix products, arithmetic and copies ran while one was open for 0% of the time, Pallas kernels for 0%

commit v1 on v0

v1 whole, which is shorter than its diff:
```python
import jax
import jax.numpy as jnp
from jax import lax
from jax.experimental import pallas as pl
from jax.experimental.pallas import tpu as pltpu
from jax.sharding import PartitionSpec as P

F32 = jnp.float32
BF16 = jnp.bfloat16
B = 64
H = 8
N = H * B
W = 3 * N
HALF = 224
VMEM = pl.BlockSpec(memory_space=pltpu.VMEM)
SMEM = pl.BlockSpec(memory_space=pltpu.SMEM)
RAD, BR = 4, (28, 52)


def params(mib):
    return pltpu.CompilerParams(vmem_limit_bytes=mib << 20)


def halves(x):
    hi = x.astype(BF16)
    return hi, (x - hi.astype(F32)).astype(BF16)


def dot3(a, b, dims):
    (ah, al), (bh, bl) = a, b

    def one(x, y):
        return lax.dot_general(x, y, (dims, ((), ())), preferred_element_type=F32)

    return one(ah, bh) + (one(ah, bl) + one(al, bh))


NN = ((1,), (0,))
NT = ((1,), (1,))


def strip(i):
    return slice(i * B, (i + 1) * B)


def window_vector(s_ref, start):
    block = lax.shift_right_logical(lax.broadcasted_iota(jnp.int32, (1, W), 1), 6)
    out = jnp.zeros((1, W), jnp.int32)
    for w in range(3 * H):
        out = jnp.where(block == w, s_ref[start + w], out)
    return out


def strip_rules(s_ref, radii, flags, i, start):
    block = lax.shift_right_logical(lax.broadcasted_iota(jnp.int32, (1, W), 1), 6)
    reach = jnp.minimum(radii, s_ref[RAD + H + i])
    keep = jnp.abs(block - (H + i)) <= reach
    pick = (flags * s_ref[start + H + i]) == 1
    return keep, pick


def pack_kernel(v_ref, out_ref):
    for i in range(H):
        out_ref[strip(i), :] = jnp.concatenate([v_ref[i, 0], v_ref[i, 1]], axis=1)


def square_kernel(s_ref, *refs):
    packs, (p1_ref, al_ref, au_ref, up_ref, down_ref, tr_ref) = refs[:8], refs[8:14]
    q_ref, r_ref, rh, rl, t_ref = refs[14:]
    yl, core = s_ref[0], s_ref[1]
    for k in range(4):
        for other in range(2):
            place = 2 * ((yl - k) & 3) + (core + other - 2 * core * other)
            q_ref[:, pl.ds(pl.multiple_of(place * 128, 128), 128)] = packs[4 * other + k][...]
    total = jnp.zeros((1, 2 * N), F32)
    for i in range(H):
        own = q_ref[strip(i), :]
        total += jnp.sum(own * own, axis=0, keepdims=True)
        at = i * B
        if i % 2:
            own = pltpu.roll(jnp.concatenate([own, jnp.zeros((B, 128), F32)], axis=1), B, 1)
            at -= B
        parts = [own]
        if at:
            parts.insert(0, jnp.zeros((B, at), F32))
        left = W - at - own.shape[1]
        if left:
            parts.append(jnp.zeros((B, left), F32))
        full = jnp.concatenate(parts, axis=1)
        r_ref[strip(i), :] = full
        rh[strip(i), :], rl[strip(i), :] = halves(full)
    tr_ref[...] = jnp.broadcast_to(jnp.sum(total, axis=1, keepdims=True), tr_ref.shape)

    def part(rows, cols):
        return rh[rows, cols], rl[rows, cols]

    lo, hi = slice(0, 256), slice(256, 512)
    p00 = dot3(part(lo, slice(0, 1280)), part(lo, slice(0, 1280)), NT)
    p01 = dot3(part(lo, slice(256, 1280)), part(hi, slice(256, 1280)), NT)
    p11 = dot3(part(hi, slice(256, W)), part(hi, slice(256, W)), NT)
    p1_ref[lo, lo] = p00
    p1_ref[lo, hi] = p01
    p1_ref[hi, lo] = p01.T
    p1_ref[hi, hi] = p11
    every = slice(0, N)
    mid = slice(N, 2 * N)
    al_ref[lo, :] = dot3(part(lo, mid), part(every, slice(0, N)), NN)
    al_ref[hi, lo] = jnp.zeros((256, 256), F32)
    al_ref[hi, hi] = dot3(part(hi, mid), part(every, slice(256, N)), NN)
    au_ref[lo, lo] = dot3(part(lo, mid), part(every, slice(2 * N, 2 * N + 256)), NN)
    au_ref[lo, hi] = jnp.zeros((256, 256), F32)
    au_ref[hi, :] = dot3(part(hi, mid), part(every, slice(2 * N, W)), NN)

    lane = lax.broadcasted_iota(jnp.int32, (B, 256), 1)
    mine = pl.ds(pl.multiple_of(core * HALF, 8), HALF)
    t_ref[lo, :] = au_ref[hi, lo]
    for a in range(1, 4):
        turned = pltpu.roll(au_ref[strip(H - a), hi], a * B, 1)
        t_ref[strip(3 + a), :] = jnp.where(lane < a * B, au_ref[strip(a), lo], turned)
    up_ref[...] = t_ref[mine, :]
    t_ref[lo, :] = al_ref[lo, hi]
    for a in range(3):
        turned = pltpu.roll(al_ref[strip(6 - a), hi], (a + 1) * B, 1)
        t_ref[strip(4 + a), :] = jnp.where(lane >= (a + 1) * B, al_ref[strip(a), lo], turned)
    down_ref[...] = t_ref[mine, :]

    radii = window_vector(s_ref, RAD)
    flags = window_vector(s_ref, BR[0])
    for i in range(H):
        keep, pick = strip_rules(s_ref, radii, flags, i, BR[0])
        for ref, at in ((al_ref, 0), (p1_ref, N), (au_ref, 2 * N)):
            span = slice(at, at + N)
            squared = jnp.where(keep[:, span], ref[strip(i), :], 0.0)
            ref[strip(i), :] = jnp.where(
                pick[:, span], 2.0 * r_ref[strip(i), span] - squared, squared
            )


def second_kernel(s_ref, p1_ref, al_ref, au_ref, tr_ref, ua, ub, da, db,
                  own_ref, part_ref, x1_ref, sums_ref, t_ref, z_ref, r_ref, mh, ml):
    core, col = s_ref[1], s_ref[2]
    lo, hi = slice(0, 256), slice(256, 512)
    lane = lax.broadcasted_iota(jnp.int32, (B, 256), 1)
    mine = pl.ds(pl.multiple_of(core * HALF, 8), HALF)
    theirs = pl.ds(pl.multiple_of((1 - core) * HALF, 8), HALF)
    nothing = jnp.zeros((256, 256), F32)
    zero = jnp.zeros((B, 256), F32)

    radii = window_vector(s_ref, RAD)
    flags = window_vector(s_ref, BR[0])

    t_ref[mine, :] = ua[...]
    t_ref[theirs, :] = ub[...]
    z_ref[lo, hi] = t_ref[lo, :].T
    z_ref[hi, lo] = nothing
    first = [zero]
    last = [zero]
    for a in range(1, 4):
        first.append(jnp.where(lane < a * B, t_ref[strip(3 + a), :], 0.0))
        turned = pltpu.roll(t_ref[strip(7 - a), :], a * B, 1)
        last.append(jnp.where(lane < a * B, turned, 0.0))
    z_ref[lo, lo] = jnp.concatenate(first, axis=0).T
    z_ref[hi, hi] = jnp.concatenate(last, axis=0).T
    square2 = jnp.zeros((1, N), F32)
    square1 = jnp.zeros((1, N), F32)
    for i in range(H):
        keep, pick = strip_rules(s_ref, radii, flags, i, BR[0])
        span = slice(0, N)
        add = jnp.where(keep[:, span], z_ref[strip(i), :], 0.0)
        new = al_ref[strip(i), :] + jnp.where(pick[:, span], -add, add)
        r_ref[strip(i), span] = new
        square2 += jnp.sum(new * new, axis=0, keepdims=True)
        inner = p1_ref[strip(i), :]
        r_ref[strip(i), N : 2 * N] = inner
        square1 += jnp.sum(inner * inner, axis=0, keepdims=True)
    t_ref[mine, :] = da[...]
    t_ref[theirs, :] = db[...]
    z_ref[lo, hi] = nothing
    z_ref[hi, lo] = t_ref[lo, :].T
    first = []
    last = []
    for a in range(3):
        first.append(jnp.where(lane >= (a + 1) * B, t_ref[strip(4 + a), :], 0.0))
        turned = pltpu.roll(t_ref[strip(6 - a), :], (a + 1) * B, 1)
        last.append(jnp.where(lane >= (a + 1) * B, turned, 0.0))
    z_ref[lo, lo] = jnp.concatenate(first + [zero], axis=0).T
    z_ref[hi, hi] = jnp.concatenate(last + [zero], axis=0).T
    for i in range(H):
        keep, pick = strip_rules(s_ref, radii, flags, i, BR[0])
        span = slice(2 * N, W)
        add = jnp.where(keep[:, span], z_ref[strip(i), :], 0.0)
        r_ref[strip(i), span] = au_ref[strip(i), :] + jnp.where(pick[:, span], -add, add)

    outer = jnp.sum(square1 + 2.0 * square2, axis=1, keepdims=True)
    spot = lax.broadcasted_iota(jnp.int32, (1, 128), 1)
    both = jnp.where(spot == 0, tr_ref[...], jnp.where(spot == 1, outer, 0.0))
    sums_ref[...] = jnp.broadcast_to(both, sums_ref.shape)

    blank = jnp.zeros((N, N), BF16)
    for ref in (mh, ml):
        for rows in (slice(0, N), slice(2 * N, W)):
            ref[rows, 0:N] = blank
            ref[rows, 2 * N : W] = blank
    mid = slice(N, 2 * N)
    for i in range(H):
        rows = slice(N + i * B, N + (i + 1) * B)
        mh[rows, :], ml[rows, :] = halves(r_ref[strip(i), :])
    mh[0:N, mid], ml[0:N, mid] = halves(r_ref[:, 0:N].T)
    mh[2 * N : W, mid], ml[2 * N : W, mid] = halves(r_ref[:, 2 * N : W].T)

    upper = (col >= 4).astype(jnp.int32)
    wide = lax.broadcasted_iota(jnp.int32, (B, 128), 1) >= B
    for i in range(H):
        rows = slice(N + i * B, N + (i + 1) * B)
        pair = pl.ds(pl.multiple_of((i + 2 * col) * B, B), 128)
        own_ref[strip(i), :] = dot3((mh[rows, :], ml[rows, :]), (mh[pair, :], ml[pair, :]), NT)
        begin = (i - i % 2 + 2 * col) * B
        if i % 2:
            held = r_ref[strip(i), pl.ds(pl.multiple_of(begin, 128), 256)]
            x1_ref[strip(i), :] = held[:, B : B + 128]
        else:
            x1_ref[strip(i), :] = r_ref[strip(i), pl.ds(pl.multiple_of(begin, 128), 128)]
        there = pl.ds(pl.multiple_of((16 * upper + i) * B, B), B)
        block = i + 6 - 2 * col + 16 * upper
        pair = pl.ds(pl.multiple_of(block * B, B), 128)
        share = dot3((mh[there, mid], ml[there, mid]), (mh[pair, mid], ml[pair, mid]), NT)
        index = block + wide.astype(jnp.int32)
        part_ref[strip(i), :] = jnp.where((index >= H) & (index < 2 * H), share, 0.0)


def last_kernel(s_ref, own_ref, part_ref, x1_ref, out_ref):
    col = s_ref[2]
    wide = lax.broadcasted_iota(jnp.int32, (B, 128), 1) >= B
    for i in range(H):
        squared = own_ref[strip(i), :] + part_ref[strip(i), :]
        keep, pick = [], []
        for h in range(2):
            far = jnp.abs(2 * col + h - H)
            reach = jnp.minimum(s_ref[RAD + H + i], s_ref[RAD + i + 2 * col + h])
            keep.append((far <= reach).astype(F32))
            pick.append((s_ref[BR[1] + H + i] * s_ref[BR[1] + i + 2 * col + h]).astype(F32))
        squared = squared * jnp.where(wide, keep[1], keep[0])
        chosen = jnp.where(wide, pick[1], pick[0]) == 1.0
        new = jnp.where(chosen, 2.0 * x1_ref[strip(i), :] - squared, squared)
        out_ref[i, 0] = new[:, :B]
        out_ref[i, 1] = new[:, B:]


def shape(*dims):
    return jax.ShapeDtypeStruct(dims, F32)


def cost(flops, moved):
    return pl.CostEstimate(flops=flops, bytes_accessed=moved, transcendentals=0)


def per_device(rows, values, radius, branch):
    both = ("row", "col")
    row, col = lax.axis_index("row"), lax.axis_index("col")
    pad = ((H, H),)
    radii = lax.dynamic_slice(jnp.pad(radius, pad, constant_values=-1), (H * row,), (3 * H,))
    flags = lax.dynamic_slice(jnp.pad(branch, ((0, 0),) + pad), (0, H * row), (2, 3 * H))
    scalars = jnp.concatenate(
        [jnp.stack([col // 2, col % 2, col, row]).astype(jnp.int32), radii, flags[0], flags[1]]
    )

    def swap(x):
        return lax.ppermute(x, "col", [(c, c ^ 1) for c in range(8)])

    def to_rows(x, pairs):
        return lax.ppermute(x, both, pairs)

    packed = pl.pallas_call(
        pack_kernel, out_shape=shape(N, 128), in_specs=[VMEM], out_specs=VMEM, name="pack",
        compiler_params=params(16),
    )(values)
    mine = [packed] + [
        lax.ppermute(packed, "col", [(c, (c + 2 * k) % 8) for c in range(8)]) for k in (1, 2, 3)
    ]
    others = [swap(x) for x in mine]

    inner, left, right, up, down, trace = pl.pallas_call(
        square_kernel,
        out_shape=[shape(N, N)] * 3 + [shape(HALF, 256)] * 2 + [shape(1, 128)],
        in_specs=[SMEM] + [VMEM] * 8,
        out_specs=[VMEM] * 6,
        scratch_shapes=[
            pltpu.VMEM((N, 2 * N), F32),
            pltpu.VMEM((N, W), F32),
            pltpu.VMEM((N, W), BF16),
            pltpu.VMEM((N, W), BF16),
            pltpu.VMEM((2 * HALF, 256), F32),
        ],
        compiler_params=params(48),
        name="square",
    )(scalars, *mine, *others)

    def index(r, c):
        return r * 8 + c

    def mirror(c):
        return 2 * (3 - c // 2) + c % 2

    ends = [(r, c) for r in range(rows - 1) for c in range(8)]
    ua = to_rows(up, [(index(r, c), index(r + 1, mirror(c))) for r, c in ends])
    da = to_rows(down, [(index(r + 1, c), index(r, mirror(c))) for r, c in ends])
    ub, db = swap(ua), swap(da)

    own, part, x1, sums = pl.pallas_call(
        second_kernel,
        out_shape=[shape(N, 128)] * 3 + [shape(rows, 128)],
        in_specs=[SMEM] + [VMEM] * 8,
        out_specs=[VMEM] * 4,
        scratch_shapes=[
            pltpu.VMEM((2 * HALF, 256), F32),
            pltpu.VMEM((N, N), F32),
            pltpu.VMEM((N, W), F32),
            pltpu.VMEM((W, W), BF16),
            pltpu.VMEM((W, W), BF16),
        ],
        compiler_params=params(48),
        name="second",
    )(scalars, inner, left, right, trace, ua, ub, da, db)

    pairs = [(index(r, c), index(r + 1, 7 - c)) for r, c in ends if c >= 4]
    pairs += [(index(r + 1, c), index(r, 7 - c)) for r, c in ends if c < 4]
    part = to_rows(part, pairs)
    sums = lax.all_to_all(sums, "row", 0, 0, tiled=True)
    purified = pl.pallas_call(
        last_kernel,
        out_shape=shape(H, 2, B, B),
        in_specs=[SMEM] + [VMEM] * 3,
        out_specs=VMEM,
        compiler_params=params(16),
        name="last",
    )(scalars, own, part, x1)
    return purified, jnp.sum(sums, axis=0)[:2]


def solution(mesh):
    rows = mesh.shape["row"]

    def run(values, radius, branch):
        return per_device(rows, values, radius, branch)

    in_specs = (P("row", "col", None, None), P(), P())
    out_specs = (P("row", "col", None, None), P())
    return jax.shard_map(
        run, mesh=mesh, in_specs=in_specs, out_specs=out_specs, check_vma=False
    )
```

time: 632 us -> 119 us (0.19)
  waiting for transfers between devices: 372 us -> 26.1 us
  blocking collectives: 114 us -> 39.4 us
  matrix products: 70.5 us -> 0 us
  local copies, waits for them, and re-layouts: 31.5 us -> 1.96 us
  starting transfers between devices: 17.7 us -> 37.6 us
  between operations: 14.2 us -> 0.82 us
  Pallas kernels: 0 us -> 12.3 us
  other arithmetic: 9.47 us -> 0.63 us
    all_gather x2 -> x0, waiting for transfers between devices: 294 us -> none  [per_device(): whole = lax.all_gather(nearby, 'col', axis=1, tiled=True)]
    psum x1 -> x0, blocking collectives: 114 us -> none  [per_device(): traces.append(lax.psum(jnp.sum(diagonal_part), ('row', 'col')))]
    dot_general x32 -> x0, matrix products: 70.5 us -> none  [turn(): jnp.einsum('qxy,qsxz->qsyz', upper_blocks, lower_blocks, precision=lax.Pr...]
    ppermute x4 -> x12, waiting for transfers between devices: 77.1 us -> 26.1 us  [the longest x3 20.5 us: to_rows(): return lax.ppermute(x, both, pairs)]
    all_to_all x0 -> x1, blocking collectives: none -> 39.4 us  [per_device(): sums = lax.all_to_all(sums, 'row', 0, 0, tiled=True)]
    pad x2 -> x0, local copies, waits for them, and re-layouts: 29 us -> none  [accumulate_panels(): padded = jnp.pad(stack, ((0, 0), (8, 8), (0, 0), (0, 0)))]
    ppermute x4 -> x12, starting transfers between devices: 17.7 us -> 37.6 us  [the longest x6 24 us: swap(): return lax.ppermute(x, 'col', [(c, c ^ 1) for c in range(8)])]
    pallas_call x0 -> x4, Pallas kernels: none -> 12.3 us  [the longest x1 6.77 us: per_device(): pl.pallas_call(second_kernel, out_shape=[shape(N, 128)] * 3 + [shape(rows...]
  transfers between devices with their start and end apart: 6 -> 12, of which waited for: 6 -> 5; matrix products, arithmetic and copies ran while one was open for 0% -> 1% of each run, Pallas kernels for 0% -> 0%
where the time goes in v1:
time: 119 us
  blocking collectives  39.4 us (33%)
  starting transfers between devices  37.6 us (32%)
  waiting for transfers between devices  26.1 us (22%)
  Pallas kernels  12.3 us (10%)
  local copies, waits for them, and re-layouts  1.96 us (2%)
    all_to_all x1, blocking collectives, per_device(): sums = lax.all_to_all(sums, 'row', 0, 0, tiled=True)  39.4 us
    ppermute x6, starting transfers between devices, swap(): return lax.ppermute(x, 'col', [(c, c ^ 1) for c in range(8)])  24 us
    ppermute x3, waiting for transfers between devices, to_rows(): return lax.ppermute(x, both, pairs)  20.5 us
    ppermute x3, starting transfers between devices, per_device(): lax.ppermute(packed, 'col', [(c, (c + 2 * k) % 8) for c in range(8)])  10.3 us
    pallas_call x1, Pallas kernels, per_device(): pl.pallas_call(second_kernel, out_shape=[shape(N, 128)] * 3 + [shape(rows...  6.77 us
    pallas_call x1, Pallas kernels, per_device(): pl.pallas_call(square_kernel, out_shape=[shape(N, N)] * 3 + [shape(HALF,...  3.96 us
    ppermute x3, starting transfers between devices, to_rows(): return lax.ppermute(x, both, pairs)  3.28 us
    ppermute x3, waiting for transfers between devices, per_device(): lax.ppermute(packed, 'col', [(c, (c + 2 * k) % 8) for c in range(8)])  3.18 us
  transfers between devices with their start and end apart: 12, of which 5 were waited for; matrix products, arithmetic and copies ran while one was open for 1% of the time, Pallas kernels for 0%

profile of v1, /device:TPU:1, one launch (start us, length us, event | category | flops | bytes accessed | tf_op | source)
XLA Modules:
  0.0 118.8 jit_solution(6786684508753484474)
XLA Ops:
  0.6 1.0 copy-done
  1.8 6.1 %collective-permute-start.2 = (f32[512,128]{1,0:T(8,128)S(1)}, f32[512,128]{1,0:T(8,128)S(1)}, u32[]{:S(2)}, u32[]{:S(2)}) collective-permute-start(f32[512,128]{1,0:T(8,128)S(1)} %pack.1.refs_0_), channel_id=1, source_target_pairs={{0,6},{1,7},{2,0},{3,1},{4,2},{5,3},{6,4},{7,5},{8,14},{9,15},{10,... | collective-permute-start | bytes 786440 | tf_op jit(solution)/shard_map/ppermute | solution.py:278
  7.9 1.9 %collective-permute-start.1 = (f32[512,128]{1,0:T(8,128)S(1)}, f32[512,128]{1,0:T(8,128)S(1)}, u32[]{:S(2)}, u32[]{:S(2)}) collective-permute-start(f32[512,128]{1,0:T(8,128)S(1)} %pack.1.refs_0_), channel_id=1, source_target_pairs={{0,4},{1,5},{2,6},{3,7},{4,0},{5,1},{6,2},{7,3},{8,12},{9,13},{10,... | collective-permute-start | bytes 786440 | tf_op jit(solution)/shard_map/ppermute | solution.py:278
  9.8 2.3 %collective-permute-start = (f32[512,128]{1,0:T(8,128)S(1)}, f32[512,128]{1,0:T(8,128)S(1)}, u32[]{:S(2)}, u32[]{:S(2)}) collective-permute-start(f32[512,128]{1,0:T(8,128)S(1)} %pack.1.refs_0_), channel_id=1, source_target_pairs={{0,2},{1,3},{2,4},{3,5},{4,6},{5,7},{6,0},{7,1},{8,10},{9,11},{10,... | collective-permute-start | bytes 786440 | tf_op jit(solution)/shard_map/ppermute | solution.py:278
  12.2 9.9 %collective-permute-start.3 = (f32[512,128]{1,0:T(8,128)S(1)}, f32[512,128]{1,0:T(8,128)S(1)}, u32[]{:S(2)}, u32[]{:S(2)}) collective-permute-start(f32[512,128]{1,0:T(8,128)S(1)} %pack.1.refs_0_), channel_id=1, source_target_pairs={{0,1},{1,0},{2,3},{3,2},{4,5},{5,4},{6,7},{7,6},{8,9},{9,8},{10,11... | collective-permute-start | bytes 786440 | tf_op jit(solution)/shard_map/ppermute | solution.py:268
  22.1 0.7 copy-done.1
  22.8 3.6 %collective-permute-start.6 = (f32[512,128]{1,0:T(8,128)S(1)}, f32[512,128]{1,0:T(8,128)S(1)}, u32[]{:S(2)}, u32[]{:S(2)}) collective-permute-start(f32[512,128]{1,0:T(8,128)S(1)} %collective-permute-done.2.refs_3_), channel_id=1, source_target_pairs={{0,1},{1,0},{2,3},{3,2},{4,5},{5,4},{6,7},{7,6},{8,9},{9,8},{10,11... | collective-permute-start | bytes 786440 | tf_op jit(solution)/shard_map/ppermute | solution.py:268
  26.4 3.2 %collective-permute-done.1.refs_2_ = f32[512,128]{1,0:T(8,128)S(1)} collective-permute-done((f32[512,128]{1,0:T(8,128)S(1)}, f32[512,128]{1,0:T(8,128)S(1)}, u32[]{:S(2)}, u32[]{:S(2)}) %collective-permute-start.1) | collective-permute-done | bytes 262176 | tf_op jit(solution)/shard_map/ppermute | solution.py:278
  29.6 3.5 %collective-permute-start.5 = (f32[512,128]{1,0:T(8,128)S(1)}, f32[512,128]{1,0:T(8,128)S(1)}, u32[]{:S(2)}, u32[]{:S(2)}) collective-permute-start(f32[512,128]{1,0:T(8,128)S(1)} %collective-permute-done.1.refs_2_), channel_id=1, source_target_pairs={{0,1},{1,0},{2,3},{3,2},{4,5},{5,4},{6,7},{7,6},{8,9},{9,8},{10,11... | collective-permute-start | bytes 786440 | tf_op jit(solution)/shard_map/ppermute | solution.py:268
  33.1 1.9 %collective-permute-start.4 = (f32[512,128]{1,0:T(8,128)S(1)}, f32[512,128]{1,0:T(8,128)S(1)}, u32[]{:S(2)}, u32[]{:S(2)}) collective-permute-start(f32[512,128]{1,0:T(8,128)S(1)} %collective-permute-done.refs_1_), channel_id=1, source_target_pairs={{0,1},{1,0},{2,3},{3,2},{4,5},{5,4},{6,7},{7,6},{8,9},{9,8},{10,11... | collective-permute-start | bytes 786440 | tf_op jit(solution)/shard_map/ppermute | solution.py:268
  35.2 1.3 %collective-permute-done.4.refs_5_ = f32[512,128]{1,0:T(8,128)S(1)} collective-permute-done((f32[512,128]{1,0:T(8,128)S(1)}, f32[512,128]{1,0:T(8,128)S(1)}, u32[]{:S(2)}, u32[]{:S(2)}) %collective-permute-start.4) | collective-permute-done | bytes 262176 | tf_op jit(solution)/shard_map/ppermute | solution.py:268
  36.5 4.0 %square.1 = (f32[512,512]{1,0:T(8,128)S(1)}, f32[512,512]{1,0:T(8,128)S(1)}, f32[512,512]{1,0:T(8,128)S(1)}, f32[224,256]{1,0:T(8,128)S(1)}, f32[224,256]{1,0:T(8,128)S(1)}, /*index=5*/f32[1,128]{1,0:T(1,128)S(1)}) custom-call(s32[76]{0:T(128)S(1)} %concatenate.3.s_ref, f32[512,128]{1,0:T(8,128)S(1)} %pack.1.refs_0_, ...), custom_call_target="tpu_custom_call" | custom-call | tf_op jit(solution)/shard_map/square/pallas_call | solution.py:282
  40.5 1.3 %collective-permute-start.7 = (f32[224,256]{1,0:T(8,128)S(1)}, f32[224,256]{1,0:T(8,128)S(1)}, u32[]{:S(2)}, u32[]{:S(2)}) collective-permute-start(f32[224,256]{1,0:T(8,128)S(1)} %get-tuple-element.16), channel_id=1, source_target_pairs={{0,14},{1,15},{2,12},{3,13},{4,10},{5,11},{6,8},{7,9},{8,22},{9,23... | collective-permute-start | bytes 688136 | tf_op jit(solution)/shard_map/ppermute | solution.py:271
  41.8 1.3 %collective-permute-start.9 = (f32[224,256]{1,0:T(8,128)S(1)}, f32[224,256]{1,0:T(8,128)S(1)}, u32[]{:S(2)}, u32[]{:S(2)}) collective-permute-start(f32[224,256]{1,0:T(8,128)S(1)} %get-tuple-element.17), channel_id=1, source_target_pairs={{8,6},{9,7},{10,4},{11,5},{12,2},{13,3},{14,0},{15,1},{16,14},{17,... | collective-permute-start | bytes 688136 | tf_op jit(solution)/shard_map/ppermute | solution.py:271
  43.1 8.5 %collective-permute-done.7.ua = f32[224,256]{1,0:T(8,128)S(1)} collective-permute-done((f32[224,256]{1,0:T(8,128)S(1)}, f32[224,256]{1,0:T(8,128)S(1)}, u32[]{:S(2)}, u32[]{:S(2)}) %collective-permute-start.7) | collective-permute-done | bytes 229408 | tf_op jit(solution)/shard_map/ppermute | solution.py:271
  51.6 2.8 %collective-permute-start.8 = (f32[224,256]{1,0:T(8,128)S(1)}, f32[224,256]{1,0:T(8,128)S(1)}, u32[]{:S(2)}, u32[]{:S(2)}) collective-permute-start(f32[224,256]{1,0:T(8,128)S(1)} %collective-permute-done.7.ua), channel_id=1, source_target_pairs={{0,1},{1,0},{2,3},{3,2},{4,5},{5,4},{6,7},{7,6},{8,9},{9,8},{10,11... | collective-permute-start | bytes 688136 | tf_op jit(solution)/shard_map/ppermute | solution.py:268
  54.4 12.0 %collective-permute-done.9.da = f32[224,256]{1,0:T(8,128)S(1)} collective-permute-done((f32[224,256]{1,0:T(8,128)S(1)}, f32[224,256]{1,0:T(8,128)S(1)}, u32[]{:S(2)}, u32[]{:S(2)}) %collective-permute-start.9) | collective-permute-done | bytes 229408 | tf_op jit(solution)/shard_map/ppermute | solution.py:271
  66.4 2.4 %collective-permute-start.10 = (f32[224,256]{1,0:T(8,128)S(1)}, f32[224,256]{1,0:T(8,128)S(1)}, u32[]{:S(2)}, u32[]{:S(2)}) collective-permute-start(f32[224,256]{1,0:T(8,128)S(1)} %collective-permute-done.9.da), channel_id=1, source_target_pairs={{0,1},{1,0},{2,3},{3,2},{4,5},{5,4},{6,7},{7,6},{8,9},{9,8},{10,11... | collective-permute-start | bytes 688136 | tf_op jit(solution)/shard_map/ppermute | solution.py:268
  68.7 1.1 collective-permute-done.10.db
  69.8 6.8 %second.1 = (f32[512,128]{1,0:T(8,128)S(1)}, f32[512,128]{1,0:T(8,128)S(1)}, f32[512,128]{1,0:T(8,128)S(1)}, f32[96,128]{1,0:T(8,128)S(1)}) custom-call(s32[76]{0:T(128)S(1)} %concatenate.3.s_ref, f32[512,512]{1,0:T(8,128)S(1)} %get-tuple-element.12.p1_ref, f32[512,512]{1,0:T(8,128)S(1)} %get-tuple-element.13.al_ref, ...), custom_call_target="tpu_custom_call" | custom-call | tf_op jit(solution)/shard_map/second/pallas_call | solution.py:309
  76.6 0.7 collective-permute-start.11
  77.3 39.4 %all_to_all.9 = f32[96,1,128]{2,1,0:T(1,128)S(1)} all-to-all(f32[96,1,128]{2,1,0:T(1,128)S(1)} %bitcast.12), channel_id=1, replica_groups=mesh['row'=96,'col'=8] {'row'}, dimensions={0} | all-to-all | bytes 98304 | tf_op jit(solution)/shard_map/all_to_all | solution.py:328
  116.7 0.6 reduce_sum.9
  117.4 1.5 %last.1 = f32[8,2,64,64]{3,2,1,0:T(8,128)} custom-call(s32[76]{0:T(128)S(1)} %concatenate.3.s_ref, f32[512,128]{1,0:T(8,128)S(1)} %get-tuple-element.18.own_ref, f32[512,128]{1,0:T(8,128)S(1)} %collective-permute-done.11.part_ref, f32[512,128]{1,0:T(8,128)S(1)} %get-tuple-element.20.x1_ref), custom_call_target="tpu_custom_call" | custom-call | tf_op jit(solution)/shard_map/last/pallas_call | solution.py:329
  (16 shorter events, 0.4 us)
Async XLA Ops:
  0.6 1.0 copy-start
  1.8 21.0 %collective-permute-start.2 = (f32[512,128]{1,0:T(8,128)S(1)}, f32[512,128]{1,0:T(8,128)S(1)}, u32[]{:S(2)}, u32[]{:S(2)}) collective-permute-start(f32[512,128]{1,0:T(8,128)S(1)} %pack.1.refs_0_), channel_id=1, source_target_pairs={{0,6},{1,7},{2,0},{3,1},{4,2},{5,3},{6,4},{7,5},{8,14},{9,15},{10,... | collective-permute-start | bytes 786440 | tf_op jit(solution)/shard_map/ppermute | solution.py:278
  7.9 21.7 %collective-permute-start.1 = (f32[512,128]{1,0:T(8,128)S(1)}, f32[512,128]{1,0:T(8,128)S(1)}, u32[]{:S(2)}, u32[]{:S(2)}) collective-permute-start(f32[512,128]{1,0:T(8,128)S(1)} %pack.1.refs_0_), channel_id=1, source_target_pairs={{0,4},{1,5},{2,6},{3,7},{4,0},{5,1},{6,2},{7,3},{8,12},{9,13},{10,... | collective-permute-start | bytes 786440 | tf_op jit(solution)/shard_map/ppermute | solution.py:278
  9.8 23.3 %collective-permute-start = (f32[512,128]{1,0:T(8,128)S(1)}, f32[512,128]{1,0:T(8,128)S(1)}, u32[]{:S(2)}, u32[]{:S(2)}) collective-permute-start(f32[512,128]{1,0:T(8,128)S(1)} %pack.1.refs_0_), channel_id=1, source_target_pairs={{0,2},{1,3},{2,4},{3,5},{4,6},{5,7},{6,0},{7,1},{8,10},{9,11},{10,... | collective-permute-start | bytes 786440 | tf_op jit(solution)/shard_map/ppermute | solution.py:278
  12.2 23.0 %collective-permute-start.3 = (f32[512,128]{1,0:T(8,128)S(1)}, f32[512,128]{1,0:T(8,128)S(1)}, u32[]{:S(2)}, u32[]{:S(2)}) collective-permute-start(f32[512,128]{1,0:T(8,128)S(1)} %pack.1.refs_0_), channel_id=1, source_target_pairs={{0,1},{1,0},{2,3},{3,2},{4,5},{5,4},{6,7},{7,6},{8,9},{9,8},{10,11... | collective-permute-start | bytes 786440 | tf_op jit(solution)/shard_map/ppermute | solution.py:268
  22.0 0.7 copy-start.1
  22.7 12.3 %copy-start.2 = (s32[768]{0:T(1024)S(1)}, s32[768]{0:T(1024)}, u32[]{:S(2)}) copy-start(s32[768]{0:T(1024)} %param.4) | copy-start | bytes 9220
  22.8 12.4 %collective-permute-start.6 = (f32[512,128]{1,0:T(8,128)S(1)}, f32[512,128]{1,0:T(8,128)S(1)}, u32[]{:S(2)}, u32[]{:S(2)}) collective-permute-start(f32[512,128]{1,0:T(8,128)S(1)} %collective-permute-done.2.refs_3_), channel_id=1, source_target_pairs={{0,1},{1,0},{2,3},{3,2},{4,5},{5,4},{6,7},{7,6},{8,9},{9,8},{10,11... | collective-permute-start | bytes 786440 | tf_op jit(solution)/shard_map/ppermute | solution.py:268
  29.6 5.6 %collective-permute-start.5 = (f32[512,128]{1,0:T(8,128)S(1)}, f32[512,128]{1,0:T(8,128)S(1)}, u32[]{:S(2)}, u32[]{:S(2)}) collective-permute-start(f32[512,128]{1,0:T(8,128)S(1)} %collective-permute-done.1.refs_2_), channel_id=1, source_target_pairs={{0,1},{1,0},{2,3},{3,2},{4,5},{5,4},{6,7},{7,6},{8,9},{9,8},{10,11... | collective-permute-start | bytes 786440 | tf_op jit(solution)/shard_map/ppermute | solution.py:268
  33.1 3.4 %collective-permute-start.4 = (f32[512,128]{1,0:T(8,128)S(1)}, f32[512,128]{1,0:T(8,128)S(1)}, u32[]{:S(2)}, u32[]{:S(2)}) collective-permute-start(f32[512,128]{1,0:T(8,128)S(1)} %collective-permute-done.refs_1_), channel_id=1, source_target_pairs={{0,1},{1,0},{2,3},{3,2},{4,5},{5,4},{6,7},{7,6},{8,9},{9,8},{10,11... | collective-permute-start | bytes 786440 | tf_op jit(solution)/shard_map/ppermute | solution.py:268
  40.5 11.2 %collective-permute-start.7 = (f32[224,256]{1,0:T(8,128)S(1)}, f32[224,256]{1,0:T(8,128)S(1)}, u32[]{:S(2)}, u32[]{:S(2)}) collective-permute-start(f32[224,256]{1,0:T(8,128)S(1)} %get-tuple-element.16), channel_id=1, source_target_pairs={{0,14},{1,15},{2,12},{3,13},{4,10},{5,11},{6,8},{7,9},{8,22},{9,23... | collective-permute-start | bytes 688136 | tf_op jit(solution)/shard_map/ppermute | solution.py:271
  41.8 24.6 %collective-permute-start.9 = (f32[224,256]{1,0:T(8,128)S(1)}, f32[224,256]{1,0:T(8,128)S(1)}, u32[]{:S(2)}, u32[]{:S(2)}) collective-permute-start(f32[224,256]{1,0:T(8,128)S(1)} %get-tuple-element.17), channel_id=1, source_target_pairs={{8,6},{9,7},{10,4},{11,5},{12,2},{13,3},{14,0},{15,1},{16,14},{17,... | collective-permute-start | bytes 688136 | tf_op jit(solution)/shard_map/ppermute | solution.py:271
  51.6 17.1 %collective-permute-start.8 = (f32[224,256]{1,0:T(8,128)S(1)}, f32[224,256]{1,0:T(8,128)S(1)}, u32[]{:S(2)}, u32[]{:S(2)}) collective-permute-start(f32[224,256]{1,0:T(8,128)S(1)} %collective-permute-done.7.ua), channel_id=1, source_target_pairs={{0,1},{1,0},{2,3},{3,2},{4,5},{5,4},{6,7},{7,6},{8,9},{9,8},{10,11... | collective-permute-start | bytes 688136 | tf_op jit(solution)/shard_map/ppermute | solution.py:268
  66.4 3.5 %collective-permute-start.10 = (f32[224,256]{1,0:T(8,128)S(1)}, f32[224,256]{1,0:T(8,128)S(1)}, u32[]{:S(2)}, u32[]{:S(2)}) collective-permute-start(f32[224,256]{1,0:T(8,128)S(1)} %collective-permute-done.9.da), channel_id=1, source_target_pairs={{0,1},{1,0},{2,3},{3,2},{4,5},{5,4},{6,7},{7,6},{8,9},{9,8},{10,11... | collective-permute-start | bytes 688136 | tf_op jit(solution)/shard_map/ppermute | solution.py:268
  76.6 40.8 %collective-permute-start.11 = (f32[512,128]{1,0:T(8,128)S(1)}, f32[512,128]{1,0:T(8,128)S(1)}, u32[]{:S(2)}, u32[]{:S(2)}) collective-permute-start(f32[512,128]{1,0:T(8,128)S(1)} %get-tuple-element.19), channel_id=1, source_target_pairs={{4,11},{5,10},{6,9},{7,8},{12,19},{13,18},{14,17},{15,16},{20,27},... | collective-permute-start | bytes 786440 | tf_op jit(solution)/shard_map/ppermute | solution.py:271

commit v2 on v1

v2 whole, which is shorter than its diff:
```python
import jax
import jax.numpy as jnp
from jax import lax
from jax.experimental import pallas as pl
from jax.experimental.pallas import tpu as pltpu
from jax.sharding import PartitionSpec as P

F32 = jnp.float32
BF16 = jnp.bfloat16
B = 64
H = 8
N = H * B
W = 3 * N
HALF = 224
VMEM = pl.BlockSpec(memory_space=pltpu.VMEM)
SMEM = pl.BlockSpec(memory_space=pltpu.SMEM)
RAD, BR = 4, (28, 52)


def params(mib):
    return pltpu.CompilerParams(vmem_limit_bytes=mib << 20)


def halves(x):
    hi = x.astype(BF16)
    return hi, (x - hi.astype(F32)).astype(BF16)


def dot3(a, b, dims):
    (ah, al), (bh, bl) = a, b

    def one(x, y):
        return lax.dot_general(x, y, (dims, ((), ())), preferred_element_type=F32)

    return one(ah, bh) + (one(ah, bl) + one(al, bh))


NN = ((1,), (0,))
NT = ((1,), (1,))


def strip(i):
    return slice(i * B, (i + 1) * B)


class Rules:
    def __init__(self, s_ref, start, rows, cols):
        self.s_ref, self.start, self.rows, self.cols = s_ref, start, rows, cols
        block = lax.shift_right_logical(lax.broadcasted_iota(jnp.int32, (1, N), 1), 6)
        radii = flags = jnp.zeros((1, N), jnp.int32)
        for k in range(H):
            radii = jnp.where(block == k, s_ref[RAD + cols + k], radii)
            flags = jnp.where(block == k, s_ref[start + cols + k], flags)
        self.block, self.radii, self.flags = block + cols, radii, flags

    def strip(self, i):
        reach = jnp.minimum(self.radii, self.s_ref[RAD + self.rows + i])
        keep = jnp.abs(self.block - (self.rows + i)) <= reach
        return keep, self.flags * self.s_ref[self.start + self.rows + i] == 1


def pack_kernel(v_ref, out_ref):
    for i in range(H):
        out_ref[strip(i), :] = jnp.concatenate([v_ref[i, 0], v_ref[i, 1]], axis=1)


def square_kernel(s_ref, *refs):
    packs, (p1_ref, g0_ref, pg_ref, send_ref, tr_ref) = refs[:8], refs[8:13]
    q_ref, r_ref, rh, rl, t_ref = refs[13:]
    yl, core, upper = s_ref[0], s_ref[1], s_ref[3]
    for k in range(4):
        for other in range(2):
            place = 2 * ((yl - k) & 3) + (core + other - 2 * core * other)
            q_ref[:, pl.ds(pl.multiple_of(place * 128, 128), 128)] = packs[4 * other + k][...]
    total = jnp.zeros((1, 2 * N), F32)
    for i in range(H):
        own = q_ref[strip(i), :]
        total += jnp.sum(own * own, axis=0, keepdims=True)
        at = i * B
        if i % 2:
            own = pltpu.roll(jnp.concatenate([own, jnp.zeros((B, 128), F32)], axis=1), B, 1)
            at -= B
        parts = [own]
        if at:
            parts.insert(0, jnp.zeros((B, at), F32))
        left = W - at - own.shape[1]
        if left:
            parts.append(jnp.zeros((B, left), F32))
        full = jnp.concatenate(parts, axis=1)
        r_ref[strip(i), :] = full
        rh[strip(i), :], rl[strip(i), :] = halves(full)
    tr_ref[...] = jnp.broadcast_to(jnp.sum(total, axis=1, keepdims=True), tr_ref.shape)

    def part(rows, cols):
        return rh[rows, cols], rl[rows, cols]

    lo, hi = slice(0, 256), slice(256, 512)
    mid = slice(N, 2 * N)
    side = pl.ds(pl.multiple_of(2 * N * upper, 128), N)
    pg_ref[...] = dot3(part(slice(None), mid), part(slice(None), side), NN)

    @pl.when(upper == 0)
    def _():
        g0_ref[...] = r_ref[:, 0:N]

    @pl.when(upper == 1)
    def _():
        g0_ref[...] = r_ref[:, 2 * N : W].T
        pg_ref[...] = pg_ref[...].T

    lane = lax.broadcasted_iota(jnp.int32, (B, 256), 1)
    t_ref[lo, :] = pg_ref[lo, hi]
    for a in range(3):
        turned = pltpu.roll(pg_ref[strip(6 - a), hi], (a + 1) * B, 1)
        t_ref[strip(4 + a), :] = jnp.where(lane >= (a + 1) * B, pg_ref[strip(a), lo], turned)
    send_ref[...] = t_ref[pl.ds(pl.multiple_of(core * HALF, 8), HALF), :]

    p01 = dot3(part(lo, slice(256, 1280)), part(hi, slice(256, 1280)), NT)
    p1_ref[lo, lo] = dot3(part(lo, slice(0, 1280)), part(lo, slice(0, 1280)), NT)
    p1_ref[lo, hi] = p01
    p1_ref[hi, lo] = p01.T
    p1_ref[hi, hi] = dot3(part(hi, slice(256, W)), part(hi, slice(256, W)), NT)
    rules = Rules(s_ref, BR[0], H, H)
    for i in range(H):
        keep, pick = rules.strip(i)
        squared = jnp.where(keep, p1_ref[strip(i), :], 0.0)
        p1_ref[strip(i), :] = jnp.where(pick, 2.0 * r_ref[strip(i), mid] - squared, squared)


def second_kernel(s_ref, p1_ref, g0_ref, pg_ref, tr_ref, xa, xb,
                  own_ref, far_ref, near_ref, sums_ref, t_ref, g_ref, mh, ml):
    core, col, upper = s_ref[1], s_ref[2], s_ref[3]
    lane = lax.broadcasted_iota(jnp.int32, (B, 256), 1)
    t_ref[pl.ds(pl.multiple_of(core * HALF, 8), HALF), :] = xa[...]
    t_ref[pl.ds(pl.multiple_of((1 - core) * HALF, 8), HALF), :] = xb[...]
    zero = jnp.zeros((B, 256), F32)
    base, other = H * (1 - upper), H * upper

    def at(block, size):
        return pl.ds(pl.multiple_of(block * B, B), size)

    def row(block, size=B):
        return at(block + 1, size)

    def lanes(block):
        return pl.ds(pl.multiple_of(block * B, 128), N)

    rules = Rules(s_ref, BR[0], H + H * upper, H * upper)
    outer = jnp.zeros((1, N), F32)
    inner = jnp.zeros((1, N), F32)
    for i in range(H):
        if i < 4:
            left = zero
            if i < 3:
                left = jnp.where(lane >= (i + 1) * B, t_ref[strip(4 + i), :], 0.0)
            right = t_ref[strip(i), :]
        else:
            left = right = zero
            if i < 7:
                turned = pltpu.roll(t_ref[strip(10 - i), :], (i - 3) * B, 1)
                right = jnp.where(lane >= (i - 3) * B, turned, 0.0)
        keep, pick = rules.strip(i)
        squared = pg_ref[strip(i), :] + jnp.concatenate([left, right], axis=1)
        squared = jnp.where(keep, squared, 0.0)
        new = jnp.where(pick, 2.0 * g0_ref[strip(i), :] - squared, squared)
        g_ref[strip(i), :] = new
        outer += jnp.sum(new * new, axis=0, keepdims=True)
        mh[row(H + i), 0:N], ml[row(H + i), 0:N] = halves(new)
        new = p1_ref[strip(i), :]
        inner += jnp.sum(new * new, axis=0, keepdims=True)
        mh[row(base + i), lanes(base)], ml[row(base + i), lanes(base)] = halves(new)
    mh[row(0, N), N : 2 * N], ml[row(0, N), N : 2 * N] = halves(g_ref[...].T)
    blank = jnp.zeros((N, N), BF16)
    mh[row(other, N), lanes(other)] = blank
    ml[row(other, N), lanes(other)] = blank

    spot = lax.broadcasted_iota(jnp.int32, (1, 128), 1)
    both = jnp.where(spot == 0, tr_ref[...], 0.0)
    both = jnp.where(spot == 1, jnp.sum(inner, axis=1, keepdims=True), both)
    both = jnp.where(spot == 2, jnp.sum(outer, axis=1, keepdims=True), both)
    sums_ref[...] = jnp.broadcast_to(both, sums_ref.shape)

    wide = (lax.broadcasted_iota(jnp.int32, (B, 128), 1) >= B).astype(jnp.int32)
    shift = 6 - 2 * col

    def share(i, rows, panel):
        block = rows + i + shift
        pair = row(jnp.clip(block, -1, 2 * H - 1), 128)
        span = lanes(panel)
        product = dot3(
            (mh[row(rows + i), span], ml[row(rows + i), span]),
            (mh[pair, span], ml[pair, span]), NT,
        )
        index = block + wide - base
        return jnp.where((index >= 0) & (index < H), product, 0.0)

    for i in range(H):
        far_ref[strip(i), :] = share(i, other, base)
        near_ref[strip(i), :] = share(i, base, other)
        here = row(base + i)
        block = base + i + 2 * col - H
        pair = row(block, 128)
        own_ref[0, strip(i), :] = dot3((mh[here, :], ml[here, :]), (mh[pair, :], ml[pair, :]), NT)
        if i % 2:
            span = pl.ds(pl.multiple_of((block - 1) * B, 128), 256)
            held = mh[here, span].astype(F32) + ml[here, span].astype(F32)
            held = held[:, B : B + 128]
        else:
            span = pl.ds(pl.multiple_of(block * B, 128), 128)
            held = mh[here, span].astype(F32) + ml[here, span].astype(F32)
        own_ref[1, strip(i), :] = held


def last_kernel(s_ref, own_ref, far_ref, near_ref, sums_ref, out_ref, traces_ref):
    col, upper = s_ref[2], s_ref[3]
    wide = lax.broadcasted_iota(jnp.int32, (B, 128), 1) >= B
    for i in range(H):
        squared = own_ref[0, strip(i), :] + (far_ref[strip(i), :] + near_ref[strip(i), :])
        keep, pick = [], []
        for h in range(2):
            far = jnp.abs(2 * col + h - H)
            reach = jnp.minimum(s_ref[RAD + H + i], s_ref[RAD + i + 2 * col + h])
            keep.append((far <= reach).astype(F32))
            pick.append((s_ref[BR[1] + H + i] * s_ref[BR[1] + i + 2 * col + h]).astype(F32))
        squared = squared * jnp.where(wide, keep[1], keep[0])
        chosen = jnp.where(wide, pick[1], pick[0]) == 1.0
        new = jnp.where(chosen, 2.0 * own_ref[1, strip(i), :] - squared, squared)
        out_ref[i, 0] = new[:, :B]
        out_ref[i, 1] = new[:, B:]
    sums = sums_ref[...]
    count = sums.shape[0]
    spot = lax.broadcasted_iota(jnp.int32, sums.shape, 1)
    line = lax.broadcasted_iota(jnp.int32, sums.shape, 0)
    turned = jnp.concatenate([sums[count - 1 :], sums[: count - 1]], axis=0)
    sums = jnp.where((spot == 2) & (upper + 0 * line == 1), turned, sums)
    total = jnp.sum(sums, axis=0, keepdims=True)
    spot = lax.broadcasted_iota(jnp.int32, total.shape, 1)
    weight = jnp.where(spot == 1, 1.0, jnp.where(spot == 2, 2.0, 0.0))
    traces_ref[0] = jnp.sum(jnp.where(spot == 0, total, 0.0))
    traces_ref[1] = jnp.sum(total * weight)


def shape(*dims):
    return jax.ShapeDtypeStruct(dims, F32)


def per_device(rows, values, radius, branch):
    both = ("row", "col")
    row, col = lax.axis_index("row"), lax.axis_index("col")
    pad = ((H, H),)
    radii = lax.dynamic_slice(jnp.pad(radius, pad, constant_values=-1), (H * row,), (3 * H,))
    flags = lax.dynamic_slice(jnp.pad(branch, ((0, 0),) + pad), (0, H * row), (2, 3 * H))
    scalars = jnp.concatenate(
        [jnp.stack([col // 2, col % 2, col, col // 4]).astype(jnp.int32), radii, flags[0], flags[1]]
    )

    def swap(x):
        return lax.ppermute(x, "col", [(c, c ^ 1) for c in range(8)])

    def to_rows(x, pairs):
        return lax.ppermute(x, both, pairs)

    packed = pl.pallas_call(
        pack_kernel, out_shape=shape(N, 128), in_specs=[VMEM], out_specs=VMEM, name="pack",
        compiler_params=params(16),
    )(values)
    mine = [packed] + [
        lax.ppermute(packed, "col", [(c, (c + 2 * k) % 8) for c in range(8)]) for k in (1, 2, 3)
    ]
    others = [swap(x) for x in mine]

    inner, old, product, send, trace = pl.pallas_call(
        square_kernel,
        out_shape=[shape(N, N)] * 3 + [shape(HALF, 256), shape(1, 128)],
        in_specs=[SMEM] + [VMEM] * 8,
        out_specs=[VMEM] * 5,
        scratch_shapes=[
            pltpu.VMEM((N, 2 * N), F32),
            pltpu.VMEM((N, W), F32),
            pltpu.VMEM((N, W), BF16),
            pltpu.VMEM((N, W), BF16),
            pltpu.VMEM((2 * HALF, 256), F32),
        ],
        compiler_params=params(48),
        name="square",
    )(scalars, *mine, *others)

    def index(r, c):
        return r * 8 + c

    ends = [(r, c) for r in range(rows - 1) for c in range(4)]
    pairs = [(index(r, c + 4), index(r + 1, c)) for r, c in ends]
    xa = lax.ppermute(send, both, pairs + [(b, a) for a, b in pairs])
    xb = swap(xa)

    own, far, near, sums = pl.pallas_call(
        second_kernel,
        out_shape=[shape(2, N, 128), shape(N, 128), shape(N, 128), shape(rows, 128)],
        in_specs=[SMEM] + [VMEM] * 6,
        out_specs=[VMEM] * 4,
        scratch_shapes=[
            pltpu.VMEM((2 * HALF, 256), F32),
            pltpu.VMEM((N, N), F32),
            pltpu.VMEM((18 * B, 2 * N), BF16),
            pltpu.VMEM((18 * B, 2 * N), BF16),
        ],
        compiler_params=params(48),
        name="second",
    )(scalars, inner, old, product, trace, xa, xb)

    pairs = [(index(r, 7 - c), index(r + 1, c)) for r, c in ends]
    far = lax.ppermute(far, both, pairs + [(b, a) for a, b in pairs])
    near = lax.ppermute(near, "col", [(c, 7 - c) for c in range(8)])
    sums = lax.all_to_all(sums, "row", 0, 0, tiled=True)
    return pl.pallas_call(
        last_kernel,
        out_shape=[shape(H, 2, B, B), shape(2)],
        in_specs=[SMEM] + [VMEM] * 4,
        out_specs=[VMEM, SMEM],
        compiler_params=params(16),
        name="last",
    )(scalars, own, far, near, sums)


def solution(mesh):
    rows = mesh.shape["row"]

    def run(values, radius, branch):
        return per_device(rows, values, radius, branch)

    in_specs = (P("row", "col", None, None), P(), P())
    out_specs = (P("row", "col", None, None), P())
    return jax.shard_map(
        run, mesh=mesh, in_specs=in_specs, out_specs=out_specs, check_vma=False
    )
```

time: 119 us -> 116 us (0.975)
  waiting for transfers between devices: 26.1 us -> 5.81 us
  starting transfers between devices: 37.6 us -> 52.4 us
  blocking collectives: 39.4 us -> 41.4 us
    ppermute x3, waiting for transfers between devices: 20.5 us -> 0.01 us  [the longest x1 0.01 us: per_device(): xa = lax.ppermute(send, both, pairs + [(b, a) for a, b in pairs])]
    ppermute x3, starting transfers between devices: 3.28 us -> 21.2 us  [the longest x1 19.9 us: per_device(): near = lax.ppermute(near, 'col', [(c, 7 - c) for c in range(8)])]
    ppermute x6 -> x5, starting transfers between devices: 24 us -> 20.9 us  [swap(): return lax.ppermute(x, 'col', [(c, c ^ 1) for c in range(8)])]
    all_to_all x1, blocking collectives: 39.4 us -> 41.4 us  [per_device(): sums = lax.all_to_all(sums, 'row', 0, 0, tiled=True)]
    ppermute x6 -> x5, waiting for transfers between devices: 2.39 us -> 2.62 us  [swap(): return lax.ppermute(x, 'col', [(c, c ^ 1) for c in range(8)])]
  transfers between devices with their start and end apart: 12 -> 11, of which waited for: 5 -> 3; matrix products, arithmetic and copies ran while one was open for 1% -> 0% of each run, Pallas kernels for 0% -> 0%
where the time goes in v2:
time: 116 us; the launch traced here: 115 us
  starting transfers between devices  52.4 us (45%)
  blocking collectives  41.4 us (36%)
  Pallas kernels  12.8 us (11%)
  waiting for transfers between devices  5.81 us (5%)
  local copies, waits for them, and re-layouts  1.96 us (2%)
    all_to_all x1, blocking collectives, per_device(): sums = lax.all_to_all(sums, 'row', 0, 0, tiled=True)  41.4 us
    ppermute x5, starting transfers between devices, swap(): return lax.ppermute(x, 'col', [(c, c ^ 1) for c in range(8)])  20.9 us
    ppermute x1, starting transfers between devices, per_device(): near = lax.ppermute(near, 'col', [(c, 7 - c) for c in range(8)])  19.9 us
    ppermute x3, starting transfers between devices, per_device(): lax.ppermute(packed, 'col', [(c, (c + 2 * k) % 8) for c in range(8)])  10.3 us
    pallas_call x1, Pallas kernels, per_device(): pl.pallas_call(second_kernel, out_shape=[shape(2, N, 128), shape(N, 128),...  6.28 us
    pallas_call x1, Pallas kernels, per_device(): pl.pallas_call(square_kernel, out_shape=[shape(N, N)] * 3 + [shape(HALF,...  4.87 us
    ppermute x3, waiting for transfers between devices, per_device(): lax.ppermute(packed, 'col', [(c, (c + 2 * k) % 8) for c in range(8)])  3.18 us
    ppermute x5, waiting for transfers between devices, swap(): return lax.ppermute(x, 'col', [(c, c ^ 1) for c in range(8)])  2.62 us
  transfers between devices with their start and end apart: 11, of which 3 were waited for; matrix products, arithmetic and copies ran while one was open for 0% of the time, Pallas kernels for 0%

profile of v2, /device:TPU:1, one launch (start us, length us, event | category | flops | bytes accessed | tf_op | source)
XLA Modules:
  0.0 115.3 jit_solution(4748021198676827603)
XLA Ops:
  0.6 1.0 copy-done
  1.7 0.1 pack.1.refs_0_
  1.8 6.1 %collective-permute-start.2 = (f32[512,128]{1,0:T(8,128)S(1)}, f32[512,128]{1,0:T(8,128)S(1)}, u32[]{:S(2)}, u32[]{:S(2)}) collective-permute-start(f32[512,128]{1,0:T(8,128)S(1)} %pack.1.refs_0_), channel_id=1, source_target_pairs={{0,6},{1,7},{2,0},{3,1},{4,2},{5,3},{6,4},{7,5},{8,14},{9,15},{10,... | collective-permute-start | bytes 786440 | tf_op jit(solution)/shard_map/ppermute | solution.py:268
  7.9 1.9 %collective-permute-start.1 = (f32[512,128]{1,0:T(8,128)S(1)}, f32[512,128]{1,0:T(8,128)S(1)}, u32[]{:S(2)}, u32[]{:S(2)}) collective-permute-start(f32[512,128]{1,0:T(8,128)S(1)} %pack.1.refs_0_), channel_id=1, source_target_pairs={{0,4},{1,5},{2,6},{3,7},{4,0},{5,1},{6,2},{7,3},{8,12},{9,13},{10,... | collective-permute-start | bytes 786440 | tf_op jit(solution)/shard_map/ppermute | solution.py:268
  9.8 2.3 %collective-permute-start = (f32[512,128]{1,0:T(8,128)S(1)}, f32[512,128]{1,0:T(8,128)S(1)}, u32[]{:S(2)}, u32[]{:S(2)}) collective-permute-start(f32[512,128]{1,0:T(8,128)S(1)} %pack.1.refs_0_), channel_id=1, source_target_pairs={{0,2},{1,3},{2,4},{3,5},{4,6},{5,7},{6,0},{7,1},{8,10},{9,11},{10,... | collective-permute-start | bytes 786440 | tf_op jit(solution)/shard_map/ppermute | solution.py:268
  12.2 9.9 %collective-permute-start.3 = (f32[512,128]{1,0:T(8,128)S(1)}, f32[512,128]{1,0:T(8,128)S(1)}, u32[]{:S(2)}, u32[]{:S(2)}) collective-permute-start(f32[512,128]{1,0:T(8,128)S(1)} %pack.1.refs_0_), channel_id=1, source_target_pairs={{0,1},{1,0},{2,3},{3,2},{4,5},{5,4},{6,7},{7,6},{8,9},{9,8},{10,11... | collective-permute-start | bytes 786440 | tf_op jit(solution)/shard_map/ppermute | solution.py:258
  22.1 0.7 copy-done.1
  22.7 0.1 pad_dynamic-slice_fusion
  22.8 3.6 %collective-permute-start.6 = (f32[512,128]{1,0:T(8,128)S(1)}, f32[512,128]{1,0:T(8,128)S(1)}, u32[]{:S(2)}, u32[]{:S(2)}) collective-permute-start(f32[512,128]{1,0:T(8,128)S(1)} %collective-permute-done.2.refs_3_), channel_id=1, source_target_pairs={{0,1},{1,0},{2,3},{3,2},{4,5},{5,4},{6,7},{7,6},{8,9},{9,8},{10,11... | collective-permute-start | bytes 786440 | tf_op jit(solution)/shard_map/ppermute | solution.py:258
  26.4 3.2 %collective-permute-done.1.refs_2_ = f32[512,128]{1,0:T(8,128)S(1)} collective-permute-done((f32[512,128]{1,0:T(8,128)S(1)}, f32[512,128]{1,0:T(8,128)S(1)}, u32[]{:S(2)}, u32[]{:S(2)}) %collective-permute-start.1) | collective-permute-done | bytes 262176 | tf_op jit(solution)/shard_map/ppermute | solution.py:268
  29.6 3.5 %collective-permute-start.5 = (f32[512,128]{1,0:T(8,128)S(1)}, f32[512,128]{1,0:T(8,128)S(1)}, u32[]{:S(2)}, u32[]{:S(2)}) collective-permute-start(f32[512,128]{1,0:T(8,128)S(1)} %collective-permute-done.1.refs_2_), channel_id=1, source_target_pairs={{0,1},{1,0},{2,3},{3,2},{4,5},{5,4},{6,7},{7,6},{8,9},{9,8},{10,11... | collective-permute-start | bytes 786440 | tf_op jit(solution)/shard_map/ppermute | solution.py:258
  33.1 1.9 %collective-permute-start.4 = (f32[512,128]{1,0:T(8,128)S(1)}, f32[512,128]{1,0:T(8,128)S(1)}, u32[]{:S(2)}, u32[]{:S(2)}) collective-permute-start(f32[512,128]{1,0:T(8,128)S(1)} %collective-permute-done.refs_1_), channel_id=1, source_target_pairs={{0,1},{1,0},{2,3},{3,2},{4,5},{5,4},{6,7},{7,6},{8,9},{9,8},{10,11... | collective-permute-start | bytes 786440 | tf_op jit(solution)/shard_map/ppermute | solution.py:258
  35.0 0.1 pad_dynamic-slice_fusion.1
  35.1 0.1 concatenate.3.s_ref
  35.2 1.3 %collective-permute-done.4.refs_5_ = f32[512,128]{1,0:T(8,128)S(1)} collective-permute-done((f32[512,128]{1,0:T(8,128)S(1)}, f32[512,128]{1,0:T(8,128)S(1)}, u32[]{:S(2)}, u32[]{:S(2)}) %collective-permute-start.4) | collective-permute-done | bytes 262176 | tf_op jit(solution)/shard_map/ppermute | solution.py:258
  36.5 4.9 %square.1 = (f32[512,512]{1,0:T(8,128)S(1)}, f32[512,512]{1,0:T(8,128)S(1)}, f32[512,512]{1,0:T(8,128)S(1)}, f32[224,256]{1,0:T(8,128)S(1)}, f32[1,128]{1,0:T(1,128)S(1)}) custom-call(s32[76]{0:T(128)S(1)} %concatenate.3.s_ref, f32[512,128]{1,0:T(8,128)S(1)} %pack.1.refs_0_, f32[512,128]{1,0:T(8,128)S(1)} %collective-permute-done.refs_1_, ...), custom_call_target="tpu_custom_call" | custom-call | tf_op jit(solution)/shard_map/square/pallas_call | solution.py:272
  41.4 0.7 collective-permute-start.7
  42.1 2.1 %collective-permute-start.8 = (f32[224,256]{1,0:T(8,128)S(1)}, f32[224,256]{1,0:T(8,128)S(1)}, u32[]{:S(2)}, u32[]{:S(2)}) collective-permute-start(f32[224,256]{1,0:T(8,128)S(1)} %collective-permute-done.7.xa), channel_id=1, source_target_pairs={{0,1},{1,0},{2,3},{3,2},{4,5},{5,4},{6,7},{7,6},{8,9},{9,8},{10,11... | collective-permute-start | bytes 688136 | tf_op jit(solution)/shard_map/ppermute | solution.py:258
  44.1 1.3 %collective-permute-done.8.xb = f32[224,256]{1,0:T(8,128)S(1)} collective-permute-done((f32[224,256]{1,0:T(8,128)S(1)}, f32[224,256]{1,0:T(8,128)S(1)}, u32[]{:S(2)}, u32[]{:S(2)}) %collective-permute-start.8) | collective-permute-done | bytes 229408 | tf_op jit(solution)/shard_map/ppermute | solution.py:258
  45.5 6.3 %second.1 = (f32[2,512,128]{2,1,0:T(8,128)S(1)}, f32[512,128]{1,0:T(8,128)S(1)}, f32[512,128]{1,0:T(8,128)S(1)}, f32[96,128]{1,0:T(8,128)S(1)}) custom-call(s32[76]{0:T(128)S(1)} %concatenate.3.s_ref, f32[512,512]{1,0:T(8,128)S(1)} %get-tuple-element.11.p1_ref, f32[512,512]{1,0:T(8,128)S(1)} %get-tuple-element.12.g0_ref, ...), custom_call_target="tpu_custom_call" | custom-call | tf_op jit(solution)/shard_map/second/pallas_call | solution.py:296
  51.8 0.7 collective-permute-start.9
  52.4 19.9 %collective-permute-start.10 = (f32[512,128]{1,0:T(8,128)S(1)}, f32[512,128]{1,0:T(8,128)S(1)}, u32[]{:S(2)}, u32[]{:S(2)}) collective-permute-start(f32[512,128]{1,0:T(8,128)S(1)} %get-tuple-element.18), channel_id=1, source_target_pairs={{0,7},{1,6},{2,5},{3,4},{4,3},{5,2},{6,1},{7,0},{8,15},{9,14},{10,... | collective-permute-start | bytes 786440 | tf_op jit(solution)/shard_map/ppermute | solution.py:313
  72.3 41.4 %all_to_all.11 = f32[96,1,128]{2,1,0:T(1,128)S(1)} all-to-all(f32[96,1,128]{2,1,0:T(1,128)S(1)} %bitcast.13), channel_id=1, replica_groups=mesh['row'=96,'col'=8] {'row'}, dimensions={0} | all-to-all | bytes 98304 | tf_op jit(solution)/shard_map/all_to_all | solution.py:314
  113.8 1.5 %last.1 = (f32[8,2,64,64]{3,2,1,0:T(8,128)}, f32[2]{0:T(128)}) custom-call(s32[76]{0:T(128)S(1)} %concatenate.3.s_ref, f32[2,512,128]{2,1,0:T(8,128)S(1)} %get-tuple-element.16.own_ref, f32[512,128]{1,0:T(8,128)S(1)} %collective-permute-done.9.far_ref, f32[512,128]{1,0:T(8,128)S(1)} %collective-permute-done.10.near_ref, f32[96,128]{1,0:T(8,128)S(1)} %bitcast.12), custom_call_target="tpu_custom_call" | custom-call | tf_op jit(solution)/shard_map/last/pallas_call | solution.py:315
  (13 shorter events, 0.0 us)
Async XLA Ops:
  0.6 1.0 copy-start
  1.8 21.0 %collective-permute-start.2 = (f32[512,128]{1,0:T(8,128)S(1)}, f32[512,128]{1,0:T(8,128)S(1)}, u32[]{:S(2)}, u32[]{:S(2)}) collective-permute-start(f32[512,128]{1,0:T(8,128)S(1)} %pack.1.refs_0_), channel_id=1, source_target_pairs={{0,6},{1,7},{2,0},{3,1},{4,2},{5,3},{6,4},{7,5},{8,14},{9,15},{10,... | collective-permute-start | bytes 786440 | tf_op jit(solution)/shard_map/ppermute | solution.py:268
  7.9 21.7 %collective-permute-start.1 = (f32[512,128]{1,0:T(8,128)S(1)}, f32[512,128]{1,0:T(8,128)S(1)}, u32[]{:S(2)}, u32[]{:S(2)}) collective-permute-start(f32[512,128]{1,0:T(8,128)S(1)} %pack.1.refs_0_), channel_id=1, source_target_pairs={{0,4},{1,5},{2,6},{3,7},{4,0},{5,1},{6,2},{7,3},{8,12},{9,13},{10,... | collective-permute-start | bytes 786440 | tf_op jit(solution)/shard_map/ppermute | solution.py:268
  9.8 23.3 %collective-permute-start = (f32[512,128]{1,0:T(8,128)S(1)}, f32[512,128]{1,0:T(8,128)S(1)}, u32[]{:S(2)}, u32[]{:S(2)}) collective-permute-start(f32[512,128]{1,0:T(8,128)S(1)} %pack.1.refs_0_), channel_id=1, source_target_pairs={{0,2},{1,3},{2,4},{3,5},{4,6},{5,7},{6,0},{7,1},{8,10},{9,11},{10,... | collective-permute-start | bytes 786440 | tf_op jit(solution)/shard_map/ppermute | solution.py:268
  12.2 23.0 %collective-permute-start.3 = (f32[512,128]{1,0:T(8,128)S(1)}, f32[512,128]{1,0:T(8,128)S(1)}, u32[]{:S(2)}, u32[]{:S(2)}) collective-permute-start(f32[512,128]{1,0:T(8,128)S(1)} %pack.1.refs_0_), channel_id=1, source_target_pairs={{0,1},{1,0},{2,3},{3,2},{4,5},{5,4},{6,7},{7,6},{8,9},{9,8},{10,11... | collective-permute-start | bytes 786440 | tf_op jit(solution)/shard_map/ppermute | solution.py:258
  22.0 0.7 copy-start.1
  22.7 12.3 %copy-start.2 = (s32[768]{0:T(1024)S(1)}, s32[768]{0:T(1024)}, u32[]{:S(2)}) copy-start(s32[768]{0:T(1024)} %param.4) | copy-start | bytes 9220
  22.8 12.4 %collective-permute-start.6 = (f32[512,128]{1,0:T(8,128)S(1)}, f32[512,128]{1,0:T(8,128)S(1)}, u32[]{:S(2)}, u32[]{:S(2)}) collective-permute-start(f32[512,128]{1,0:T(8,128)S(1)} %collective-permute-done.2.refs_3_), channel_id=1, source_target_pairs={{0,1},{1,0},{2,3},{3,2},{4,5},{5,4},{6,7},{7,6},{8,9},{9,8},{10,11... | collective-permute-start | bytes 786440 | tf_op jit(solution)/shard_map/ppermute | solution.py:258
  29.6 5.6 %collective-permute-start.5 = (f32[512,128]{1,0:T(8,128)S(1)}, f32[512,128]{1,0:T(8,128)S(1)}, u32[]{:S(2)}, u32[]{:S(2)}) collective-permute-start(f32[512,128]{1,0:T(8,128)S(1)} %collective-permute-done.1.refs_2_), channel_id=1, source_target_pairs={{0,1},{1,0},{2,3},{3,2},{4,5},{5,4},{6,7},{7,6},{8,9},{9,8},{10,11... | collective-permute-start | bytes 786440 | tf_op jit(solution)/shard_map/ppermute | solution.py:258
  33.1 3.4 %collective-permute-start.4 = (f32[512,128]{1,0:T(8,128)S(1)}, f32[512,128]{1,0:T(8,128)S(1)}, u32[]{:S(2)}, u32[]{:S(2)}) collective-permute-start(f32[512,128]{1,0:T(8,128)S(1)} %collective-permute-done.refs_1_), channel_id=1, source_target_pairs={{0,1},{1,0},{2,3},{3,2},{4,5},{5,4},{6,7},{7,6},{8,9},{9,8},{10,11... | collective-permute-start | bytes 786440 | tf_op jit(solution)/shard_map/ppermute | solution.py:258
  41.4 0.7 collective-permute-start.7
  42.1 3.4 %collective-permute-start.8 = (f32[224,256]{1,0:T(8,128)S(1)}, f32[224,256]{1,0:T(8,128)S(1)}, u32[]{:S(2)}, u32[]{:S(2)}) collective-permute-start(f32[224,256]{1,0:T(8,128)S(1)} %collective-permute-done.7.xa), channel_id=1, source_target_pairs={{0,1},{1,0},{2,3},{3,2},{4,5},{5,4},{6,7},{7,6},{8,9},{9,8},{10,11... | collective-permute-start | bytes 688136 | tf_op jit(solution)/shard_map/ppermute | solution.py:258
  51.8 62.0 %collective-permute-start.9 = (f32[512,128]{1,0:T(8,128)S(1)}, f32[512,128]{1,0:T(8,128)S(1)}, u32[]{:S(2)}, u32[]{:S(2)}) collective-permute-start(f32[512,128]{1,0:T(8,128)S(1)} %get-tuple-element.17), channel_id=1, source_target_pairs={{7,8},{6,9},{5,10},{4,11},{15,16},{14,17},{13,18},{12,19},{23,24},... | collective-permute-start | bytes 786440 | tf_op jit(solution)/shard_map/ppermute | solution.py:312
  52.4 61.3 %collective-permute-start.10 = (f32[512,128]{1,0:T(8,128)S(1)}, f32[512,128]{1,0:T(8,128)S(1)}, u32[]{:S(2)}, u32[]{:S(2)}) collective-permute-start(f32[512,128]{1,0:T(8,128)S(1)} %get-tuple-element.18), channel_id=1, source_target_pairs={{0,7},{1,6},{2,5},{3,4},{4,3},{5,2},{6,1},{7,0},{8,15},{9,14},{10,... | collective-permute-start | bytes 786440 | tf_op jit(solution)/shard_map/ppermute | solution.py:313

commit v3 on v2

--- a/solution.py
+++ b/solution.py
@@ -11,7 +11,6 @@
 H = 8
 N = H * B
 W = 3 * N
-HALF = 224
 VMEM = pl.BlockSpec(memory_space=pltpu.VMEM)
 SMEM = pl.BlockSpec(memory_space=pltpu.SMEM)
 RAD, BR = 4, (28, 52)
@@ -59,18 +58,52 @@
         return keep, self.flags * self.s_ref[self.start + self.rows + i] == 1
 
 
-def pack_kernel(v_ref, out_ref):
+def pack_kernel(v_ref, out_ref, diag_ref):
     for i in range(H):
         out_ref[strip(i), :] = jnp.concatenate([v_ref[i, 0], v_ref[i, 1]], axis=1)
+    for i in range(4):
+        diag_ref[strip(i), :] = jnp.concatenate([v_ref[i, 0], v_ref[i + 4, 0]], axis=1)
+
+
+def triangle_kernel(s_ref, own_ref, near_ref, d1_ref, d2_ref, out_ref, low, high):
+    odd, core, upper = (s_ref[0] & 1) == 1, s_ref[1], s_ref[3]
+    low[...] = jnp.where(odd, near_ref[...], own_ref[...])
+    high[...] = jnp.where(odd, own_ref[...], near_ref[...])
+
+    def rows(ref, first, last):
+        return ref[first * B : (last + 1) * B, :]
+
+    @pl.when((upper == 0) & (core == 0))
+    def _():
+        out_ref[0:256, :] = rows(high, 3, 6)
+        out_ref[256:512, :] = d1_ref[...] + d2_ref[...]
+        out_ref[512:640, :] = jnp.zeros((128, 128), F32)
+
+    @pl.when((upper == 0) & (core == 1))
+    def _():
+        out_ref[0:384, :] = rows(high, 1, 6)
+        out_ref[384:512, :] = rows(low, 5, 6)
+        out_ref[512:640, :] = jnp.zeros((128, 128), F32)
+
+    @pl.when((upper == 1) & (core == 0))
+    def _():
+        out_ref[0:448, :] = rows(low, 1, 7)
+        out_ref[448:640, :] = rows(high, 1, 3)
+
+    @pl.when((upper == 1) & (core == 1))
+    def _():
+        out_ref[0:320, :] = rows(low, 1, 5)
+        out_ref[320:384, :] = rows(high, 1, 1)
+        out_ref[384:640, :] = jnp.zeros((256, 128), F32)
 
 
 def square_kernel(s_ref, *refs):
-    packs, (p1_ref, g0_ref, pg_ref, send_ref, tr_ref) = refs[:8], refs[8:13]
-    q_ref, r_ref, rh, rl, t_ref = refs[13:]
+    packs, (p1_ref, v_ref, vh_ref, vl_ref, pv_ref, tr_ref) = refs[:8], refs[8:14]
+    q_ref, r_ref, rh, rl = refs[14:]
     yl, core, upper = s_ref[0], s_ref[1], s_ref[3]
     for k in range(4):
         for other in range(2):
-            place = 2 * ((yl - k) & 3) + (core + other - 2 * core * other)
+            place = 2 * (yl ^ k) + (core ^ other)
             q_ref[:, pl.ds(pl.multiple_of(place * 128, 128), 128)] = packs[4 * other + k][...]
     total = jnp.zeros((1, 2 * N), F32)
     for i in range(H):
@@ -97,23 +130,9 @@
     lo, hi = slice(0, 256), slice(256, 512)
     mid = slice(N, 2 * N)
     side = pl.ds(pl.multiple_of(2 * N * upper, 128), N)
-    pg_ref[...] = dot3(part(slice(None), mid), part(slice(None), side), NN)
-
-    @pl.when(upper == 0)
-    def _():
-        g0_ref[...] = r_ref[:, 0:N]
-
-    @pl.when(upper == 1)
-    def _():
-        g0_ref[...] = r_ref[:, 2 * N : W].T
-        pg_ref[...] = pg_ref[...].T
-
-    lane = lax.broadcasted_iota(jnp.int32, (B, 256), 1)
-    t_ref[lo, :] = pg_ref[lo, hi]
-    for a in range(3):
-        turned = pltpu.roll(pg_ref[strip(6 - a), hi], (a + 1) * B, 1)
-        t_ref[strip(4 + a), :] = jnp.where(lane >= (a + 1) * B, pg_ref[strip(a), lo], turned)
-    send_ref[...] = t_ref[pl.ds(pl.multiple_of(core * HALF, 8), HALF), :]
+    v_ref[...] = r_ref[:, side]
+    vh_ref[...], vl_ref[...] = rh[:, side], rl[:, side]
+    pv_ref[...] = dot3(part(slice(None), mid), (vh_ref[...], vl_ref[...]), NN)
 
     p01 = dot3(part(lo, slice(256, 1280)), part(hi, slice(256, 1280)), NT)
     p1_ref[lo, lo] = dot3(part(lo, slice(0, 1280)), part(lo, slice(0, 1280)), NT)
@@ -127,14 +146,54 @@
         p1_ref[strip(i), :] = jnp.where(pick, 2.0 * r_ref[strip(i), mid] - squared, squared)
 
 
-def second_kernel(s_ref, p1_ref, g0_ref, pg_ref, tr_ref, xa, xb,
-                  own_ref, far_ref, near_ref, sums_ref, t_ref, g_ref, mh, ml):
+def second_kernel(s_ref, p1_ref, v_ref, vh_ref, vl_ref, pv_ref, tr_ref, ta, tb,
+                  own_ref, far_ref, near_ref, sums_ref, t_ref, w_ref, mh, ml):
     core, col, upper = s_ref[1], s_ref[2], s_ref[3]
-    lane = lax.broadcasted_iota(jnp.int32, (B, 256), 1)
-    t_ref[pl.ds(pl.multiple_of(core * HALF, 8), HALF), :] = xa[...]
-    t_ref[pl.ds(pl.multiple_of((1 - core) * HALF, 8), HALF), :] = xb[...]
-    zero = jnp.zeros((B, 256), F32)
+    lane = lax.broadcasted_iota(jnp.int32, (B, N), 1)
+    zero = jnp.zeros((B, 128), F32)
     base, other = H * (1 - upper), H * upper
+    t_ref[core, :, :] = ta[...]
+    t_ref[1 - core, :, :] = tb[...]
+
+    def line(which, start):
+        return t_ref[which, start * B : (start + 1) * B, :]
+
+    @pl.when(upper == 0)
+    def _():
+        w_ref[strip(0), :] = jnp.zeros((B, N), F32)
+        for k in range(1, H):
+            parts = [line(0, k - 1), zero, zero, zero]
+            if k < 6:
+                parts[1] = line(1, k - 1)
+            if k < 4:
+                parts[2] = line(0, 6 + k)
+            if k < 2:
+                parts[3] = line(1, 4 + k)
+            turned = pltpu.roll(jnp.concatenate(parts, axis=1), k * B, 1)
+            w_ref[strip(k), :] = jnp.where(lane >= k * B, turned, 0.0)
+
+    @pl.when(upper == 1)
+    def _():
+        w_ref[strip(7), :] = jnp.zeros((B, N), F32)
+        for k in range(7):
+            diag = line(0, 4 + k % 4)
+            if k >= 4:
+                diag = pltpu.roll(diag, B, 1)
+            parts = [zero, zero, zero, diag]
+            if k >= 5:
+                parts[0] = line(1, k + 1)
+            if k >= 3:
+                parts[1] = line(0, k - 3)
+            if k >= 1:
+                parts[2] = line(1, k - 1)
+            turned = pltpu.roll(jnp.concatenate(parts, axis=1), ((k + 2) % 8) * B, 1)
+            w_ref[strip(k), :] = jnp.where(lane < (k + 1) * B, turned, 0.0)
+
+    full = w_ref[...]
+    above = lax.shift_right_logical(lax.broadcasted_iota(jnp.int32, (N, N), 0), 6)
+    along = lax.shift_right_logical(lax.broadcasted_iota(jnp.int32, (N, N), 1), 6)
+    full = jnp.where(above == along, full, full + full.T)
+    w_ref[...] = pv_ref[...] + dot3((vh_ref[...], vl_ref[...]), halves(full), NN)
 
     def at(block, size):
         return pl.ds(pl.multiple_of(block * B, B), size)
@@ -145,34 +204,32 @@
     def lanes(block):
         return pl.ds(pl.multiple_of(block * B, 128), N)
 
-    rules = Rules(s_ref, BR[0], H + H * upper, H * upper)
-    outer = jnp.zeros((1, N), F32)
+    rules = Rules(s_ref, BR[0], H, 2 * H * upper)
     inner = jnp.zeros((1, N), F32)
     for i in range(H):
-        if i < 4:
-            left = zero
-            if i < 3:
-                left = jnp.where(lane >= (i + 1) * B, t_ref[strip(4 + i), :], 0.0)
-            right = t_ref[strip(i), :]
-        else:
-            left = right = zero
-            if i < 7:
-                turned = pltpu.roll(t_ref[strip(10 - i), :], (i - 3) * B, 1)
-                right = jnp.where(lane >= (i - 3) * B, turned, 0.0)
         keep, pick = rules.strip(i)
-        squared = pg_ref[strip(i), :] + jnp.concatenate([left, right], axis=1)
-        squared = jnp.where(keep, squared, 0.0)
-        new = jnp.where(pick, 2.0 * g0_ref[strip(i), :] - squared, squared)
-        g_ref[strip(i), :] = new
-        outer += jnp.sum(new * new, axis=0, keepdims=True)
-        mh[row(H + i), 0:N], ml[row(H + i), 0:N] = halves(new)
+        squared = jnp.where(keep, w_ref[strip(i), :], 0.0)
+        new = jnp.where(pick, 2.0 * v_ref[strip(i), :] - squared, squared)
+        w_ref[strip(i), :] = new
+        here = row(base + i)
+        mh[here, lanes(other)], ml[here, lanes(other)] = halves(new)
         new = p1_ref[strip(i), :]
         inner += jnp.sum(new * new, axis=0, keepdims=True)
-        mh[row(base + i), lanes(base)], ml[row(base + i), lanes(base)] = halves(new)
-    mh[row(0, N), N : 2 * N], ml[row(0, N), N : 2 * N] = halves(g_ref[...].T)
+        mh[here, lanes(base)], ml[here, lanes(base)] = halves(new)
+    turned = w_ref[...].T
+    there = row(other, N)
+    mh[there, lanes(base)], ml[there, lanes(base)] = halves(turned)
     blank = jnp.zeros((N, N), BF16)
-    mh[row(other, N), lanes(other)] = blank
-    ml[row(other, N), lanes(other)] = blank
+    mh[there, lanes(other)] = blank
+    ml[there, lanes(other)] = blank
+
+    @pl.when(upper == 1)
+    def _():
+        w_ref[...] = turned
+
+    outer = jnp.zeros((1, N), F32)
+    for i in range(H):
+        outer += jnp.sum(w_ref[strip(i), :] * w_ref[strip(i), :], axis=0, keepdims=True)
 
     spot = lax.broadcasted_iota(jnp.int32, (1, 128), 1)
     both = jnp.where(spot == 0, tr_ref[...], 0.0)
@@ -260,53 +317,67 @@
     def to_rows(x, pairs):
         return lax.ppermute(x, both, pairs)
 
-    packed = pl.pallas_call(
-        pack_kernel, out_shape=shape(N, 128), in_specs=[VMEM], out_specs=VMEM, name="pack",
+    def index(r, c):
+        return r * 8 + c
+
+    ends = [(r, c) for r in range(rows - 1) for c in range(4)]
+
+    packed, diag = pl.pallas_call(
+        pack_kernel, out_shape=[shape(N, 128), shape(256, 128)], in_specs=[VMEM],
+        out_specs=[VMEM] * 2, compiler_params=params(16), name="pack",
+    )(values)
+    near = lax.ppermute(packed, "col", [(c, c ^ 2) for c in range(8)])
+    cross = lax.ppermute(packed, "col", [(c, c ^ 4) for c in range(8)])
+    d1 = lax.ppermute(diag, "col", [(4, 2)])
+    d2 = lax.ppermute(diag, "col", [(4, 0)])
+    triangle = pl.pallas_call(
+        triangle_kernel,
+        out_shape=shape(640, 128),
+        in_specs=[SMEM] + [VMEM] * 4,
+        out_specs=VMEM,
+        scratch_shapes=[pltpu.VMEM((N, 128), F32)] * 2,
         compiler_params=params(16),
-    )(values)
-    mine = [packed] + [
-        lax.ppermute(packed, "col", [(c, (c + 2 * k) % 8) for c in range(8)]) for k in (1, 2, 3)
-    ]
+        name="triangle",
+    )(scalars, packed, near, d1, d2)
+    pairs = [(index(r, c + 4), index(r + 1, c)) for r, c in ends]
+    ta = lax.ppermute(triangle, both, pairs + [(b, a) for a, b in pairs])
+    forward = lax.ppermute(cross, "col", [(c, c ^ 2) for c in range(8)])
+    mine = [packed, near, cross, forward]
     others = [swap(x) for x in mine]
-
-    inner, old, product, send, trace = pl.pallas_call(
+    tb = swap(ta)
+
+    *old, trace = pl.pallas_call(
         square_kernel,
-        out_shape=[shape(N, N)] * 3 + [shape(HALF, 256), shape(1, 128)],
+        out_shape=[
+            shape(N, N), shape(N, N), jax.ShapeDtypeStruct((N, N), BF16),
+            jax.ShapeDtypeStruct((N, N), BF16), shape(N, N), shape(1, 128),
+        ],
         in_specs=[SMEM] + [VMEM] * 8,
-        out_specs=[VMEM] * 5,
+        out_specs=[VMEM] * 6,
         scratch_shapes=[
             pltpu.VMEM((N, 2 * N), F32),
             pltpu.VMEM((N, W), F32),
             pltpu.VMEM((N, W), BF16),
             pltpu.VMEM((N, W), BF16),
-            pltpu.VMEM((2 * HALF, 256), F32),
         ],
         compiler_params=params(48),
         name="square",
     )(scalars, *mine, *others)
 
-    def index(r, c):
-        return r * 8 + c
-
-    ends = [(r, c) for r in range(rows - 1) for c in range(4)]
-    pairs = [(index(r, c + 4), index(r + 1, c)) for r, c in ends]
-    xa = lax.ppermute(send, both, pairs + [(b, a) for a, b in pairs])
-    xb = swap(xa)
-
     own, far, near, sums = pl.pallas_call(
         second_kernel,
         out_shape=[shape(2, N, 128), shape(N, 128), shape(N, 128), shape(rows, 128)],
-        in_specs=[SMEM] + [VMEM] * 6,
+        in_specs=[SMEM] + [VMEM] * 8,
         out_specs=[VMEM] * 4,
         scratch_shapes=[
-            pltpu.VMEM((2 * HALF, 256), F32),
+            pltpu.VMEM((2, 640, 128), F32),
             pltpu.VMEM((N, N), F32),
             pltpu.VMEM((18 * B, 2 * N), BF16),
             pltpu.VMEM((18 * B, 2 * N), BF16),
         ],
         compiler_params=params(48),
         name="second",
-    )(scalars, inner, old, product, trace, xa, xb)
+    )(scalars, *old, trace, ta, tb)
 
     pairs = [(index(r, 7 - c), index(r + 1, c)) for r, c in ends]
     far = lax.ppermute(far, both, pairs + [(b, a) for a, b in pairs])

time: 116 us -> 115 us (level)
  starting transfers between devices: 52.4 us -> 49 us
  blocking collectives: 41.4 us -> 44.4 us
  waiting for transfers between devices: 5.81 us -> 2.99 us
  local copies, waits for them, and re-layouts: 1.96 us -> 3.86 us
    ppermute x1, starting transfers between devices: 19.9 us -> 12.6 us  [per_device(): near = lax.ppermute(near, 'col', [(c, 7 - c) for c in range(8)])]
    ppermute x4 -> x6, starting transfers between devices: 11 us -> 15.5 us  [the longest x1 5.24 us: per_device(): forward = lax.ppermute(cross, 'col', [(c, c ^ 2) for c in range(8)])]
    all_to_all x1, blocking collectives: 41.4 us -> 44.4 us  [per_device(): sums = lax.all_to_all(sums, 'row', 0, 0, tiled=True)]
    unnamed x6 -> x8, local copies, waits for them, and re-layouts: 1.71 us -> 3.62 us
    ppermute x5, waiting for transfers between devices: 2.62 us -> 1.12 us  [swap(): return lax.ppermute(x, 'col', [(c, c ^ 1) for c in range(8)])]
    ppermute x4 -> x6, waiting for transfers between devices: 3.18 us -> 1.86 us  [the longest x1 1.36 us: per_device(): near = lax.ppermute(packed, 'col', [(c, c ^ 2) for c in range(8)])]
    pallas_call x2 -> x3, Pallas kernels: 5 us -> 4.71 us  [the longest x1 3.95 us: per_device(): pl.pallas_call(square_kernel, out_shape=[shape(N, N), shape(N, N), jax.Sh...]
  transfers between devices with their start and end apart: 11 -> 13, of which waited for: 3 -> 3; matrix products, arithmetic and copies ran while one was open for 0% -> 0% of each run, Pallas kernels for 0% -> 4%
where the time goes in v3:
time: 115 us; the launch traced here: 114 us
  starting transfers between devices  49 us (43%)
  blocking collectives  44.4 us (39%)
  Pallas kernels  12.8 us (11%)
  local copies, waits for them, and re-layouts  3.86 us (3%)
  waiting for transfers between devices  2.99 us (3%)
    all_to_all x1, blocking collectives, per_device(): sums = lax.all_to_all(sums, 'row', 0, 0, tiled=True)  44.4 us
    ppermute x5, starting transfers between devices, swap(): return lax.ppermute(x, 'col', [(c, c ^ 1) for c in range(8)])  20.2 us
    ppermute x1, starting transfers between devices, per_device(): near = lax.ppermute(near, 'col', [(c, 7 - c) for c in range(8)])  12.6 us
    pallas_call x1, Pallas kernels, per_device(): pl.pallas_call(second_kernel, out_shape=[shape(2, N, 128), shape(N, 128),...  6.59 us
    ppermute x1, starting transfers between devices, per_device(): forward = lax.ppermute(cross, 'col', [(c, c ^ 2) for c in range(8)])  5.24 us
    ppermute x1, starting transfers between devices, per_device(): cross = lax.ppermute(packed, 'col', [(c, c ^ 4) for c in range(8)])  5.05 us
    pallas_call x1, Pallas kernels, per_device(): pl.pallas_call(square_kernel, out_shape=[shape(N, N), shape(N, N), jax.Sh...  3.95 us
    unnamed x8, local copies, waits for them, and re-layouts  3.62 us
  transfers between devices with their start and end apart: 13, of which 3 were waited for; matrix products, arithmetic and copies ran while one was open for 0% of the time, Pallas kernels for 4%

profile of v3, /device:TPU:1, one launch (start us, length us, event | category | flops | bytes accessed | tf_op | source)
XLA Modules:
  0.0 113.9 jit_solution(781530490255128932)
XLA Ops:
  0.6 1.0 copy-done.1
  1.8 5.0 %collective-permute-start.1 = (f32[512,128]{1,0:T(8,128)S(1)}, f32[512,128]{1,0:T(8,128)S(1)}, u32[]{:S(2)}, u32[]{:S(2)}) collective-permute-start(f32[512,128]{1,0:T(8,128)S(1)} %get-tuple-element.14.refs_0_.own_ref), channel_id=1, source_target_pairs={{0,4},{1,5},{2,6},{3,7},{4,0},{5,1},{6,2},{7,3},{8,12},{9,13},{10,... | collective-permute-start | bytes 786440 | tf_op jit(solution)/shard_map/ppermute | solution.py:330
  6.9 3.2 %collective-permute-start = (f32[512,128]{1,0:T(8,128)S(1)}, f32[512,128]{1,0:T(8,128)S(1)}, u32[]{:S(2)}, u32[]{:S(2)}) collective-permute-start(f32[512,128]{1,0:T(8,128)S(1)} %get-tuple-element.14.refs_0_.own_ref), channel_id=1, source_target_pairs={{0,2},{1,3},{2,0},{3,1},{4,6},{5,7},{6,4},{7,5},{8,10},{9,11},{10,... | collective-permute-start | bytes 786440 | tf_op jit(solution)/shard_map/ppermute | solution.py:329
  10.1 0.7 collective-permute-start.7
  10.8 0.7 collective-permute-start.8
  11.5 0.7 copy-done.2
  12.2 0.7 copy-done.3
  13.1 1.4 %collective-permute-done.refs_1_.near_ref = f32[512,128]{1,0:T(8,128)S(1)} collective-permute-done((f32[512,128]{1,0:T(8,128)S(1)}, f32[512,128]{1,0:T(8,128)S(1)}, u32[]{:S(2)}, u32[]{:S(2)}) %collective-permute-start) | collective-permute-done | bytes 262176 | tf_op jit(solution)/shard_map/ppermute | solution.py:329
  14.5 0.6 triangle.1
  15.1 0.7 collective-permute-start.9
  16.3 5.2 %collective-permute-start.2 = (f32[512,128]{1,0:T(8,128)S(1)}, f32[512,128]{1,0:T(8,128)S(1)}, u32[]{:S(2)}, u32[]{:S(2)}) collective-permute-start(f32[512,128]{1,0:T(8,128)S(1)} %collective-permute-done.1.refs_2_), channel_id=1, source_target_pairs={{0,2},{1,3},{2,0},{3,1},{4,6},{5,7},{6,4},{7,5},{8,10},{9,11},{10,... | collective-permute-start | bytes 786440 | tf_op jit(solution)/shard_map/ppermute | solution.py:344
  21.5 10.5 %collective-permute-start.10 = (f32[640,128]{1,0:T(8,128)S(1)}, f32[640,128]{1,0:T(8,128)S(1)}, u32[]{:S(2)}, u32[]{:S(2)}) collective-permute-start(f32[640,128]{1,0:T(8,128)S(1)} %collective-permute-done.9.ta), channel_id=1, source_target_pairs={{0,1},{1,0},{2,3},{3,2},{4,5},{5,4},{6,7},{7,6},{8,9},{9,8},{10,11... | collective-permute-start | bytes 983048 | tf_op jit(solution)/shard_map/ppermute | solution.py:315
  32.0 1.9 %collective-permute-start.3 = (f32[512,128]{1,0:T(8,128)S(1)}, f32[512,128]{1,0:T(8,128)S(1)}, u32[]{:S(2)}, u32[]{:S(2)}) collective-permute-start(f32[512,128]{1,0:T(8,128)S(1)} %get-tuple-element.14.refs_0_.own_ref), channel_id=1, source_target_pairs={{0,1},{1,0},{2,3},{3,2},{4,5},{5,4},{6,7},{7,6},{8,9},{9,8},{10,11... | collective-permute-start | bytes 786440 | tf_op jit(solution)/shard_map/ppermute | solution.py:315
  34.0 2.4 %collective-permute-start.4 = (f32[512,128]{1,0:T(8,128)S(1)}, f32[512,128]{1,0:T(8,128)S(1)}, u32[]{:S(2)}, u32[]{:S(2)}) collective-permute-start(f32[512,128]{1,0:T(8,128)S(1)} %collective-permute-done.refs_1_.near_ref), channel_id=1, source_target_pairs={{0,1},{1,0},{2,3},{3,2},{4,5},{5,4},{6,7},{7,6},{8,9},{9,8},{10,11... | collective-permute-start | bytes 786440 | tf_op jit(solution)/shard_map/ppermute | solution.py:315
  36.4 1.9 %collective-permute-start.5 = (f32[512,128]{1,0:T(8,128)S(1)}, f32[512,128]{1,0:T(8,128)S(1)}, u32[]{:S(2)}, u32[]{:S(2)}) collective-permute-start(f32[512,128]{1,0:T(8,128)S(1)} %collective-permute-done.1.refs_2_), channel_id=1, source_target_pairs={{0,1},{1,0},{2,3},{3,2},{4,5},{5,4},{6,7},{7,6},{8,9},{9,8},{10,11... | collective-permute-start | bytes 786440 | tf_op jit(solution)/shard_map/ppermute | solution.py:315
  38.3 3.5 %collective-permute-start.6 = (f32[512,128]{1,0:T(8,128)S(1)}, f32[512,128]{1,0:T(8,128)S(1)}, u32[]{:S(2)}, u32[]{:S(2)}) collective-permute-start(f32[512,128]{1,0:T(8,128)S(1)} %collective-permute-done.2.refs_3_), channel_id=1, source_target_pairs={{0,1},{1,0},{2,3},{3,2},{4,5},{5,4},{6,7},{7,6},{8,9},{9,8},{10,11... | collective-permute-start | bytes 786440 | tf_op jit(solution)/shard_map/ppermute | solution.py:315
  41.8 1.1 collective-permute-done.6.refs_7_
  42.9 3.9 %square.1 = (f32[512,512]{1,0:T(8,128)S(1)}, f32[512,512]{1,0:T(8,128)S(1)}, bf16[512,512]{1,0:T(8,128)(2,1)S(1)}, bf16[512,512]{1,0:T(8,128)(2,1)S(1)}, f32[512,512]{1,0:T(8,128)}, /*index=5*/f32[1,128]{1,0:T(1,128)S(1)}) custom-call(s32[76]{0:T(128)S(1)} %concatenate.3.s_ref, f32[512,128]{1,0:T(8,128)S(1)} %get-tuple-element.14.refs_0_.own_ref, ...), custom_call_target="tpu_custom_call" | custom-call | tf_op jit(solution)/shard_map/square/pallas_call | solution.py:349
  46.9 1.2 %copy-done = f32[512,512]{1,0:T(8,128)S(1)} copy-done((f32[512,512]{1,0:T(8,128)S(1)}, f32[512,512]{1,0:T(8,128)}, u32[]{:S(2)}) %copy-start) | copy-done | bytes 1048600
  48.1 6.6 %second.1 = (f32[2,512,128]{2,1,0:T(8,128)S(1)}, f32[512,128]{1,0:T(8,128)S(1)}, f32[512,128]{1,0:T(8,128)S(1)}, f32[96,128]{1,0:T(8,128)S(1)}) custom-call(s32[76]{0:T(128)S(1)} %concatenate.3.s_ref, f32[512,512]{1,0:T(8,128)S(1)} %get-tuple-element.15.p1_ref, f32[512,512]{1,0:T(8,128)S(1)} %get-tuple-element.16.v_ref, ...), custom_call_target="tpu_custom_call" | custom-call | tf_op jit(solution)/shard_map/second/pallas_call | solution.py:367
  54.7 0.7 collective-permute-start.11
  55.4 12.6 %collective-permute-start.12 = (f32[512,128]{1,0:T(8,128)S(1)}, f32[512,128]{1,0:T(8,128)S(1)}, u32[]{:S(2)}, u32[]{:S(2)}) collective-permute-start(f32[512,128]{1,0:T(8,128)S(1)} %get-tuple-element.24), channel_id=1, source_target_pairs={{0,7},{1,6},{2,5},{3,4},{4,3},{5,2},{6,1},{7,0},{8,15},{9,14},{10,... | collective-permute-start | bytes 786440 | tf_op jit(solution)/shard_map/ppermute | solution.py:384
  68.0 44.4 %all_to_all.11 = f32[96,1,128]{2,1,0:T(1,128)S(1)} all-to-all(f32[96,1,128]{2,1,0:T(1,128)S(1)} %bitcast.13), channel_id=1, replica_groups=mesh['row'=96,'col'=8] {'row'}, dimensions={0} | all-to-all | bytes 98304 | tf_op jit(solution)/shard_map/all_to_all | solution.py:385
  112.4 1.5 %last.1 = (f32[8,2,64,64]{3,2,1,0:T(8,128)}, f32[2]{0:T(128)}) custom-call(s32[76]{0:T(128)S(1)} %concatenate.3.s_ref, f32[2,512,128]{2,1,0:T(8,128)S(1)} %get-tuple-element.22.own_ref, f32[512,128]{1,0:T(8,128)S(1)} %collective-permute-done.11.far_ref, f32[512,128]{1,0:T(8,128)S(1)} %collective-permute-done.12.near_ref, f32[96,128]{1,0:T(8,128)S(1)} %bitcast.12), custom_call_target="tpu_custom_call" | custom-call | tf_op jit(solution)/shard_map/last/pallas_call | solution.py:386
  (20 shorter events, 0.9 us)
Async XLA Ops:
  0.6 1.0 copy-start.1
  1.8 14.4 %collective-permute-start.1 = (f32[512,128]{1,0:T(8,128)S(1)}, f32[512,128]{1,0:T(8,128)S(1)}, u32[]{:S(2)}, u32[]{:S(2)}) collective-permute-start(f32[512,128]{1,0:T(8,128)S(1)} %get-tuple-element.14.refs_0_.own_ref), channel_id=1, source_target_pairs={{0,4},{1,5},{2,6},{3,7},{4,0},{5,1},{6,2},{7,3},{8,12},{9,13},{10,... | collective-permute-start | bytes 786440 | tf_op jit(solution)/shard_map/ppermute | solution.py:330
  6.9 7.6 %collective-permute-start = (f32[512,128]{1,0:T(8,128)S(1)}, f32[512,128]{1,0:T(8,128)S(1)}, u32[]{:S(2)}, u32[]{:S(2)}) collective-permute-start(f32[512,128]{1,0:T(8,128)S(1)} %get-tuple-element.14.refs_0_.own_ref), channel_id=1, source_target_pairs={{0,2},{1,3},{2,0},{3,1},{4,6},{5,7},{6,4},{7,5},{8,10},{9,11},{10,... | collective-permute-start | bytes 786440 | tf_op jit(solution)/shard_map/ppermute | solution.py:329
  10.1 3.0 %collective-permute-start.7 = (f32[256,128]{1,0:T(8,128)S(1)}, f32[256,128]{1,0:T(8,128)S(1)}, u32[]{:S(2)}, u32[]{:S(2)}) collective-permute-start(f32[256,128]{1,0:T(8,128)S(1)} %get-tuple-element.21), channel_id=1, source_target_pairs={{4,2},{12,10},{20,18},{28,26},{36,34},{44,42},{52,50},{60,58},{68,... | collective-permute-start | bytes 393224 | tf_op jit(solution)/shard_map/ppermute | solution.py:331
  10.8 2.3 %collective-permute-start.8 = (f32[256,128]{1,0:T(8,128)S(1)}, f32[256,128]{1,0:T(8,128)S(1)}, u32[]{:S(2)}, u32[]{:S(2)}) collective-permute-start(f32[256,128]{1,0:T(8,128)S(1)} %get-tuple-element.21), channel_id=1, source_target_pairs={{4,0},{12,8},{20,16},{28,24},{36,32},{44,40},{52,48},{60,56},{68,6... | collective-permute-start | bytes 393224 | tf_op jit(solution)/shard_map/ppermute | solution.py:332
  11.5 0.7 copy-start.2
  12.2 0.7 copy-start.3
  15.1 6.4 %collective-permute-start.9 = (f32[640,128]{1,0:T(8,128)S(1)}, f32[640,128]{1,0:T(8,128)S(1)}, u32[]{:S(2)}, u32[]{:S(2)}) collective-permute-start(f32[640,128]{1,0:T(8,128)S(1)} %triangle.1), channel_id=1, source_target_pairs={{4,8},{5,9},{6,10},{7,11},{12,16},{13,17},{14,18},{15,19},{20,24},... | collective-permute-start | bytes 983048 | tf_op jit(solution)/shard_map/ppermute | solution.py:343
  16.3 22.1 %collective-permute-start.2 = (f32[512,128]{1,0:T(8,128)S(1)}, f32[512,128]{1,0:T(8,128)S(1)}, u32[]{:S(2)}, u32[]{:S(2)}) collective-permute-start(f32[512,128]{1,0:T(8,128)S(1)} %collective-permute-done.1.refs_2_), channel_id=1, source_target_pairs={{0,2},{1,3},{2,0},{3,1},{4,6},{5,7},{6,4},{7,5},{8,10},{9,11},{10,... | collective-permute-start | bytes 786440 | tf_op jit(solution)/shard_map/ppermute | solution.py:344
  21.5 25.4 %collective-permute-start.10 = (f32[640,128]{1,0:T(8,128)S(1)}, f32[640,128]{1,0:T(8,128)S(1)}, u32[]{:S(2)}, u32[]{:S(2)}) collective-permute-start(f32[640,128]{1,0:T(8,128)S(1)} %collective-permute-done.9.ta), channel_id=1, source_target_pairs={{0,1},{1,0},{2,3},{3,2},{4,5},{5,4},{6,7},{7,6},{8,9},{9,8},{10,11... | collective-permute-start | bytes 983048 | tf_op jit(solution)/shard_map/ppermute | solution.py:315
  32.0 9.7 %collective-permute-start.3 = (f32[512,128]{1,0:T(8,128)S(1)}, f32[512,128]{1,0:T(8,128)S(1)}, u32[]{:S(2)}, u32[]{:S(2)}) collective-permute-start(f32[512,128]{1,0:T(8,128)S(1)} %get-tuple-element.14.refs_0_.own_ref), channel_id=1, source_target_pairs={{0,1},{1,0},{2,3},{3,2},{4,5},{5,4},{6,7},{7,6},{8,9},{9,8},{10,11... | collective-permute-start | bytes 786440 | tf_op jit(solution)/shard_map/ppermute | solution.py:315
  34.0 7.8 %collective-permute-start.4 = (f32[512,128]{1,0:T(8,128)S(1)}, f32[512,128]{1,0:T(8,128)S(1)}, u32[]{:S(2)}, u32[]{:S(2)}) collective-permute-start(f32[512,128]{1,0:T(8,128)S(1)} %collective-permute-done.refs_1_.near_ref), channel_id=1, source_target_pairs={{0,1},{1,0},{2,3},{3,2},{4,5},{5,4},{6,7},{7,6},{8,9},{9,8},{10,11... | collective-permute-start | bytes 786440 | tf_op jit(solution)/shard_map/ppermute | solution.py:315
  36.4 5.4 %collective-permute-start.5 = (f32[512,128]{1,0:T(8,128)S(1)}, f32[512,128]{1,0:T(8,128)S(1)}, u32[]{:S(2)}, u32[]{:S(2)}) collective-permute-start(f32[512,128]{1,0:T(8,128)S(1)} %collective-permute-done.1.refs_2_), channel_id=1, source_target_pairs={{0,1},{1,0},{2,3},{3,2},{4,5},{5,4},{6,7},{7,6},{8,9},{9,8},{10,11... | collective-permute-start | bytes 786440 | tf_op jit(solution)/shard_map/ppermute | solution.py:315
  38.3 4.6 %collective-permute-start.6 = (f32[512,128]{1,0:T(8,128)S(1)}, f32[512,128]{1,0:T(8,128)S(1)}, u32[]{:S(2)}, u32[]{:S(2)}) collective-permute-start(f32[512,128]{1,0:T(8,128)S(1)} %collective-permute-done.2.refs_3_), channel_id=1, source_target_pairs={{0,1},{1,0},{2,3},{3,2},{4,5},{5,4},{6,7},{7,6},{8,9},{9,8},{10,11... | collective-permute-start | bytes 786440 | tf_op jit(solution)/shard_map/ppermute | solution.py:315
  46.9 1.2 %copy-start = (f32[512,512]{1,0:T(8,128)S(1)}, f32[512,512]{1,0:T(8,128)}, u32[]{:S(2)}) copy-start(f32[512,512]{1,0:T(8,128)} %get-tuple-element.19.pv_ref) | copy-start | bytes 3145732
  54.7 57.7 %collective-permute-start.11 = (f32[512,128]{1,0:T(8,128)S(1)}, f32[512,128]{1,0:T(8,128)S(1)}, u32[]{:S(2)}, u32[]{:S(2)}) collective-permute-start(f32[512,128]{1,0:T(8,128)S(1)} %get-tuple-element.23), channel_id=1, source_target_pairs={{7,8},{6,9},{5,10},{4,11},{15,16},{14,17},{13,18},{12,19},{23,24},... | collective-permute-start | bytes 786440 | tf_op jit(solution)/shard_map/ppermute | solution.py:383
  55.4 57.0 %collective-permute-start.12 = (f32[512,128]{1,0:T(8,128)S(1)}, f32[512,128]{1,0:T(8,128)S(1)}, u32[]{:S(2)}, u32[]{:S(2)}) collective-permute-start(f32[512,128]{1,0:T(8,128)S(1)} %get-tuple-element.24), channel_id=1, source_target_pairs={{0,7},{1,6},{2,5},{3,4},{4,3},{5,2},{6,1},{7,0},{8,15},{9,14},{10,... | collective-permute-start | bytes 786440 | tf_op jit(solution)/shard_map/ppermute | solution.py:384

commit v4 on v3

--- a/solution.py
+++ b/solution.py
@@ -324,27 +324,30 @@
 
     packed, diag = pl.pallas_call(
         pack_kernel, out_shape=[shape(N, 128), shape(256, 128)], in_specs=[VMEM],
-        out_specs=[VMEM] * 2, compiler_params=params(16), name="pack",
+        out_specs=[VMEM] * 2, compiler_params=params(8), name="pack",
     )(values)
     near = lax.ppermute(packed, "col", [(c, c ^ 2) for c in range(8)])
-    cross = lax.ppermute(packed, "col", [(c, c ^ 4) for c in range(8)])
     d1 = lax.ppermute(diag, "col", [(4, 2)])
     d2 = lax.ppermute(diag, "col", [(4, 0)])
+    later, d1 = lax.optimization_barrier((packed, d1))
+    cross = lax.ppermute(later, "col", [(c, c ^ 4) for c in range(8)])
+    near, packed2 = lax.optimization_barrier((near, swap(later)))
     triangle = pl.pallas_call(
         triangle_kernel,
         out_shape=shape(640, 128),
         in_specs=[SMEM] + [VMEM] * 4,
         out_specs=VMEM,
         scratch_shapes=[pltpu.VMEM((N, 128), F32)] * 2,
-        compiler_params=params(16),
+        compiler_params=params(8),
         name="triangle",
     )(scalars, packed, near, d1, d2)
     pairs = [(index(r, c + 4), index(r + 1, c)) for r, c in ends]
     ta = lax.ppermute(triangle, both, pairs + [(b, a) for a, b in pairs])
+    near, triangle = lax.optimization_barrier((near, triangle))
+    cross, near2 = lax.optimization_barrier((cross, swap(near)))
     forward = lax.ppermute(cross, "col", [(c, c ^ 2) for c in range(8)])
     mine = [packed, near, cross, forward]
-    others = [swap(x) for x in mine]
-    tb = swap(ta)
+    others = [packed2, near2, swap(cross), swap(forward)]
 
     *old, trace = pl.pallas_call(
         square_kernel,
@@ -360,10 +363,12 @@
             pltpu.VMEM((N, W), BF16),
             pltpu.VMEM((N, W), BF16),
         ],
-        compiler_params=params(48),
+        compiler_params=params(24),
         name="square",
     )(scalars, *mine, *others)
 
+    ta, trace = lax.optimization_barrier((ta, trace))
+    tb = swap(ta)
     own, far, near, sums = pl.pallas_call(
         second_kernel,
         out_shape=[shape(2, N, 128), shape(N, 128), shape(N, 128), shape(rows, 128)],
@@ -375,7 +380,7 @@
             pltpu.VMEM((18 * B, 2 * N), BF16),
             pltpu.VMEM((18 * B, 2 * N), BF16),
         ],
-        compiler_params=params(48),
+        compiler_params=params(24),
         name="second",
     )(scalars, *old, trace, ta, tb)
 
@@ -388,7 +393,7 @@
         out_shape=[shape(H, 2, B, B), shape(2)],
         in_specs=[SMEM] + [VMEM] * 4,
         out_specs=[VMEM, SMEM],
-        compiler_params=params(16),
+        compiler_params=params(8),
         name="last",
     )(scalars, own, far, near, sums)
 

time: 115 us -> 114 us (level)
  waiting for transfers between devices: 2.99 us -> 19.6 us
  blocking collectives: 44.4 us -> 35.1 us
  starting transfers between devices: 49 us -> 42.5 us
  local copies, waits for them, and re-layouts: 3.86 us -> 2.62 us
    all_to_all x1, blocking collectives: 44.4 us -> 35.1 us  [per_device(): sums = lax.all_to_all(sums, 'row', 0, 0, tiled=True)]
    ppermute x1, waiting for transfers between devices: 0.49 us -> 9.41 us  [per_device(): cross = lax.ppermute(later, 'col', [(c, c ^ 4) for c in range(8)])]
    ppermute x1, waiting for transfers between devices: 0.01 us -> 7.77 us  [per_device(): forward = lax.ppermute(cross, 'col', [(c, c ^ 2) for c in range(8)])]
    ppermute x1, starting transfers between devices: 12.6 us -> 5.4 us  [per_device(): near = lax.ppermute(near, 'col', [(c, 7 - c) for c in range(8)])]
    ppermute x1, starting transfers between devices: 5.24 us -> 2.49 us  [per_device(): forward = lax.ppermute(cross, 'col', [(c, c ^ 2) for c in range(8)])]
    ppermute x5, starting transfers between devices: 20.2 us -> 22.7 us  [swap(): return lax.ppermute(x, 'col', [(c, c ^ 1) for c in range(8)])]
    ppermute x1, waiting for transfers between devices: 1.36 us -> 0.01 us  [per_device(): near = lax.ppermute(packed, 'col', [(c, c ^ 2) for c in range(8)])]
    ppermute x5, waiting for transfers between devices: 1.12 us -> 2.37 us  [swap(): return lax.ppermute(x, 'col', [(c, c ^ 1) for c in range(8)])]
  transfers between devices with their start and end apart: 13 -> 13, of which waited for: 3 -> 4; matrix products, arithmetic and copies ran while one was open for 0% -> 0% of each run, Pallas kernels for 4% -> 4%
where the time goes in v4:
time: 114 us
  starting transfers between devices  42.5 us (37%)
  blocking collectives  35.1 us (31%)
  waiting for transfers between devices  19.6 us (17%)
  Pallas kernels  12.8 us (11%)
  local copies, waits for them, and re-layouts  2.62 us (2%)
    all_to_all x1, blocking collectives, per_device(): sums = lax.all_to_all(sums, 'row', 0, 0, tiled=True)  35.1 us
    ppermute x5, starting transfers between devices, swap(): return lax.ppermute(x, 'col', [(c, c ^ 1) for c in range(8)])  22.7 us
    ppermute x1, waiting for transfers between devices, per_device(): cross = lax.ppermute(later, 'col', [(c, c ^ 4) for c in range(8)])  9.41 us
    ppermute x1, waiting for transfers between devices, per_device(): forward = lax.ppermute(cross, 'col', [(c, c ^ 2) for c in range(8)])  7.77 us
    pallas_call x1, Pallas kernels, per_device(): pl.pallas_call(second_kernel, out_shape=[shape(2, N, 128), shape(N, 128),...  6.6 us
    ppermute x1, starting transfers between devices, per_device(): near = lax.ppermute(near, 'col', [(c, 7 - c) for c in range(8)])  5.4 us
    ppermute x1, starting transfers between devices, per_device(): cross = lax.ppermute(later, 'col', [(c, c ^ 4) for c in range(8)])  5.17 us
    ppermute x1, starting transfers between devices, per_device(): near = lax.ppermute(packed, 'col', [(c, c ^ 2) for c in range(8)])  4.03 us
  transfers between devices with their start and end apart: 13, of which 4 were waited for; matrix products, arithmetic and copies ran while one was open for 0% of the time, Pallas kernels for 4%

profile of v4, /device:TPU:1, one launch (start us, length us, event | category | flops | bytes accessed | tf_op | source)
XLA Modules:
  0.0 113.5 jit_solution(1808817306477298982)
XLA Ops:
  0.6 1.0 copy-done
  1.8 0.7 collective-permute-start.1
  2.5 0.7 collective-permute-start.3
  3.2 4.0 %collective-permute-start = (f32[512,128]{1,0:T(8,128)S(1)}, f32[512,128]{1,0:T(8,128)S(1)}, u32[]{:S(2)}, u32[]{:S(2)}) collective-permute-start(f32[512,128]{1,0:T(8,128)S(1)} %get-tuple-element.25.own_ref.refs_0_), channel_id=1, source_target_pairs={{0,2},{1,3},{2,0},{3,1},{4,6},{5,7},{6,4},{7,5},{8,10},{9,11},{10,... | collective-permute-start | bytes 786440 | tf_op jit(solution)/shard_map/ppermute | solution.py:329
  7.3 0.7 copy-done.1
  8.0 10.9 %collective-permute-start.2 = (f32[512,128]{1,0:T(8,128)S(1)}, f32[512,128]{1,0:T(8,128)S(1)}, u32[]{:S(2)}, u32[]{:S(2)}) collective-permute-start(f32[512,128]{1,0:T(8,128)S(1)} %get-tuple-element.25.own_ref.refs_0_), channel_id=1, source_target_pairs={{0,1},{1,0},{2,3},{3,2},{4,5},{5,4},{6,7},{7,6},{8,9},{9,8},{10,11... | collective-permute-start | bytes 786440 | tf_op jit(solution)/shard_map/ppermute | solution.py:315
  19.0 0.7 copy-done.2
  19.8 5.2 %collective-permute-start.4 = (f32[512,128]{1,0:T(8,128)S(1)}, f32[512,128]{1,0:T(8,128)S(1)}, u32[]{:S(2)}, u32[]{:S(2)}) collective-permute-start(f32[512,128]{1,0:T(8,128)S(1)} %get-tuple-element.25.own_ref.refs_0_), channel_id=1, source_target_pairs={{0,4},{1,5},{2,6},{3,7},{4,0},{5,1},{6,2},{7,3},{8,12},{9,13},{10,... | collective-permute-start | bytes 786440 | tf_op jit(solution)/shard_map/ppermute | solution.py:333
  25.7 2.2 %collective-permute-start.5 = (f32[512,128]{1,0:T(8,128)S(1)}, f32[512,128]{1,0:T(8,128)S(1)}, u32[]{:S(2)}, u32[]{:S(2)}) collective-permute-start(f32[512,128]{1,0:T(8,128)S(1)} %collective-permute-done.near_ref.refs_1_), channel_id=1, source_target_pairs={{0,1},{1,0},{2,3},{3,2},{4,5},{5,4},{6,7},{7,6},{8,9},{9,8},{10,11... | collective-permute-start | bytes 786440 | tf_op jit(solution)/shard_map/ppermute | solution.py:315
  27.9 9.4 %collective-permute-done.4.refs_2_ = f32[512,128]{1,0:T(8,128)S(1)} collective-permute-done((f32[512,128]{1,0:T(8,128)S(1)}, f32[512,128]{1,0:T(8,128)S(1)}, u32[]{:S(2)}, u32[]{:S(2)}) %collective-permute-start.4) | collective-permute-done | bytes 262176 | tf_op jit(solution)/shard_map/ppermute | solution.py:333
  37.3 2.5 %collective-permute-start.6 = (f32[512,128]{1,0:T(8,128)S(1)}, f32[512,128]{1,0:T(8,128)S(1)}, u32[]{:S(2)}, u32[]{:S(2)}) collective-permute-start(f32[512,128]{1,0:T(8,128)S(1)} %collective-permute-done.4.refs_2_), channel_id=1, source_target_pairs={{0,2},{1,3},{2,0},{3,1},{4,6},{5,7},{6,4},{7,5},{8,10},{9,11},{10,... | collective-permute-start | bytes 786440 | tf_op jit(solution)/shard_map/ppermute | solution.py:348
  39.8 0.7 collective-permute-start.9
  40.5 2.7 %collective-permute-start.7 = (f32[512,128]{1,0:T(8,128)S(1)}, f32[512,128]{1,0:T(8,128)S(1)}, u32[]{:S(2)}, u32[]{:S(2)}) collective-permute-start(f32[512,128]{1,0:T(8,128)S(1)} %collective-permute-done.4.refs_2_), channel_id=1, source_target_pairs={{0,1},{1,0},{2,3},{3,2},{4,5},{5,4},{6,7},{7,6},{8,9},{9,8},{10,11... | collective-permute-start | bytes 786440 | tf_op jit(solution)/shard_map/ppermute | solution.py:315
  43.1 7.8 %collective-permute-done.6.refs_3_ = f32[512,128]{1,0:T(8,128)S(1)} collective-permute-done((f32[512,128]{1,0:T(8,128)S(1)}, f32[512,128]{1,0:T(8,128)S(1)}, u32[]{:S(2)}, u32[]{:S(2)}) %collective-permute-start.6) | collective-permute-done | bytes 262176 | tf_op jit(solution)/shard_map/ppermute | solution.py:348
  50.9 4.7 %collective-permute-start.8 = (f32[512,128]{1,0:T(8,128)S(1)}, f32[512,128]{1,0:T(8,128)S(1)}, u32[]{:S(2)}, u32[]{:S(2)}) collective-permute-start(f32[512,128]{1,0:T(8,128)S(1)} %collective-permute-done.6.refs_3_), channel_id=1, source_target_pairs={{0,1},{1,0},{2,3},{3,2},{4,5},{5,4},{6,7},{7,6},{8,9},{9,8},{10,11... | collective-permute-start | bytes 786440 | tf_op jit(solution)/shard_map/ppermute | solution.py:315
  55.6 1.1 collective-permute-done.8.refs_7_
  56.7 3.9 %square.1 = (f32[512,512]{1,0:T(8,128)S(1)}, f32[512,512]{1,0:T(8,128)S(1)}, bf16[512,512]{1,0:T(8,128)(2,1)S(1)}, bf16[512,512]{1,0:T(8,128)(2,1)S(1)}, f32[512,512]{1,0:T(8,128)S(1)}, /*index=5*/f32[1,128]{1,0:T(1,128)S(1)}) custom-call(s32[76]{0:T(128)S(1)} %concatenate.3.s_ref, f32[512,128]{1,0:T(8,128)S(1)} %get-tuple-element.25.own_ref.refs_0_, ...), custom_call_target="tpu_custom_call" | custom-call | tf_op jit(solution)/shard_map/square/pallas_call | solution.py:352
  60.7 2.3 %collective-permute-start.10 = (f32[640,128]{1,0:T(8,128)S(1)}, f32[640,128]{1,0:T(8,128)S(1)}, u32[]{:S(2)}, u32[]{:S(2)}) collective-permute-start(f32[640,128]{1,0:T(8,128)S(1)} %collective-permute-done.9.ta), channel_id=1, source_target_pairs={{0,1},{1,0},{2,3},{3,2},{4,5},{5,4},{6,7},{7,6},{8,9},{9,8},{10,11... | collective-permute-start | bytes 983048 | tf_op jit(solution)/shard_map/ppermute | solution.py:315
  62.9 1.2 %collective-permute-done.10.tb = f32[640,128]{1,0:T(8,128)S(1)} collective-permute-done((f32[640,128]{1,0:T(8,128)S(1)}, f32[640,128]{1,0:T(8,128)S(1)}, u32[]{:S(2)}, u32[]{:S(2)}) %collective-permute-start.10) | collective-permute-done | bytes 327712 | tf_op jit(solution)/shard_map/ppermute | solution.py:315
  64.2 6.6 %second.1 = (f32[2,512,128]{2,1,0:T(8,128)S(1)}, f32[512,128]{1,0:T(8,128)S(1)}, f32[512,128]{1,0:T(8,128)S(1)}, f32[96,128]{1,0:T(8,128)S(1)}) custom-call(s32[76]{0:T(128)S(1)} %concatenate.3.s_ref, f32[512,512]{1,0:T(8,128)S(1)} %get-tuple-element.32.p1_ref, f32[512,512]{1,0:T(8,128)S(1)} %get-tuple-element.33.v_ref, ...), custom_call_target="tpu_custom_call" | custom-call | tf_op jit(solution)/shard_map/second/pallas_call | solution.py:372
  70.8 0.7 collective-permute-start.11
  71.5 5.4 %collective-permute-start.12 = (f32[512,128]{1,0:T(8,128)S(1)}, f32[512,128]{1,0:T(8,128)S(1)}, u32[]{:S(2)}, u32[]{:S(2)}) collective-permute-start(f32[512,128]{1,0:T(8,128)S(1)} %get-tuple-element.42), channel_id=1, source_target_pairs={{0,7},{1,6},{2,5},{3,4},{4,3},{5,2},{6,1},{7,0},{8,15},{9,14},{10,... | collective-permute-start | bytes 786440 | tf_op jit(solution)/shard_map/ppermute | solution.py:389
  76.9 35.1 %all_to_all.11 = f32[96,1,128]{2,1,0:T(1,128)S(1)} all-to-all(f32[96,1,128]{2,1,0:T(1,128)S(1)} %bitcast.13), channel_id=1, replica_groups=mesh['row'=96,'col'=8] {'row'}, dimensions={0} | all-to-all | bytes 98304 | tf_op jit(solution)/shard_map/all_to_all | solution.py:390
  112.0 1.5 %last.1 = (f32[8,2,64,64]{3,2,1,0:T(8,128)}, f32[2]{0:T(128)}) custom-call(s32[76]{0:T(128)S(1)} %concatenate.3.s_ref, f32[2,512,128]{2,1,0:T(8,128)S(1)} %get-tuple-element.40.own_ref, f32[512,128]{1,0:T(8,128)S(1)} %collective-permute-done.11.far_ref, f32[512,128]{1,0:T(8,128)S(1)} %collective-permute-done.12.near_ref, f32[96,128]{1,0:T(8,128)S(1)} %bitcast.12), custom_call_target="tpu_custom_call" | custom-call | tf_op jit(solution)/shard_map/last/pallas_call | solution.py:391
  (18 shorter events, 1.0 us)
Async XLA Ops:
  0.6 1.0 copy-start
  1.8 6.2 %collective-permute-start.1 = (f32[256,128]{1,0:T(8,128)S(1)}, f32[256,128]{1,0:T(8,128)S(1)}, u32[]{:S(2)}, u32[]{:S(2)}) collective-permute-start(f32[256,128]{1,0:T(8,128)S(1)} %get-tuple-element.24), channel_id=1, source_target_pairs={{4,2},{12,10},{20,18},{28,26},{36,34},{44,42},{52,50},{60,58},{68,... | collective-permute-start | bytes 393224 | tf_op jit(solution)/shard_map/ppermute | solution.py:330
  2.5 22.5 %collective-permute-start.3 = (f32[256,128]{1,0:T(8,128)S(1)}, f32[256,128]{1,0:T(8,128)S(1)}, u32[]{:S(2)}, u32[]{:S(2)}) collective-permute-start(f32[256,128]{1,0:T(8,128)S(1)} %get-tuple-element.24), channel_id=1, source_target_pairs={{4,0},{12,8},{20,16},{28,24},{36,32},{44,40},{52,48},{60,56},{68,6... | collective-permute-start | bytes 393224 | tf_op jit(solution)/shard_map/ppermute | solution.py:331
  3.2 21.8 %collective-permute-start = (f32[512,128]{1,0:T(8,128)S(1)}, f32[512,128]{1,0:T(8,128)S(1)}, u32[]{:S(2)}, u32[]{:S(2)}) collective-permute-start(f32[512,128]{1,0:T(8,128)S(1)} %get-tuple-element.25.own_ref.refs_0_), channel_id=1, source_target_pairs={{0,2},{1,3},{2,0},{3,1},{4,6},{5,7},{6,4},{7,5},{8,10},{9,11},{10,... | collective-permute-start | bytes 786440 | tf_op jit(solution)/shard_map/ppermute | solution.py:329
  7.2 0.7 copy-start.1
  8.0 17.0 %collective-permute-start.2 = (f32[512,128]{1,0:T(8,128)S(1)}, f32[512,128]{1,0:T(8,128)S(1)}, u32[]{:S(2)}, u32[]{:S(2)}) collective-permute-start(f32[512,128]{1,0:T(8,128)S(1)} %get-tuple-element.25.own_ref.refs_0_), channel_id=1, source_target_pairs={{0,1},{1,0},{2,3},{3,2},{4,5},{5,4},{6,7},{7,6},{8,9},{9,8},{10,11... | collective-permute-start | bytes 786440 | tf_op jit(solution)/shard_map/ppermute | solution.py:315
  19.0 0.7 copy-start.2
  19.8 17.4 %collective-permute-start.4 = (f32[512,128]{1,0:T(8,128)S(1)}, f32[512,128]{1,0:T(8,128)S(1)}, u32[]{:S(2)}, u32[]{:S(2)}) collective-permute-start(f32[512,128]{1,0:T(8,128)S(1)} %get-tuple-element.25.own_ref.refs_0_), channel_id=1, source_target_pairs={{0,4},{1,5},{2,6},{3,7},{4,0},{5,1},{6,2},{7,3},{8,12},{9,13},{10,... | collective-permute-start | bytes 786440 | tf_op jit(solution)/shard_map/ppermute | solution.py:333
  25.7 11.6 %collective-permute-start.5 = (f32[512,128]{1,0:T(8,128)S(1)}, f32[512,128]{1,0:T(8,128)S(1)}, u32[]{:S(2)}, u32[]{:S(2)}) collective-permute-start(f32[512,128]{1,0:T(8,128)S(1)} %collective-permute-done.near_ref.refs_1_), channel_id=1, source_target_pairs={{0,1},{1,0},{2,3},{3,2},{4,5},{5,4},{6,7},{7,6},{8,9},{9,8},{10,11... | collective-permute-start | bytes 786440 | tf_op jit(solution)/shard_map/ppermute | solution.py:315
  37.3 13.6 %collective-permute-start.6 = (f32[512,128]{1,0:T(8,128)S(1)}, f32[512,128]{1,0:T(8,128)S(1)}, u32[]{:S(2)}, u32[]{:S(2)}) collective-permute-start(f32[512,128]{1,0:T(8,128)S(1)} %collective-permute-done.4.refs_2_), channel_id=1, source_target_pairs={{0,2},{1,3},{2,0},{3,1},{4,6},{5,7},{6,4},{7,5},{8,10},{9,11},{10,... | collective-permute-start | bytes 786440 | tf_op jit(solution)/shard_map/ppermute | solution.py:348
  39.8 20.9 %collective-permute-start.9 = (f32[640,128]{1,0:T(8,128)S(1)}, f32[640,128]{1,0:T(8,128)S(1)}, u32[]{:S(2)}, u32[]{:S(2)}) collective-permute-start(f32[640,128]{1,0:T(8,128)S(1)} %triangle.1), channel_id=1, source_target_pairs={{4,8},{5,9},{6,10},{7,11},{12,16},{13,17},{14,18},{15,19},{20,24},... | collective-permute-start | bytes 983048 | tf_op jit(solution)/shard_map/ppermute | solution.py:345
  40.5 15.1 %collective-permute-start.7 = (f32[512,128]{1,0:T(8,128)S(1)}, f32[512,128]{1,0:T(8,128)S(1)}, u32[]{:S(2)}, u32[]{:S(2)}) collective-permute-start(f32[512,128]{1,0:T(8,128)S(1)} %collective-permute-done.4.refs_2_), channel_id=1, source_target_pairs={{0,1},{1,0},{2,3},{3,2},{4,5},{5,4},{6,7},{7,6},{8,9},{9,8},{10,11... | collective-permute-start | bytes 786440 | tf_op jit(solution)/shard_map/ppermute | solution.py:315
  50.9 5.8 %collective-permute-start.8 = (f32[512,128]{1,0:T(8,128)S(1)}, f32[512,128]{1,0:T(8,128)S(1)}, u32[]{:S(2)}, u32[]{:S(2)}) collective-permute-start(f32[512,128]{1,0:T(8,128)S(1)} %collective-permute-done.6.refs_3_), channel_id=1, source_target_pairs={{0,1},{1,0},{2,3},{3,2},{4,5},{5,4},{6,7},{7,6},{8,9},{9,8},{10,11... | collective-permute-start | bytes 786440 | tf_op jit(solution)/shard_map/ppermute | solution.py:315
  60.7 3.5 %collective-permute-start.10 = (f32[640,128]{1,0:T(8,128)S(1)}, f32[640,128]{1,0:T(8,128)S(1)}, u32[]{:S(2)}, u32[]{:S(2)}) collective-permute-start(f32[640,128]{1,0:T(8,128)S(1)} %collective-permute-done.9.ta), channel_id=1, source_target_pairs={{0,1},{1,0},{2,3},{3,2},{4,5},{5,4},{6,7},{7,6},{8,9},{9,8},{10,11... | collective-permute-start | bytes 983048 | tf_op jit(solution)/shard_map/ppermute | solution.py:315
  70.8 41.2 %collective-permute-start.11 = (f32[512,128]{1,0:T(8,128)S(1)}, f32[512,128]{1,0:T(8,128)S(1)}, u32[]{:S(2)}, u32[]{:S(2)}) collective-permute-start(f32[512,128]{1,0:T(8,128)S(1)} %get-tuple-element.41), channel_id=1, source_target_pairs={{7,8},{6,9},{5,10},{4,11},{15,16},{14,17},{13,18},{12,19},{23,24},... | collective-permute-start | bytes 786440 | tf_op jit(solution)/shard_map/ppermute | solution.py:388
  71.5 40.5 %collective-permute-start.12 = (f32[512,128]{1,0:T(8,128)S(1)}, f32[512,128]{1,0:T(8,128)S(1)}, u32[]{:S(2)}, u32[]{:S(2)}) collective-permute-start(f32[512,128]{1,0:T(8,128)S(1)} %get-tuple-element.42), channel_id=1, source_target_pairs={{0,7},{1,6},{2,5},{3,4},{4,3},{5,2},{6,1},{7,0},{8,15},{9,14},{10,... | collective-permute-start | bytes 786440 | tf_op jit(solution)/shard_map/ppermute | solution.py:389

commit v5 on v4

--- a/solution.py
+++ b/solution.py
@@ -16,8 +16,13 @@
 RAD, BR = 4, (28, 52)
 
 
-def params(mib):
-    return pltpu.CompilerParams(vmem_limit_bytes=mib << 20)
+def call(kernel, mib, name, **rest):
+    return pl.pallas_call(
+        kernel,
+        name=name,
+        compiler_params=pltpu.CompilerParams(vmem_limit_bytes=mib << 20),
+        **rest,
+    )
 
 
 def halves(x):
@@ -322,34 +327,34 @@
 
     ends = [(r, c) for r in range(rows - 1) for c in range(4)]
 
-    packed, diag = pl.pallas_call(
+    packed, diag = call(
         pack_kernel, out_shape=[shape(N, 128), shape(256, 128)], in_specs=[VMEM],
-        out_specs=[VMEM] * 2, compiler_params=params(8), name="pack",
+        out_specs=[VMEM] * 2, mib=8, name="pack",
     )(values)
     near = lax.ppermute(packed, "col", [(c, c ^ 2) for c in range(8)])
     d1 = lax.ppermute(diag, "col", [(4, 2)])
     d2 = lax.ppermute(diag, "col", [(4, 0)])
     later, d1 = lax.optimization_barrier((packed, d1))
     cross = lax.ppermute(later, "col", [(c, c ^ 4) for c in range(8)])
-    near, packed2 = lax.optimization_barrier((near, swap(later)))
-    triangle = pl.pallas_call(
+    triangle = call(
         triangle_kernel,
         out_shape=shape(640, 128),
         in_specs=[SMEM] + [VMEM] * 4,
         out_specs=VMEM,
         scratch_shapes=[pltpu.VMEM((N, 128), F32)] * 2,
-        compiler_params=params(8),
-        name="triangle",
+        mib=8, name="triangle",
     )(scalars, packed, near, d1, d2)
     pairs = [(index(r, c + 4), index(r + 1, c)) for r, c in ends]
     ta = lax.ppermute(triangle, both, pairs + [(b, a) for a, b in pairs])
-    near, triangle = lax.optimization_barrier((near, triangle))
-    cross, near2 = lax.optimization_barrier((cross, swap(near)))
+    packed, near, triangle = lax.optimization_barrier((packed, near, triangle))
+    packed2, near2 = swap(packed), swap(near)
+    cross, packed2, near2 = lax.optimization_barrier((cross, packed2, near2))
     forward = lax.ppermute(cross, "col", [(c, c ^ 2) for c in range(8)])
+    forward, ta, cross2 = lax.optimization_barrier((forward, ta, swap(cross)))
     mine = [packed, near, cross, forward]
-    others = [packed2, near2, swap(cross), swap(forward)]
-
-    *old, trace = pl.pallas_call(
+    others = [packed2, near2, cross2, swap(forward)]
+
+    *old, trace = call(
         square_kernel,
         out_shape=[
             shape(N, N), shape(N, N), jax.ShapeDtypeStruct((N, N), BF16),
@@ -363,13 +368,11 @@
             pltpu.VMEM((N, W), BF16),
             pltpu.VMEM((N, W), BF16),
         ],
-        compiler_params=params(24),
-        name="square",
+        mib=24, name="square",
     )(scalars, *mine, *others)
 
-    ta, trace = lax.optimization_barrier((ta, trace))
     tb = swap(ta)
-    own, far, near, sums = pl.pallas_call(
+    own, far, near, sums = call(
         second_kernel,
         out_shape=[shape(2, N, 128), shape(N, 128), shape(N, 128), shape(rows, 128)],
         in_specs=[SMEM] + [VMEM] * 8,
@@ -380,21 +383,19 @@
             pltpu.VMEM((18 * B, 2 * N), BF16),
             pltpu.VMEM((18 * B, 2 * N), BF16),
         ],
-        compiler_params=params(24),
-        name="second",
+        mib=24, name="second",
     )(scalars, *old, trace, ta, tb)
 
     pairs = [(index(r, 7 - c), index(r + 1, c)) for r, c in ends]
     far = lax.ppermute(far, both, pairs + [(b, a) for a, b in pairs])
     near = lax.ppermute(near, "col", [(c, 7 - c) for c in range(8)])
     sums = lax.all_to_all(sums, "row", 0, 0, tiled=True)
-    return pl.pallas_call(
+    return call(
         last_kernel,
         out_shape=[shape(H, 2, B, B), shape(2)],
         in_specs=[SMEM] + [VMEM] * 4,
         out_specs=[VMEM, SMEM],
-        compiler_params=params(8),
-        name="last",
+        mib=8, name="last",
     )(scalars, own, far, near, sums)
 
 

time: 114 us -> 109 us (0.956)
  waiting for transfers between devices: 19.6 us -> 11.9 us
    ppermute x1, waiting for transfers between devices: 9.41 us -> 0.01 us  [per_device(): cross = lax.ppermute(later, 'col', [(c, c ^ 4) for c in range(8)])]
    ppermute x1, starting transfers between devices: 5.4 us -> 8.07 us  [per_device(): near = lax.ppermute(near, 'col', [(c, 7 - c) for c in range(8)])]
    ppermute x1, waiting for transfers between devices: 7.77 us -> 9.57 us  [per_device(): forward = lax.ppermute(cross, 'col', [(c, c ^ 2) for c in range(8)])]
  transfers between devices with their start and end apart: 13 -> 13, of which waited for: 4 -> 3; matrix products, arithmetic and copies ran while one was open for 0% -> 0% of each run, Pallas kernels for 4% -> 4%
where the time goes in v5:
time: 109 us; the launch traced here: 108 us
  starting transfers between devices  43.6 us (40%)
  blocking collectives  36.2 us (33%)
  Pallas kernels  12.8 us (12%)
  waiting for transfers between devices  11.9 us (11%)
  local copies, waits for them, and re-layouts  2.64 us (2%)
    all_to_all x1, blocking collectives, per_device(): sums = lax.all_to_all(sums, 'row', 0, 0, tiled=True)  36.2 us
    ppermute x5, starting transfers between devices, swap(): return lax.ppermute(x, 'col', [(c, c ^ 1) for c in range(8)])  22 us
    ppermute x1, waiting for transfers between devices, per_device(): forward = lax.ppermute(cross, 'col', [(c, c ^ 2) for c in range(8)])  9.57 us
    ppermute x1, starting transfers between devices, per_device(): near = lax.ppermute(near, 'col', [(c, 7 - c) for c in range(8)])  8.07 us
    pallas_call x1, Pallas kernels, per_device(): call(second_kernel, out_shape=[shape(2, N, 128), shape(N, 128), shape(N,...  6.6 us
    ppermute x1, starting transfers between devices, per_device(): cross = lax.ppermute(later, 'col', [(c, c ^ 4) for c in range(8)])  4.22 us
    ppermute x1, starting transfers between devices, per_device(): near = lax.ppermute(packed, 'col', [(c, c ^ 2) for c in range(8)])  4.03 us
    pallas_call x1, Pallas kernels, per_device(): call(square_kernel, out_shape=[shape(N, N), shape(N, N), jax.ShapeDtypeSt...  3.94 us
  transfers between devices with their start and end apart: 13, of which 3 were waited for; matrix products, arithmetic and copies ran while one was open for 0% of the time, Pallas kernels for 4%

profile of v5, /device:TPU:1, one launch (start us, length us, event | category | flops | bytes accessed | tf_op | source)
XLA Modules:
  0.0 108.0 jit_solution(10674412496067876014)
XLA Ops:
  0.6 1.0 copy-done
  1.8 0.7 collective-permute-start.1
  2.5 0.7 collective-permute-start.2
  3.2 4.0 %collective-permute-start = (f32[512,128]{1,0:T(8,128)S(1)}, f32[512,128]{1,0:T(8,128)S(1)}, u32[]{:S(2)}, u32[]{:S(2)}) collective-permute-start(f32[512,128]{1,0:T(8,128)S(1)} %get-tuple-element.29.own_ref.refs_0_), channel_id=1, source_target_pairs={{0,2},{1,3},{2,0},{3,1},{4,6},{5,7},{6,4},{7,5},{8,10},{9,11},{10,... | collective-permute-start | bytes 786440 | tf_op jit(solution)/shard_map/ppermute | solution.py:334
  7.3 0.7 copy-done.1
  8.0 0.7 copy-done.2
  8.9 4.2 %collective-permute-start.3 = (f32[512,128]{1,0:T(8,128)S(1)}, f32[512,128]{1,0:T(8,128)S(1)}, u32[]{:S(2)}, u32[]{:S(2)}) collective-permute-start(f32[512,128]{1,0:T(8,128)S(1)} %get-tuple-element.29.own_ref.refs_0_), channel_id=1, source_target_pairs={{0,4},{1,5},{2,6},{3,7},{4,0},{5,1},{6,2},{7,3},{8,12},{9,13},{10,... | collective-permute-start | bytes 786440 | tf_op jit(solution)/shard_map/ppermute | solution.py:338
  13.1 0.6 triangle.1
  13.7 13.2 %collective-permute-start.4 = (f32[512,128]{1,0:T(8,128)S(1)}, f32[512,128]{1,0:T(8,128)S(1)}, u32[]{:S(2)}, u32[]{:S(2)}) collective-permute-start(f32[512,128]{1,0:T(8,128)S(1)} %get-tuple-element.29.own_ref.refs_0_), channel_id=1, source_target_pairs={{0,1},{1,0},{2,3},{3,2},{4,5},{5,4},{6,7},{7,6},{8,9},{9,8},{10,11... | collective-permute-start | bytes 786440 | tf_op jit(solution)/shard_map/ppermute | solution.py:320
  27.0 1.9 %collective-permute-start.5 = (f32[512,128]{1,0:T(8,128)S(1)}, f32[512,128]{1,0:T(8,128)S(1)}, u32[]{:S(2)}, u32[]{:S(2)}) collective-permute-start(f32[512,128]{1,0:T(8,128)S(1)} %collective-permute-done.near_ref.refs_1_), channel_id=1, source_target_pairs={{0,1},{1,0},{2,3},{3,2},{4,5},{5,4},{6,7},{7,6},{8,9},{9,8},{10,11... | collective-permute-start | bytes 786440 | tf_op jit(solution)/shard_map/ppermute | solution.py:320
  28.9 0.7 collective-permute-start.7
  29.6 0.8 collective-permute-done.5.refs_5_
  30.4 2.6 %collective-permute-start.6 = (f32[512,128]{1,0:T(8,128)S(1)}, f32[512,128]{1,0:T(8,128)S(1)}, u32[]{:S(2)}, u32[]{:S(2)}) collective-permute-start(f32[512,128]{1,0:T(8,128)S(1)} %collective-permute-done.3.refs_2_), channel_id=1, source_target_pairs={{0,2},{1,3},{2,0},{3,1},{4,6},{5,7},{6,4},{7,5},{8,10},{9,11},{10,... | collective-permute-start | bytes 786440 | tf_op jit(solution)/shard_map/ppermute | solution.py:352
  33.0 2.4 %collective-permute-start.8 = (f32[512,128]{1,0:T(8,128)S(1)}, f32[512,128]{1,0:T(8,128)S(1)}, u32[]{:S(2)}, u32[]{:S(2)}) collective-permute-start(f32[512,128]{1,0:T(8,128)S(1)} %collective-permute-done.3.refs_2_), channel_id=1, source_target_pairs={{0,1},{1,0},{2,3},{3,2},{4,5},{5,4},{6,7},{7,6},{8,9},{9,8},{10,11... | collective-permute-start | bytes 786440 | tf_op jit(solution)/shard_map/ppermute | solution.py:320
  35.3 9.6 %collective-permute-done.6.refs_3_ = f32[512,128]{1,0:T(8,128)S(1)} collective-permute-done((f32[512,128]{1,0:T(8,128)S(1)}, f32[512,128]{1,0:T(8,128)S(1)}, u32[]{:S(2)}, u32[]{:S(2)}) %collective-permute-start.6) | collective-permute-done | bytes 262176 | tf_op jit(solution)/shard_map/ppermute | solution.py:352
  44.9 2.6 %collective-permute-start.10 = (f32[640,128]{1,0:T(8,128)S(1)}, f32[640,128]{1,0:T(8,128)S(1)}, u32[]{:S(2)}, u32[]{:S(2)}) collective-permute-start(f32[640,128]{1,0:T(8,128)S(1)} %collective-permute-done.7.ta), channel_id=1, source_target_pairs={{0,1},{1,0},{2,3},{3,2},{4,5},{5,4},{6,7},{7,6},{8,9},{9,8},{10,11... | collective-permute-start | bytes 983048 | tf_op jit(solution)/shard_map/ppermute | solution.py:320
  47.5 1.9 %collective-permute-start.9 = (f32[512,128]{1,0:T(8,128)S(1)}, f32[512,128]{1,0:T(8,128)S(1)}, u32[]{:S(2)}, u32[]{:S(2)}) collective-permute-start(f32[512,128]{1,0:T(8,128)S(1)} %collective-permute-done.6.refs_3_), channel_id=1, source_target_pairs={{0,1},{1,0},{2,3},{3,2},{4,5},{5,4},{6,7},{7,6},{8,9},{9,8},{10,11... | collective-permute-start | bytes 786440 | tf_op jit(solution)/shard_map/ppermute | solution.py:320
  49.5 1.5 %collective-permute-done.9.refs_7_ = f32[512,128]{1,0:T(8,128)S(1)} collective-permute-done((f32[512,128]{1,0:T(8,128)S(1)}, f32[512,128]{1,0:T(8,128)S(1)}, u32[]{:S(2)}, u32[]{:S(2)}) %collective-permute-start.9) | collective-permute-done | bytes 262176 | tf_op jit(solution)/shard_map/ppermute | solution.py:320
  51.0 3.9 %square.1 = (f32[512,512]{1,0:T(8,128)S(1)}, f32[512,512]{1,0:T(8,128)S(1)}, bf16[512,512]{1,0:T(8,128)(2,1)S(1)}, bf16[512,512]{1,0:T(8,128)(2,1)S(1)}, f32[512,512]{1,0:T(8,128)S(1)}, /*index=5*/f32[1,128]{1,0:T(1,128)S(1)}) custom-call(s32[76]{0:T(128)S(1)} %concatenate.3.s_ref, f32[512,128]{1,0:T(8,128)S(1)} %get-tuple-element.29.own_ref.refs_0_, ...), custom_call_target="tpu_custom_call" | custom-call | tf_op jit(solution)/shard_map/square/pallas_call | solution.py:357
  54.9 6.6 %second.1 = (f32[2,512,128]{2,1,0:T(8,128)S(1)}, f32[512,128]{1,0:T(8,128)S(1)}, f32[512,128]{1,0:T(8,128)S(1)}, f32[96,128]{1,0:T(8,128)S(1)}) custom-call(s32[76]{0:T(128)S(1)} %concatenate.3.s_ref, f32[512,512]{1,0:T(8,128)S(1)} %get-tuple-element.35.p1_ref, f32[512,512]{1,0:T(8,128)S(1)} %get-tuple-element.36.v_ref, ...), custom_call_target="tpu_custom_call" | custom-call | tf_op jit(solution)/shard_map/second/pallas_call | solution.py:375
  61.5 0.7 collective-permute-start.11
  62.2 8.1 %collective-permute-start.12 = (f32[512,128]{1,0:T(8,128)S(1)}, f32[512,128]{1,0:T(8,128)S(1)}, u32[]{:S(2)}, u32[]{:S(2)}) collective-permute-start(f32[512,128]{1,0:T(8,128)S(1)} %get-tuple-element.44), channel_id=1, source_target_pairs={{0,7},{1,6},{2,5},{3,4},{4,3},{5,2},{6,1},{7,0},{8,15},{9,14},{10,... | collective-permute-start | bytes 786440 | tf_op jit(solution)/shard_map/ppermute | solution.py:391
  70.3 36.2 %all_to_all.11 = f32[96,1,128]{2,1,0:T(1,128)S(1)} all-to-all(f32[96,1,128]{2,1,0:T(1,128)S(1)} %bitcast.13), channel_id=1, replica_groups=mesh['row'=96,'col'=8] {'row'}, dimensions={0} | all-to-all | bytes 98304 | tf_op jit(solution)/shard_map/all_to_all | solution.py:392
  106.5 1.5 %last.1 = (f32[8,2,64,64]{3,2,1,0:T(8,128)}, f32[2]{0:T(128)}) custom-call(s32[76]{0:T(128)S(1)} %concatenate.3.s_ref, f32[2,512,128]{2,1,0:T(8,128)S(1)} %get-tuple-element.42.own_ref, f32[512,128]{1,0:T(8,128)S(1)} %collective-permute-done.11.far_ref, f32[512,128]{1,0:T(8,128)S(1)} %collective-permute-done.12.near_ref, f32[96,128]{1,0:T(8,128)S(1)} %bitcast.12), custom_call_target="tpu_custom_call" | custom-call | tf_op jit(solution)/shard_map/last/pallas_call | solution.py:393
  (18 shorter events, 0.4 us)
Async XLA Ops:
  0.6 1.0 copy-start
  1.8 7.0 %collective-permute-start.1 = (f32[256,128]{1,0:T(8,128)S(1)}, f32[256,128]{1,0:T(8,128)S(1)}, u32[]{:S(2)}, u32[]{:S(2)}) collective-permute-start(f32[256,128]{1,0:T(8,128)S(1)} %get-tuple-element.25), channel_id=1, source_target_pairs={{4,2},{12,10},{20,18},{28,26},{36,34},{44,42},{52,50},{60,58},{68,... | collective-permute-start | bytes 393224 | tf_op jit(solution)/shard_map/ppermute | solution.py:335
  2.5 10.6 %collective-permute-start.2 = (f32[256,128]{1,0:T(8,128)S(1)}, f32[256,128]{1,0:T(8,128)S(1)}, u32[]{:S(2)}, u32[]{:S(2)}) collective-permute-start(f32[256,128]{1,0:T(8,128)S(1)} %get-tuple-element.25), channel_id=1, source_target_pairs={{4,0},{12,8},{20,16},{28,24},{36,32},{44,40},{52,48},{60,56},{68,6... | collective-permute-start | bytes 393224 | tf_op jit(solution)/shard_map/ppermute | solution.py:336
  3.2 9.9 %collective-permute-start = (f32[512,128]{1,0:T(8,128)S(1)}, f32[512,128]{1,0:T(8,128)S(1)}, u32[]{:S(2)}, u32[]{:S(2)}) collective-permute-start(f32[512,128]{1,0:T(8,128)S(1)} %get-tuple-element.29.own_ref.refs_0_), channel_id=1, source_target_pairs={{0,2},{1,3},{2,0},{3,1},{4,6},{5,7},{6,4},{7,5},{8,10},{9,11},{10,... | collective-permute-start | bytes 786440 | tf_op jit(solution)/shard_map/ppermute | solution.py:334
  7.2 0.7 copy-start.1
  8.0 0.7 copy-start.2
  8.9 20.7 %collective-permute-start.3 = (f32[512,128]{1,0:T(8,128)S(1)}, f32[512,128]{1,0:T(8,128)S(1)}, u32[]{:S(2)}, u32[]{:S(2)}) collective-permute-start(f32[512,128]{1,0:T(8,128)S(1)} %get-tuple-element.29.own_ref.refs_0_), channel_id=1, source_target_pairs={{0,4},{1,5},{2,6},{3,7},{4,0},{5,1},{6,2},{7,3},{8,12},{9,13},{10,... | collective-permute-start | bytes 786440 | tf_op jit(solution)/shard_map/ppermute | solution.py:338
  13.7 15.9 %collective-permute-start.4 = (f32[512,128]{1,0:T(8,128)S(1)}, f32[512,128]{1,0:T(8,128)S(1)}, u32[]{:S(2)}, u32[]{:S(2)}) collective-permute-start(f32[512,128]{1,0:T(8,128)S(1)} %get-tuple-element.29.own_ref.refs_0_), channel_id=1, source_target_pairs={{0,1},{1,0},{2,3},{3,2},{4,5},{5,4},{6,7},{7,6},{8,9},{9,8},{10,11... | collective-permute-start | bytes 786440 | tf_op jit(solution)/shard_map/ppermute | solution.py:320
  27.0 3.4 %collective-permute-start.5 = (f32[512,128]{1,0:T(8,128)S(1)}, f32[512,128]{1,0:T(8,128)S(1)}, u32[]{:S(2)}, u32[]{:S(2)}) collective-permute-start(f32[512,128]{1,0:T(8,128)S(1)} %collective-permute-done.near_ref.refs_1_), channel_id=1, source_target_pairs={{0,1},{1,0},{2,3},{3,2},{4,5},{5,4},{6,7},{7,6},{8,9},{9,8},{10,11... | collective-permute-start | bytes 786440 | tf_op jit(solution)/shard_map/ppermute | solution.py:320
  28.9 6.4 %collective-permute-start.7 = (f32[640,128]{1,0:T(8,128)S(1)}, f32[640,128]{1,0:T(8,128)S(1)}, u32[]{:S(2)}, u32[]{:S(2)}) collective-permute-start(f32[640,128]{1,0:T(8,128)S(1)} %triangle.1), channel_id=1, source_target_pairs={{4,8},{5,9},{6,10},{7,11},{12,16},{13,17},{14,18},{15,19},{20,24},... | collective-permute-start | bytes 983048 | tf_op jit(solution)/shard_map/ppermute | solution.py:348
  30.4 14.5 %collective-permute-start.6 = (f32[512,128]{1,0:T(8,128)S(1)}, f32[512,128]{1,0:T(8,128)S(1)}, u32[]{:S(2)}, u32[]{:S(2)}) collective-permute-start(f32[512,128]{1,0:T(8,128)S(1)} %collective-permute-done.3.refs_2_), channel_id=1, source_target_pairs={{0,2},{1,3},{2,0},{3,1},{4,6},{5,7},{6,4},{7,5},{8,10},{9,11},{10,... | collective-permute-start | bytes 786440 | tf_op jit(solution)/shard_map/ppermute | solution.py:352
  33.0 11.9 %collective-permute-start.8 = (f32[512,128]{1,0:T(8,128)S(1)}, f32[512,128]{1,0:T(8,128)S(1)}, u32[]{:S(2)}, u32[]{:S(2)}) collective-permute-start(f32[512,128]{1,0:T(8,128)S(1)} %collective-permute-done.3.refs_2_), channel_id=1, source_target_pairs={{0,1},{1,0},{2,3},{3,2},{4,5},{5,4},{6,7},{7,6},{8,9},{9,8},{10,11... | collective-permute-start | bytes 786440 | tf_op jit(solution)/shard_map/ppermute | solution.py:320
  44.9 10.0 %collective-permute-start.10 = (f32[640,128]{1,0:T(8,128)S(1)}, f32[640,128]{1,0:T(8,128)S(1)}, u32[]{:S(2)}, u32[]{:S(2)}) collective-permute-start(f32[640,128]{1,0:T(8,128)S(1)} %collective-permute-done.7.ta), channel_id=1, source_target_pairs={{0,1},{1,0},{2,3},{3,2},{4,5},{5,4},{6,7},{7,6},{8,9},{9,8},{10,11... | collective-permute-start | bytes 983048 | tf_op jit(solution)/shard_map/ppermute | solution.py:320
  47.5 3.4 %collective-permute-start.9 = (f32[512,128]{1,0:T(8,128)S(1)}, f32[512,128]{1,0:T(8,128)S(1)}, u32[]{:S(2)}, u32[]{:S(2)}) collective-permute-start(f32[512,128]{1,0:T(8,128)S(1)} %collective-permute-done.6.refs_3_), channel_id=1, source_target_pairs={{0,1},{1,0},{2,3},{3,2},{4,5},{5,4},{6,7},{7,6},{8,9},{9,8},{10,11... | collective-permute-start | bytes 786440 | tf_op jit(solution)/shard_map/ppermute | solution.py:320
  61.5 45.0 %collective-permute-start.11 = (f32[512,128]{1,0:T(8,128)S(1)}, f32[512,128]{1,0:T(8,128)S(1)}, u32[]{:S(2)}, u32[]{:S(2)}) collective-permute-start(f32[512,128]{1,0:T(8,128)S(1)} %get-tuple-element.43), channel_id=1, source_target_pairs={{7,8},{6,9},{5,10},{4,11},{15,16},{14,17},{13,18},{12,19},{23,24},... | collective-permute-start | bytes 786440 | tf_op jit(solution)/shard_map/ppermute | solution.py:390
  62.2 44.3 %collective-permute-start.12 = (f32[512,128]{1,0:T(8,128)S(1)}, f32[512,128]{1,0:T(8,128)S(1)}, u32[]{:S(2)}, u32[]{:S(2)}) collective-permute-start(f32[512,128]{1,0:T(8,128)S(1)} %get-tuple-element.44), channel_id=1, source_target_pairs={{0,7},{1,6},{2,5},{3,4},{4,3},{5,2},{6,1},{7,0},{8,15},{9,14},{10,... | collective-permute-start | bytes 786440 | tf_op jit(solution)/shard_map/ppermute | solution.py:391

commit v6 on v5

--- a/solution.py
+++ b/solution.py
@@ -82,24 +82,26 @@
     def _():
         out_ref[0:256, :] = rows(high, 3, 6)
         out_ref[256:512, :] = d1_ref[...] + d2_ref[...]
-        out_ref[512:640, :] = jnp.zeros((128, 128), F32)
+        out_ref[512:576, :] = jnp.zeros((B, 128), F32)
 
     @pl.when((upper == 0) & (core == 1))
     def _():
         out_ref[0:384, :] = rows(high, 1, 6)
         out_ref[384:512, :] = rows(low, 5, 6)
-        out_ref[512:640, :] = jnp.zeros((128, 128), F32)
+        out_ref[512:576, :] = jnp.zeros((B, 128), F32)
 
     @pl.when((upper == 1) & (core == 0))
     def _():
-        out_ref[0:448, :] = rows(low, 1, 7)
-        out_ref[448:640, :] = rows(high, 1, 3)
+        out_ref[0:384, :] = rows(low, 1, 6)
+        out_ref[384:512, :] = rows(high, 1, 2)
+        last = jnp.concatenate([rows(high, 3, 3)[:, :B], rows(low, 7, 7)[:, :B]], axis=1)
+        out_ref[512:576, :] = last
 
     @pl.when((upper == 1) & (core == 1))
     def _():
         out_ref[0:320, :] = rows(low, 1, 5)
         out_ref[320:384, :] = rows(high, 1, 1)
-        out_ref[384:640, :] = jnp.zeros((256, 128), F32)
+        out_ref[384:576, :] = jnp.zeros((192, 128), F32)
 
 
 def square_kernel(s_ref, *refs):
@@ -168,10 +170,12 @@
         w_ref[strip(0), :] = jnp.zeros((B, N), F32)
         for k in range(1, H):
             parts = [line(0, k - 1), zero, zero, zero]
+            if k == 7:
+                parts[0] = pltpu.roll(line(0, 8), B, 1)
             if k < 6:
                 parts[1] = line(1, k - 1)
             if k < 4:
-                parts[2] = line(0, 6 + k)
+                parts[2] = line(0, 5 + k)
             if k < 2:
                 parts[3] = line(1, 4 + k)
             turned = pltpu.roll(jnp.concatenate(parts, axis=1), k * B, 1)
@@ -338,7 +342,7 @@
     cross = lax.ppermute(later, "col", [(c, c ^ 4) for c in range(8)])
     triangle = call(
         triangle_kernel,
-        out_shape=shape(640, 128),
+        out_shape=shape(576, 128),
         in_specs=[SMEM] + [VMEM] * 4,
         out_specs=VMEM,
         scratch_shapes=[pltpu.VMEM((N, 128), F32)] * 2,
@@ -346,13 +350,12 @@
     )(scalars, packed, near, d1, d2)
     pairs = [(index(r, c + 4), index(r + 1, c)) for r, c in ends]
     ta = lax.ppermute(triangle, both, pairs + [(b, a) for a, b in pairs])
-    packed, near, triangle = lax.optimization_barrier((packed, near, triangle))
-    packed2, near2 = swap(packed), swap(near)
-    cross, packed2, near2 = lax.optimization_barrier((cross, packed2, near2))
+    packed, near, cross, triangle = lax.optimization_barrier((packed, near, cross, triangle))
     forward = lax.ppermute(cross, "col", [(c, c ^ 2) for c in range(8)])
-    forward, ta, cross2 = lax.optimization_barrier((forward, ta, swap(cross)))
+    swapped = [swap(packed), swap(near), swap(cross)]
+    forward, ta, *swapped = lax.optimization_barrier((forward, ta, *swapped))
     mine = [packed, near, cross, forward]
-    others = [packed2, near2, cross2, swap(forward)]
+    others = swapped + [swap(forward)]
 
     *old, trace = call(
         square_kernel,
@@ -378,7 +381,7 @@
         in_specs=[SMEM] + [VMEM] * 8,
         out_specs=[VMEM] * 4,
         scratch_shapes=[
-            pltpu.VMEM((2, 640, 128), F32),
+            pltpu.VMEM((2, 576, 128), F32),
             pltpu.VMEM((N, N), F32),
             pltpu.VMEM((18 * B, 2 * N), BF16),
             pltpu.VMEM((18 * B, 2 * N), BF16),

time: 109 us -> 102 us (0.936)
  waiting for transfers between devices: 11.9 us -> 7.17 us
  blocking collectives: 36.2 us -> 32.9 us
    ppermute x1, waiting for transfers between devices: 9.57 us -> 0.01 us  [per_device(): forward = lax.ppermute(cross, 'col', [(c, c ^ 2) for c in range(8)])]
    ppermute x1, waiting for transfers between devices: 0.01 us -> 4.67 us  [per_device(): cross = lax.ppermute(later, 'col', [(c, c ^ 4) for c in range(8)])]
    all_to_all x1, blocking collectives: 36.2 us -> 32.9 us  [per_device(): sums = lax.all_to_all(sums, 'row', 0, 0, tiled=True)]
    ppermute x5, starting transfers between devices: 22 us -> 24.1 us  [swap(): return lax.ppermute(x, 'col', [(c, c ^ 1) for c in range(8)])]
  transfers between devices with their start and end apart: 13 -> 13, of which waited for: 3 -> 3; matrix products, arithmetic and copies ran while one was open for 0% -> 0% of each run, Pallas kernels for 4% -> 5%
where the time goes in v6:
time: 102 us; the launch traced here: 101 us
  starting transfers between devices  44.2 us (43%)
  blocking collectives  32.9 us (32%)
  Pallas kernels  12.9 us (13%)
  waiting for transfers between devices  7.17 us (7%)
  local copies, waits for them, and re-layouts  2.62 us (3%)
    all_to_all x1, blocking collectives, per_device(): sums = lax.all_to_all(sums, 'row', 0, 0, tiled=True)  32.9 us
    ppermute x5, starting transfers between devices, swap(): return lax.ppermute(x, 'col', [(c, c ^ 1) for c in range(8)])  24.1 us
    ppermute x1, starting transfers between devices, per_device(): near = lax.ppermute(near, 'col', [(c, 7 - c) for c in range(8)])  7.23 us
    pallas_call x1, Pallas kernels, per_device(): call(second_kernel, out_shape=[shape(2, N, 128), shape(N, 128), shape(N,...  6.64 us
    ppermute x1, waiting for transfers between devices, per_device(): cross = lax.ppermute(later, 'col', [(c, c ^ 4) for c in range(8)])  4.67 us
    ppermute x1, starting transfers between devices, per_device(): cross = lax.ppermute(later, 'col', [(c, c ^ 4) for c in range(8)])  4.21 us
    ppermute x1, starting transfers between devices, per_device(): near = lax.ppermute(packed, 'col', [(c, c ^ 2) for c in range(8)])  4.03 us
    pallas_call x1, Pallas kernels, per_device(): call(square_kernel, out_shape=[shape(N, N), shape(N, N), jax.ShapeDtypeSt...  3.94 us
  transfers between devices with their start and end apart: 13, of which 3 were waited for; matrix products, arithmetic and copies ran while one was open for 0% of the time, Pallas kernels for 5%

profile of v6, /device:TPU:1, one launch (start us, length us, event | category | flops | bytes accessed | tf_op | source)
XLA Modules:
  0.0 100.6 jit_solution(15513545346001514479)
XLA Ops:
  0.6 1.0 %copy-done = f32[8,2,64,64]{3,2,1,0:T(8,128)S(1)} copy-done((f32[8,2,64,64]{3,2,1,0:T(8,128)S(1)}, f32[8,2,64,64]{3,2,1,0:T(8,128)}, u32[]{:S(2)}) %copy-start) | copy-done | bytes 262168
  1.8 0.7 collective-permute-start.1
  2.5 0.7 collective-permute-start.3
  3.2 4.0 %collective-permute-start = (f32[512,128]{1,0:T(8,128)S(1)}, f32[512,128]{1,0:T(8,128)S(1)}, u32[]{:S(2)}, u32[]{:S(2)}) collective-permute-start(f32[512,128]{1,0:T(8,128)S(1)} %get-tuple-element.28.own_ref.refs_0_), channel_id=1, source_target_pairs={{0,2},{1,3},{2,0},{3,1},{4,6},{5,7},{6,4},{7,5},{8,10},{9,11},{10,... | collective-permute-start | bytes 786440 | tf_op jit(solution)/shard_map/ppermute | solution.py:338
  7.3 0.7 copy-done.1
  8.0 4.2 %collective-permute-start.2 = (f32[512,128]{1,0:T(8,128)S(1)}, f32[512,128]{1,0:T(8,128)S(1)}, u32[]{:S(2)}, u32[]{:S(2)}) collective-permute-start(f32[512,128]{1,0:T(8,128)S(1)} %get-tuple-element.28.own_ref.refs_0_), channel_id=1, source_target_pairs={{0,4},{1,5},{2,6},{3,7},{4,0},{5,1},{6,2},{7,3},{8,12},{9,13},{10,... | collective-permute-start | bytes 786440 | tf_op jit(solution)/shard_map/ppermute | solution.py:342
  12.3 0.7 copy-done.2
  13.1 0.6 triangle.1
  13.7 0.7 collective-permute-start.5
  14.4 4.7 %collective-permute-done.2.refs_2_ = f32[512,128]{1,0:T(8,128)S(1)} collective-permute-done((f32[512,128]{1,0:T(8,128)S(1)}, f32[512,128]{1,0:T(8,128)S(1)}, u32[]{:S(2)}, u32[]{:S(2)}) %collective-permute-start.2) | collective-permute-done | bytes 262176 | tf_op jit(solution)/shard_map/ppermute | solution.py:342
  19.1 1.9 %collective-permute-start.4 = (f32[512,128]{1,0:T(8,128)S(1)}, f32[512,128]{1,0:T(8,128)S(1)}, u32[]{:S(2)}, u32[]{:S(2)}) collective-permute-start(f32[512,128]{1,0:T(8,128)S(1)} %collective-permute-done.2.refs_2_), channel_id=1, source_target_pairs={{0,2},{1,3},{2,0},{3,1},{4,6},{5,7},{6,4},{7,5},{8,10},{9,11},{10,... | collective-permute-start | bytes 786440 | tf_op jit(solution)/shard_map/ppermute | solution.py:354
  21.0 15.5 %collective-permute-start.6 = (f32[512,128]{1,0:T(8,128)S(1)}, f32[512,128]{1,0:T(8,128)S(1)}, u32[]{:S(2)}, u32[]{:S(2)}) collective-permute-start(f32[512,128]{1,0:T(8,128)S(1)} %get-tuple-element.28.own_ref.refs_0_), channel_id=1, source_target_pairs={{0,1},{1,0},{2,3},{3,2},{4,5},{5,4},{6,7},{7,6},{8,9},{9,8},{10,11... | collective-permute-start | bytes 786440 | tf_op jit(solution)/shard_map/ppermute | solution.py:324
  36.5 1.9 %collective-permute-start.7 = (f32[512,128]{1,0:T(8,128)S(1)}, f32[512,128]{1,0:T(8,128)S(1)}, u32[]{:S(2)}, u32[]{:S(2)}) collective-permute-start(f32[512,128]{1,0:T(8,128)S(1)} %collective-permute-done.near_ref.refs_1_), channel_id=1, source_target_pairs={{0,1},{1,0},{2,3},{3,2},{4,5},{5,4},{6,7},{7,6},{8,9},{9,8},{10,11... | collective-permute-start | bytes 786440 | tf_op jit(solution)/shard_map/ppermute | solution.py:324
  38.4 2.4 %collective-permute-start.8 = (f32[512,128]{1,0:T(8,128)S(1)}, f32[512,128]{1,0:T(8,128)S(1)}, u32[]{:S(2)}, u32[]{:S(2)}) collective-permute-start(f32[512,128]{1,0:T(8,128)S(1)} %collective-permute-done.2.refs_2_), channel_id=1, source_target_pairs={{0,1},{1,0},{2,3},{3,2},{4,5},{5,4},{6,7},{7,6},{8,9},{9,8},{10,11... | collective-permute-start | bytes 786440 | tf_op jit(solution)/shard_map/ppermute | solution.py:324
  40.9 1.1 %collective-permute-done.8.refs_6_ = f32[512,128]{1,0:T(8,128)S(1)} collective-permute-done((f32[512,128]{1,0:T(8,128)S(1)}, f32[512,128]{1,0:T(8,128)S(1)}, u32[]{:S(2)}, u32[]{:S(2)}) %collective-permute-start.8) | collective-permute-done | bytes 262176 | tf_op jit(solution)/shard_map/ppermute | solution.py:324
  42.0 2.3 %collective-permute-start.10 = (f32[576,128]{1,0:T(8,128)S(1)}, f32[576,128]{1,0:T(8,128)S(1)}, u32[]{:S(2)}, u32[]{:S(2)}) collective-permute-start(f32[576,128]{1,0:T(8,128)S(1)} %collective-permute-done.5.ta), channel_id=1, source_target_pairs={{0,1},{1,0},{2,3},{3,2},{4,5},{5,4},{6,7},{7,6},{8,9},{9,8},{10,11... | collective-permute-start | bytes 884744 | tf_op jit(solution)/shard_map/ppermute | solution.py:324
  44.3 2.0 %collective-permute-start.9 = (f32[512,128]{1,0:T(8,128)S(1)}, f32[512,128]{1,0:T(8,128)S(1)}, u32[]{:S(2)}, u32[]{:S(2)}) collective-permute-start(f32[512,128]{1,0:T(8,128)S(1)} %collective-permute-done.4.refs_3_), channel_id=1, source_target_pairs={{0,1},{1,0},{2,3},{3,2},{4,5},{5,4},{6,7},{7,6},{8,9},{9,8},{10,11... | collective-permute-start | bytes 786440 | tf_op jit(solution)/shard_map/ppermute | solution.py:324
  46.3 1.4 %collective-permute-done.9.refs_7_ = f32[512,128]{1,0:T(8,128)S(1)} collective-permute-done((f32[512,128]{1,0:T(8,128)S(1)}, f32[512,128]{1,0:T(8,128)S(1)}, u32[]{:S(2)}, u32[]{:S(2)}) %collective-permute-start.9) | collective-permute-done | bytes 262176 | tf_op jit(solution)/shard_map/ppermute | solution.py:324
  47.7 3.9 %square.1 = (f32[512,512]{1,0:T(8,128)S(1)}, f32[512,512]{1,0:T(8,128)S(1)}, bf16[512,512]{1,0:T(8,128)(2,1)S(1)}, bf16[512,512]{1,0:T(8,128)(2,1)S(1)}, f32[512,512]{1,0:T(8,128)S(1)}, /*index=5*/f32[1,128]{1,0:T(1,128)S(1)}) custom-call(s32[76]{0:T(128)S(1)} %concatenate.3.s_ref, f32[512,128]{1,0:T(8,128)S(1)} %get-tuple-element.28.own_ref.refs_0_, ...), custom_call_target="tpu_custom_call" | custom-call | tf_op jit(solution)/shard_map/square/pallas_call | solution.py:360
  51.7 6.6 %second.1 = (f32[2,512,128]{2,1,0:T(8,128)S(1)}, f32[512,128]{1,0:T(8,128)S(1)}, f32[512,128]{1,0:T(8,128)S(1)}, f32[96,128]{1,0:T(8,128)S(1)}) custom-call(s32[76]{0:T(128)S(1)} %concatenate.3.s_ref, f32[512,512]{1,0:T(8,128)S(1)} %get-tuple-element.35.p1_ref, f32[512,512]{1,0:T(8,128)S(1)} %get-tuple-element.36.v_ref, ...), custom_call_target="tpu_custom_call" | custom-call | tf_op jit(solution)/shard_map/second/pallas_call | solution.py:378
  58.3 0.7 collective-permute-start.11
  59.0 7.2 %collective-permute-start.12 = (f32[512,128]{1,0:T(8,128)S(1)}, f32[512,128]{1,0:T(8,128)S(1)}, u32[]{:S(2)}, u32[]{:S(2)}) collective-permute-start(f32[512,128]{1,0:T(8,128)S(1)} %get-tuple-element.44), channel_id=1, source_target_pairs={{0,7},{1,6},{2,5},{3,4},{4,3},{5,2},{6,1},{7,0},{8,15},{9,14},{10,... | collective-permute-start | bytes 786440 | tf_op jit(solution)/shard_map/ppermute | solution.py:394
  66.2 32.9 %all_to_all.11 = f32[96,1,128]{2,1,0:T(1,128)S(1)} all-to-all(f32[96,1,128]{2,1,0:T(1,128)S(1)} %bitcast.13), channel_id=1, replica_groups=mesh['row'=96,'col'=8] {'row'}, dimensions={0} | all-to-all | bytes 98304 | tf_op jit(solution)/shard_map/all_to_all | solution.py:395
  99.1 1.5 %last.1 = (f32[8,2,64,64]{3,2,1,0:T(8,128)}, f32[2]{0:T(128)}) custom-call(s32[76]{0:T(128)S(1)} %concatenate.3.s_ref, f32[2,512,128]{2,1,0:T(8,128)S(1)} %get-tuple-element.42.own_ref, f32[512,128]{1,0:T(8,128)S(1)} %collective-permute-done.11.far_ref, f32[512,128]{1,0:T(8,128)S(1)} %collective-permute-done.12.near_ref, f32[96,128]{1,0:T(8,128)S(1)} %bitcast.12), custom_call_target="tpu_custom_call" | custom-call | tf_op jit(solution)/shard_map/last/pallas_call | solution.py:396
  (18 shorter events, 0.4 us)
Async XLA Ops:
  0.6 1.0 %copy-start = (f32[8,2,64,64]{3,2,1,0:T(8,128)S(1)}, f32[8,2,64,64]{3,2,1,0:T(8,128)}, u32[]{:S(2)}) copy-start(f32[8,2,64,64]{3,2,1,0:T(8,128)} %v_ref.1) | copy-start | bytes 786436
  1.8 6.2 %collective-permute-start.1 = (f32[256,128]{1,0:T(8,128)S(1)}, f32[256,128]{1,0:T(8,128)S(1)}, u32[]{:S(2)}, u32[]{:S(2)}) collective-permute-start(f32[256,128]{1,0:T(8,128)S(1)} %get-tuple-element.25), channel_id=1, source_target_pairs={{4,2},{12,10},{20,18},{28,26},{36,34},{44,42},{52,50},{60,58},{68,... | collective-permute-start | bytes 393224 | tf_op jit(solution)/shard_map/ppermute | solution.py:339
  2.5 10.6 %collective-permute-start.3 = (f32[256,128]{1,0:T(8,128)S(1)}, f32[256,128]{1,0:T(8,128)S(1)}, u32[]{:S(2)}, u32[]{:S(2)}) collective-permute-start(f32[256,128]{1,0:T(8,128)S(1)} %get-tuple-element.25), channel_id=1, source_target_pairs={{4,0},{12,8},{20,16},{28,24},{36,32},{44,40},{52,48},{60,56},{68,6... | collective-permute-start | bytes 393224 | tf_op jit(solution)/shard_map/ppermute | solution.py:340
  3.2 9.9 %collective-permute-start = (f32[512,128]{1,0:T(8,128)S(1)}, f32[512,128]{1,0:T(8,128)S(1)}, u32[]{:S(2)}, u32[]{:S(2)}) collective-permute-start(f32[512,128]{1,0:T(8,128)S(1)} %get-tuple-element.28.own_ref.refs_0_), channel_id=1, source_target_pairs={{0,2},{1,3},{2,0},{3,1},{4,6},{5,7},{6,4},{7,5},{8,10},{9,11},{10,... | collective-permute-start | bytes 786440 | tf_op jit(solution)/shard_map/ppermute | solution.py:338
  7.2 0.7 copy-start.1
  8.0 11.1 %collective-permute-start.2 = (f32[512,128]{1,0:T(8,128)S(1)}, f32[512,128]{1,0:T(8,128)S(1)}, u32[]{:S(2)}, u32[]{:S(2)}) collective-permute-start(f32[512,128]{1,0:T(8,128)S(1)} %get-tuple-element.28.own_ref.refs_0_), channel_id=1, source_target_pairs={{0,4},{1,5},{2,6},{3,7},{4,0},{5,1},{6,2},{7,3},{8,12},{9,13},{10,... | collective-permute-start | bytes 786440 | tf_op jit(solution)/shard_map/ppermute | solution.py:342
  12.3 0.7 copy-start.2
  13.7 27.1 %collective-permute-start.5 = (f32[576,128]{1,0:T(8,128)S(1)}, f32[576,128]{1,0:T(8,128)S(1)}, u32[]{:S(2)}, u32[]{:S(2)}) collective-permute-start(f32[576,128]{1,0:T(8,128)S(1)} %triangle.1), channel_id=1, source_target_pairs={{4,8},{5,9},{6,10},{7,11},{12,16},{13,17},{14,18},{15,19},{20,24},... | collective-permute-start | bytes 884744 | tf_op jit(solution)/shard_map/ppermute | solution.py:352
  19.1 21.8 %collective-permute-start.4 = (f32[512,128]{1,0:T(8,128)S(1)}, f32[512,128]{1,0:T(8,128)S(1)}, u32[]{:S(2)}, u32[]{:S(2)}) collective-permute-start(f32[512,128]{1,0:T(8,128)S(1)} %collective-permute-done.2.refs_2_), channel_id=1, source_target_pairs={{0,2},{1,3},{2,0},{3,1},{4,6},{5,7},{6,4},{7,5},{8,10},{9,11},{10,... | collective-permute-start | bytes 786440 | tf_op jit(solution)/shard_map/ppermute | solution.py:354
  21.0 19.9 %collective-permute-start.6 = (f32[512,128]{1,0:T(8,128)S(1)}, f32[512,128]{1,0:T(8,128)S(1)}, u32[]{:S(2)}, u32[]{:S(2)}) collective-permute-start(f32[512,128]{1,0:T(8,128)S(1)} %get-tuple-element.28.own_ref.refs_0_), channel_id=1, source_target_pairs={{0,1},{1,0},{2,3},{3,2},{4,5},{5,4},{6,7},{7,6},{8,9},{9,8},{10,11... | collective-permute-start | bytes 786440 | tf_op jit(solution)/shard_map/ppermute | solution.py:324
  36.5 4.4 %collective-permute-start.7 = (f32[512,128]{1,0:T(8,128)S(1)}, f32[512,128]{1,0:T(8,128)S(1)}, u32[]{:S(2)}, u32[]{:S(2)}) collective-permute-start(f32[512,128]{1,0:T(8,128)S(1)} %collective-permute-done.near_ref.refs_1_), channel_id=1, source_target_pairs={{0,1},{1,0},{2,3},{3,2},{4,5},{5,4},{6,7},{7,6},{8,9},{9,8},{10,11... | collective-permute-start | bytes 786440 | tf_op jit(solution)/shard_map/ppermute | solution.py:324
  38.4 3.6 %collective-permute-start.8 = (f32[512,128]{1,0:T(8,128)S(1)}, f32[512,128]{1,0:T(8,128)S(1)}, u32[]{:S(2)}, u32[]{:S(2)}) collective-permute-start(f32[512,128]{1,0:T(8,128)S(1)} %collective-permute-done.2.refs_2_), channel_id=1, source_target_pairs={{0,1},{1,0},{2,3},{3,2},{4,5},{5,4},{6,7},{7,6},{8,9},{9,8},{10,11... | collective-permute-start | bytes 786440 | tf_op jit(solution)/shard_map/ppermute | solution.py:324
  42.0 9.7 %collective-permute-start.10 = (f32[576,128]{1,0:T(8,128)S(1)}, f32[576,128]{1,0:T(8,128)S(1)}, u32[]{:S(2)}, u32[]{:S(2)}) collective-permute-start(f32[576,128]{1,0:T(8,128)S(1)} %collective-permute-done.5.ta), channel_id=1, source_target_pairs={{0,1},{1,0},{2,3},{3,2},{4,5},{5,4},{6,7},{7,6},{8,9},{9,8},{10,11... | collective-permute-start | bytes 884744 | tf_op jit(solution)/shard_map/ppermute | solution.py:324
  44.3 3.4 %collective-permute-start.9 = (f32[512,128]{1,0:T(8,128)S(1)}, f32[512,128]{1,0:T(8,128)S(1)}, u32[]{:S(2)}, u32[]{:S(2)}) collective-permute-start(f32[512,128]{1,0:T(8,128)S(1)} %collective-permute-done.4.refs_3_), channel_id=1, source_target_pairs={{0,1},{1,0},{2,3},{3,2},{4,5},{5,4},{6,7},{7,6},{8,9},{9,8},{10,11... | collective-permute-start | bytes 786440 | tf_op jit(solution)/shard_map/ppermute | solution.py:324
  58.3 40.8 %collective-permute-start.11 = (f32[512,128]{1,0:T(8,128)S(1)}, f32[512,128]{1,0:T(8,128)S(1)}, u32[]{:S(2)}, u32[]{:S(2)}) collective-permute-start(f32[512,128]{1,0:T(8,128)S(1)} %get-tuple-element.43), channel_id=1, source_target_pairs={{7,8},{6,9},{5,10},{4,11},{15,16},{14,17},{13,18},{12,19},{23,24},... | collective-permute-start | bytes 786440 | tf_op jit(solution)/shard_map/ppermute | solution.py:393
  59.0 40.1 %collective-permute-start.12 = (f32[512,128]{1,0:T(8,128)S(1)}, f32[512,128]{1,0:T(8,128)S(1)}, u32[]{:S(2)}, u32[]{:S(2)}) collective-permute-start(f32[512,128]{1,0:T(8,128)S(1)} %get-tuple-element.44), channel_id=1, source_target_pairs={{0,7},{1,6},{2,5},{3,4},{4,3},{5,2},{6,1},{7,0},{8,15},{9,14},{10,... | collective-permute-start | bytes 786440 | tf_op jit(solution)/shard_map/ppermute | solution.py:394

commit v7 on v6

--- a/solution.py
+++ b/solution.py
@@ -70,8 +70,10 @@
         diag_ref[strip(i), :] = jnp.concatenate([v_ref[i, 0], v_ref[i + 4, 0]], axis=1)
 
 
-def triangle_kernel(s_ref, own_ref, near_ref, d1_ref, d2_ref, out_ref, low, high):
+def triangle_kernel(s_ref, own_ref, near_ref, d1_ref, d2_ref, out_ref, both_ref, low, high):
     odd, core, upper = (s_ref[0] & 1) == 1, s_ref[1], s_ref[3]
+    both_ref[0:N, :] = own_ref[...]
+    both_ref[N : 2 * N, :] = near_ref[...]
     low[...] = jnp.where(odd, near_ref[...], own_ref[...])
     high[...] = jnp.where(odd, own_ref[...], near_ref[...])
 
@@ -105,13 +107,14 @@
 
 
 def square_kernel(s_ref, *refs):
-    packs, (p1_ref, v_ref, vh_ref, vl_ref, pv_ref, tr_ref) = refs[:8], refs[8:14]
-    q_ref, r_ref, rh, rl = refs[14:]
+    packs, (p1_ref, v_ref, vh_ref, vl_ref, pv_ref, tr_ref) = refs[:6], refs[6:12]
+    q_ref, r_ref, rh, rl = refs[12:]
     yl, core, upper = s_ref[0], s_ref[1], s_ref[3]
     for k in range(4):
         for other in range(2):
             place = 2 * (yl ^ k) + (core ^ other)
-            q_ref[:, pl.ds(pl.multiple_of(place * 128, 128), 128)] = packs[4 * other + k][...]
+            part = packs[2 * k - 2 + other][...] if k > 1 else packs[other][k * N : (k + 1) * N, :]
+            q_ref[:, pl.ds(pl.multiple_of(place * 128, 128), 128)] = part
     total = jnp.zeros((1, 2 * N), F32)
     for i in range(H):
         own = q_ref[strip(i), :]
@@ -340,22 +343,23 @@
     d2 = lax.ppermute(diag, "col", [(4, 0)])
     later, d1 = lax.optimization_barrier((packed, d1))
     cross = lax.ppermute(later, "col", [(c, c ^ 4) for c in range(8)])
-    triangle = call(
+    triangle, joined = call(
         triangle_kernel,
-        out_shape=shape(576, 128),
+        out_shape=[shape(576, 128), shape(2 * N, 128)],
         in_specs=[SMEM] + [VMEM] * 4,
-        out_specs=VMEM,
+        out_specs=[VMEM] * 2,
         scratch_shapes=[pltpu.VMEM((N, 128), F32)] * 2,
         mib=8, name="triangle",
     )(scalars, packed, near, d1, d2)
     pairs = [(index(r, c + 4), index(r + 1, c)) for r, c in ends]
     ta = lax.ppermute(triangle, both, pairs + [(b, a) for a, b in pairs])
-    packed, near, cross, triangle = lax.optimization_barrier((packed, near, cross, triangle))
+    cross, joined, triangle = lax.optimization_barrier((cross, joined, triangle))
     forward = lax.ppermute(cross, "col", [(c, c ^ 2) for c in range(8)])
-    swapped = [swap(packed), swap(near), swap(cross)]
-    forward, ta, *swapped = lax.optimization_barrier((forward, ta, *swapped))
-    mine = [packed, near, cross, forward]
-    others = swapped + [swap(forward)]
+    joined2, cross2 = swap(joined), swap(cross)
+    forward, cross2 = lax.optimization_barrier((forward, cross2))
+    forward2 = swap(forward)
+    ta, forward = lax.optimization_barrier((ta, forward))
+    tb = swap(ta)
 
     *old, trace = call(
         square_kernel,
@@ -363,7 +367,7 @@
             shape(N, N), shape(N, N), jax.ShapeDtypeStruct((N, N), BF16),
             jax.ShapeDtypeStruct((N, N), BF16), shape(N, N), shape(1, 128),
         ],
-        in_specs=[SMEM] + [VMEM] * 8,
+        in_specs=[SMEM] + [VMEM] * 6,
         out_specs=[VMEM] * 6,
         scratch_shapes=[
             pltpu.VMEM((N, 2 * N), F32),
@@ -372,9 +376,8 @@
             pltpu.VMEM((N, W), BF16),
         ],
         mib=24, name="square",
-    )(scalars, *mine, *others)
-
-    tb = swap(ta)
+    )(scalars, joined, joined2, cross, cross2, forward, forward2)
+
     own, far, near, sums = call(
         second_kernel,
         out_shape=[shape(2, N, 128), shape(N, 128), shape(N, 128), shape(rows, 128)],

time: 102 us -> 101 us (level)
  blocking collectives: 32.9 us -> 35.9 us
  starting transfers between devices: 44.2 us -> 41.8 us
    all_to_all x1, blocking collectives: 32.9 us -> 35.9 us  [per_device(): sums = lax.all_to_all(sums, 'row', 0, 0, tiled=True)]
    ppermute x1, starting transfers between devices: 7.23 us -> 5.97 us  [per_device(): near = lax.ppermute(near, 'col', [(c, 7 - c) for c in range(8)])]
    ppermute x5 -> x4, starting transfers between devices: 24.1 us -> 23 us  [swap(): return lax.ppermute(x, 'col', [(c, c ^ 1) for c in range(8)])]
    ppermute x5 -> x4, waiting for transfers between devices: 2.48 us -> 1.51 us  [swap(): return lax.ppermute(x, 'col', [(c, c ^ 1) for c in range(8)])]
  transfers between devices with their start and end apart: 13 -> 12, of which waited for: 3 -> 2; matrix products, arithmetic and copies ran while one was open for 0% -> 0% of each run, Pallas kernels for 5% -> 5%
where the time goes in v7:
time: 101 us; the launch traced here: 100 us
  starting transfers between devices  41.8 us (41%)
  blocking collectives  35.9 us (36%)
  Pallas kernels  12.9 us (13%)
  waiting for transfers between devices  6.16 us (6%)
  local copies, waits for them, and re-layouts  2.62 us (3%)
    all_to_all x1, blocking collectives, per_device(): sums = lax.all_to_all(sums, 'row', 0, 0, tiled=True)  35.9 us
    ppermute x4, starting transfers between devices, swap(): return lax.ppermute(x, 'col', [(c, c ^ 1) for c in range(8)])  23 us
    pallas_call x1, Pallas kernels, per_device(): call(second_kernel, out_shape=[shape(2, N, 128), shape(N, 128), shape(N,...  6.64 us
    ppermute x1, starting transfers between devices, per_device(): near = lax.ppermute(near, 'col', [(c, 7 - c) for c in range(8)])  5.97 us
    ppermute x1, waiting for transfers between devices, per_device(): cross = lax.ppermute(later, 'col', [(c, c ^ 4) for c in range(8)])  4.64 us
    ppermute x1, starting transfers between devices, per_device(): cross = lax.ppermute(later, 'col', [(c, c ^ 4) for c in range(8)])  4.21 us
    ppermute x1, starting transfers between devices, per_device(): near = lax.ppermute(packed, 'col', [(c, c ^ 2) for c in range(8)])  4.03 us
    pallas_call x1, Pallas kernels, per_device(): call(square_kernel, out_shape=[shape(N, N), shape(N, N), jax.ShapeDtypeSt...  3.94 us
  transfers between devices with their start and end apart: 12, of which 2 were waited for; matrix products, arithmetic and copies ran while one was open for 0% of the time, Pallas kernels for 5%

profile of v7, /device:TPU:1, one launch (start us, length us, event | category | flops | bytes accessed | tf_op | source)
XLA Modules:
  0.0 100.2 jit_solution(9916871897304631395)
XLA Ops:
  0.6 1.0 %copy-done = f32[8,2,64,64]{3,2,1,0:T(8,128)S(1)} copy-done((f32[8,2,64,64]{3,2,1,0:T(8,128)S(1)}, f32[8,2,64,64]{3,2,1,0:T(8,128)}, u32[]{:S(2)}) %copy-start) | copy-done | bytes 262168
  1.7 0.2 pack.1
  1.8 0.7 collective-permute-start
  2.5 0.7 collective-permute-start.3
  3.2 4.0 %collective-permute-start.2 = (f32[512,128]{1,0:T(8,128)S(1)}, f32[512,128]{1,0:T(8,128)S(1)}, u32[]{:S(2)}, u32[]{:S(2)}) collective-permute-start(f32[512,128]{1,0:T(8,128)S(1)} %get-tuple-element.26.own_ref), channel_id=1, source_target_pairs={{0,2},{1,3},{2,0},{3,1},{4,6},{5,7},{6,4},{7,5},{8,10},{9,11},{10,... | collective-permute-start | bytes 786440 | tf_op jit(solution)/shard_map/ppermute | solution.py:341
  7.3 0.7 copy-done.1
  8.0 4.2 %collective-permute-start.1 = (f32[512,128]{1,0:T(8,128)S(1)}, f32[512,128]{1,0:T(8,128)S(1)}, u32[]{:S(2)}, u32[]{:S(2)}) collective-permute-start(f32[512,128]{1,0:T(8,128)S(1)} %get-tuple-element.26.own_ref), channel_id=1, source_target_pairs={{0,4},{1,5},{2,6},{3,7},{4,0},{5,1},{6,2},{7,3},{8,12},{9,13},{10,... | collective-permute-start | bytes 786440 | tf_op jit(solution)/shard_map/ppermute | solution.py:345
  12.3 0.7 copy-done.2
  13.0 0.1 pad_dynamic-slice_fusion.1
  13.1 0.6 triangle.1
  13.8 0.7 collective-permute-start.7
  14.5 4.6 %collective-permute-done.1.refs_2_ = f32[512,128]{1,0:T(8,128)S(1)} collective-permute-done((f32[512,128]{1,0:T(8,128)S(1)}, f32[512,128]{1,0:T(8,128)S(1)}, u32[]{:S(2)}, u32[]{:S(2)}) %collective-permute-start.1) | collective-permute-done | bytes 262176 | tf_op jit(solution)/shard_map/ppermute | solution.py:345
  19.1 1.9 %collective-permute-start.5 = (f32[512,128]{1,0:T(8,128)S(1)}, f32[512,128]{1,0:T(8,128)S(1)}, u32[]{:S(2)}, u32[]{:S(2)}) collective-permute-start(f32[512,128]{1,0:T(8,128)S(1)} %collective-permute-done.1.refs_2_), channel_id=1, source_target_pairs={{0,2},{1,3},{2,0},{3,1},{4,6},{5,7},{6,4},{7,5},{8,10},{9,11},{10,... | collective-permute-start | bytes 786440 | tf_op jit(solution)/shard_map/ppermute | solution.py:357
  21.0 15.5 %collective-permute-start.6 = (f32[512,128]{1,0:T(8,128)S(1)}, f32[512,128]{1,0:T(8,128)S(1)}, u32[]{:S(2)}, u32[]{:S(2)}) collective-permute-start(f32[512,128]{1,0:T(8,128)S(1)} %collective-permute-done.1.refs_2_), channel_id=1, source_target_pairs={{0,1},{1,0},{2,3},{3,2},{4,5},{5,4},{6,7},{7,6},{8,9},{9,8},{10,11... | collective-permute-start | bytes 786440 | tf_op jit(solution)/shard_map/ppermute | solution.py:327
  36.5 1.9 %collective-permute-start.4 = (f32[1024,128]{1,0:T(8,128)S(1)}, f32[1024,128]{1,0:T(8,128)S(1)}, u32[]{:S(2)}, u32[]{:S(2)}) collective-permute-start(f32[1024,128]{1,0:T(8,128)S(1)} %get-tuple-element.30.refs_0_), channel_id=1, source_target_pairs={{0,1},{1,0},{2,3},{3,2},{4,5},{5,4},{6,7},{7,6},{8,9},{9,8},{10,11... | collective-permute-start | bytes 1572872 | tf_op jit(solution)/shard_map/ppermute | solution.py:327
  38.5 3.7 %collective-permute-start.9 = (f32[576,128]{1,0:T(8,128)S(1)}, f32[576,128]{1,0:T(8,128)S(1)}, u32[]{:S(2)}, u32[]{:S(2)}) collective-permute-start(f32[576,128]{1,0:T(8,128)S(1)} %collective-permute-done.7.ta), channel_id=1, source_target_pairs={{0,1},{1,0},{2,3},{3,2},{4,5},{5,4},{6,7},{7,6},{8,9},{9,8},{10,11... | collective-permute-start | bytes 884744 | tf_op jit(solution)/shard_map/ppermute | solution.py:327
  42.1 1.9 %collective-permute-start.8 = (f32[512,128]{1,0:T(8,128)S(1)}, f32[512,128]{1,0:T(8,128)S(1)}, u32[]{:S(2)}, u32[]{:S(2)}) collective-permute-start(f32[512,128]{1,0:T(8,128)S(1)} %collective-permute-done.5.refs_4_), channel_id=1, source_target_pairs={{0,1},{1,0},{2,3},{3,2},{4,5},{5,4},{6,7},{7,6},{8,9},{9,8},{10,11... | collective-permute-start | bytes 786440 | tf_op jit(solution)/shard_map/ppermute | solution.py:327
  44.1 1.5 %collective-permute-done.8.refs_5_ = f32[512,128]{1,0:T(8,128)S(1)} collective-permute-done((f32[512,128]{1,0:T(8,128)S(1)}, f32[512,128]{1,0:T(8,128)S(1)}, u32[]{:S(2)}, u32[]{:S(2)}) %collective-permute-start.8) | collective-permute-done | bytes 262176 | tf_op jit(solution)/shard_map/ppermute | solution.py:327
  45.6 3.9 %square.1 = (f32[512,512]{1,0:T(8,128)S(1)}, f32[512,512]{1,0:T(8,128)S(1)}, bf16[512,512]{1,0:T(8,128)(2,1)S(1)}, bf16[512,512]{1,0:T(8,128)(2,1)S(1)}, f32[512,512]{1,0:T(8,128)S(1)}, /*index=5*/f32[1,128]{1,0:T(1,128)S(1)}) custom-call(s32[76]{0:T(128)S(1)} %concatenate.3.s_ref, f32[1024,128]{1,0:T(8,128)S(1)} %get-tuple-element.30.refs_0_, ...), custom_call_target="tpu_custom_call" | custom-call | tf_op jit(solution)/shard_map/square/pallas_call | solution.py:364
  49.5 6.6 %second.1 = (f32[2,512,128]{2,1,0:T(8,128)S(1)}, f32[512,128]{1,0:T(8,128)S(1)}, f32[512,128]{1,0:T(8,128)S(1)}, f32[96,128]{1,0:T(8,128)S(1)}) custom-call(s32[76]{0:T(128)S(1)} %concatenate.3.s_ref, f32[512,512]{1,0:T(8,128)S(1)} %get-tuple-element.35.p1_ref, f32[512,512]{1,0:T(8,128)S(1)} %get-tuple-element.36.v_ref, ...), custom_call_target="tpu_custom_call" | custom-call | tf_op jit(solution)/shard_map/second/pallas_call | solution.py:381
  56.2 0.7 collective-permute-start.10
  56.8 6.0 %collective-permute-start.11 = (f32[512,128]{1,0:T(8,128)S(1)}, f32[512,128]{1,0:T(8,128)S(1)}, u32[]{:S(2)}, u32[]{:S(2)}) collective-permute-start(f32[512,128]{1,0:T(8,128)S(1)} %get-tuple-element.44), channel_id=1, source_target_pairs={{0,7},{1,6},{2,5},{3,4},{4,3},{5,2},{6,1},{7,0},{8,15},{9,14},{10,... | collective-permute-start | bytes 786440 | tf_op jit(solution)/shard_map/ppermute | solution.py:397
  62.8 35.9 %all_to_all.11 = f32[96,1,128]{2,1,0:T(1,128)S(1)} all-to-all(f32[96,1,128]{2,1,0:T(1,128)S(1)} %bitcast.13), channel_id=1, replica_groups=mesh['row'=96,'col'=8] {'row'}, dimensions={0} | all-to-all | bytes 98304 | tf_op jit(solution)/shard_map/all_to_all | solution.py:398
  98.7 1.5 %last.1 = (f32[8,2,64,64]{3,2,1,0:T(8,128)}, f32[2]{0:T(128)}) custom-call(s32[76]{0:T(128)S(1)} %concatenate.3.s_ref, f32[2,512,128]{2,1,0:T(8,128)S(1)} %get-tuple-element.42.own_ref, f32[512,128]{1,0:T(8,128)S(1)} %collective-permute-done.10.far_ref, f32[512,128]{1,0:T(8,128)S(1)} %collective-permute-done.11.near_ref, f32[96,128]{1,0:T(8,128)S(1)} %bitcast.12), custom_call_target="tpu_custom_call" | custom-call | tf_op jit(solution)/shard_map/last/pallas_call | solution.py:399
  (16 shorter events, 0.2 us)
Async XLA Ops:
  0.6 1.0 %copy-start = (f32[8,2,64,64]{3,2,1,0:T(8,128)S(1)}, f32[8,2,64,64]{3,2,1,0:T(8,128)}, u32[]{:S(2)}) copy-start(f32[8,2,64,64]{3,2,1,0:T(8,128)} %v_ref.1) | copy-start | bytes 786436
  1.8 6.2 %collective-permute-start = (f32[256,128]{1,0:T(8,128)S(1)}, f32[256,128]{1,0:T(8,128)S(1)}, u32[]{:S(2)}, u32[]{:S(2)}) collective-permute-start(f32[256,128]{1,0:T(8,128)S(1)} %get-tuple-element.25), channel_id=1, source_target_pairs={{4,2},{12,10},{20,18},{28,26},{36,34},{44,42},{52,50},{60,58},{68,... | collective-permute-start | bytes 393224 | tf_op jit(solution)/shard_map/ppermute | solution.py:342
  2.5 10.6 %collective-permute-start.3 = (f32[256,128]{1,0:T(8,128)S(1)}, f32[256,128]{1,0:T(8,128)S(1)}, u32[]{:S(2)}, u32[]{:S(2)}) collective-permute-start(f32[256,128]{1,0:T(8,128)S(1)} %get-tuple-element.25), channel_id=1, source_target_pairs={{4,0},{12,8},{20,16},{28,24},{36,32},{44,40},{52,48},{60,56},{68,6... | collective-permute-start | bytes 393224 | tf_op jit(solution)/shard_map/ppermute | solution.py:343
  3.2 9.9 %collective-permute-start.2 = (f32[512,128]{1,0:T(8,128)S(1)}, f32[512,128]{1,0:T(8,128)S(1)}, u32[]{:S(2)}, u32[]{:S(2)}) collective-permute-start(f32[512,128]{1,0:T(8,128)S(1)} %get-tuple-element.26.own_ref), channel_id=1, source_target_pairs={{0,2},{1,3},{2,0},{3,1},{4,6},{5,7},{6,4},{7,5},{8,10},{9,11},{10,... | collective-permute-start | bytes 786440 | tf_op jit(solution)/shard_map/ppermute | solution.py:341
  7.2 0.7 copy-start.1
  8.0 11.1 %collective-permute-start.1 = (f32[512,128]{1,0:T(8,128)S(1)}, f32[512,128]{1,0:T(8,128)S(1)}, u32[]{:S(2)}, u32[]{:S(2)}) collective-permute-start(f32[512,128]{1,0:T(8,128)S(1)} %get-tuple-element.26.own_ref), channel_id=1, source_target_pairs={{0,4},{1,5},{2,6},{3,7},{4,0},{5,1},{6,2},{7,3},{8,12},{9,13},{10,... | collective-permute-start | bytes 786440 | tf_op jit(solution)/shard_map/ppermute | solution.py:345
  12.3 0.7 copy-start.2
  13.8 24.7 %collective-permute-start.7 = (f32[576,128]{1,0:T(8,128)S(1)}, f32[576,128]{1,0:T(8,128)S(1)}, u32[]{:S(2)}, u32[]{:S(2)}) collective-permute-start(f32[576,128]{1,0:T(8,128)S(1)} %get-tuple-element.29), channel_id=1, source_target_pairs={{4,8},{5,9},{6,10},{7,11},{12,16},{13,17},{14,18},{15,19},{20,24},... | collective-permute-start | bytes 884744 | tf_op jit(solution)/shard_map/ppermute | solution.py:355
  19.1 19.3 %collective-permute-start.5 = (f32[512,128]{1,0:T(8,128)S(1)}, f32[512,128]{1,0:T(8,128)S(1)}, u32[]{:S(2)}, u32[]{:S(2)}) collective-permute-start(f32[512,128]{1,0:T(8,128)S(1)} %collective-permute-done.1.refs_2_), channel_id=1, source_target_pairs={{0,2},{1,3},{2,0},{3,1},{4,6},{5,7},{6,4},{7,5},{8,10},{9,11},{10,... | collective-permute-start | bytes 786440 | tf_op jit(solution)/shard_map/ppermute | solution.py:357
  21.0 17.4 %collective-permute-start.6 = (f32[512,128]{1,0:T(8,128)S(1)}, f32[512,128]{1,0:T(8,128)S(1)}, u32[]{:S(2)}, u32[]{:S(2)}) collective-permute-start(f32[512,128]{1,0:T(8,128)S(1)} %collective-permute-done.1.refs_2_), channel_id=1, source_target_pairs={{0,1},{1,0},{2,3},{3,2},{4,5},{5,4},{6,7},{7,6},{8,9},{9,8},{10,11... | collective-permute-start | bytes 786440 | tf_op jit(solution)/shard_map/ppermute | solution.py:327
  36.5 9.1 %collective-permute-start.4 = (f32[1024,128]{1,0:T(8,128)S(1)}, f32[1024,128]{1,0:T(8,128)S(1)}, u32[]{:S(2)}, u32[]{:S(2)}) collective-permute-start(f32[1024,128]{1,0:T(8,128)S(1)} %get-tuple-element.30.refs_0_), channel_id=1, source_target_pairs={{0,1},{1,0},{2,3},{3,2},{4,5},{5,4},{6,7},{7,6},{8,9},{9,8},{10,11... | collective-permute-start | bytes 1572872 | tf_op jit(solution)/shard_map/ppermute | solution.py:327
  38.5 11.0 %collective-permute-start.9 = (f32[576,128]{1,0:T(8,128)S(1)}, f32[576,128]{1,0:T(8,128)S(1)}, u32[]{:S(2)}, u32[]{:S(2)}) collective-permute-start(f32[576,128]{1,0:T(8,128)S(1)} %collective-permute-done.7.ta), channel_id=1, source_target_pairs={{0,1},{1,0},{2,3},{3,2},{4,5},{5,4},{6,7},{7,6},{8,9},{9,8},{10,11... | collective-permute-start | bytes 884744 | tf_op jit(solution)/shard_map/ppermute | solution.py:327
  42.1 3.4 %collective-permute-start.8 = (f32[512,128]{1,0:T(8,128)S(1)}, f32[512,128]{1,0:T(8,128)S(1)}, u32[]{:S(2)}, u32[]{:S(2)}) collective-permute-start(f32[512,128]{1,0:T(8,128)S(1)} %collective-permute-done.5.refs_4_), channel_id=1, source_target_pairs={{0,1},{1,0},{2,3},{3,2},{4,5},{5,4},{6,7},{7,6},{8,9},{9,8},{10,11... | collective-permute-start | bytes 786440 | tf_op jit(solution)/shard_map/ppermute | solution.py:327
  56.2 42.5 %collective-permute-start.10 = (f32[512,128]{1,0:T(8,128)S(1)}, f32[512,128]{1,0:T(8,128)S(1)}, u32[]{:S(2)}, u32[]{:S(2)}) collective-permute-start(f32[512,128]{1,0:T(8,128)S(1)} %get-tuple-element.43), channel_id=1, source_target_pairs={{7,8},{6,9},{5,10},{4,11},{15,16},{14,17},{13,18},{12,19},{23,24},... | collective-permute-start | bytes 786440 | tf_op jit(solution)/shard_map/ppermute | solution.py:396
  56.8 41.8 %collective-permute-start.11 = (f32[512,128]{1,0:T(8,128)S(1)}, f32[512,128]{1,0:T(8,128)S(1)}, u32[]{:S(2)}, u32[]{:S(2)}) collective-permute-start(f32[512,128]{1,0:T(8,128)S(1)} %get-tuple-element.44), channel_id=1, source_target_pairs={{0,7},{1,6},{2,5},{3,4},{4,3},{5,2},{6,1},{7,0},{8,15},{9,14},{10,... | collective-permute-start | bytes 786440 | tf_op jit(solution)/shard_map/ppermute | solution.py:397

commit v8 on v7

--- a/solution.py
+++ b/solution.py
@@ -70,6 +70,11 @@
         diag_ref[strip(i), :] = jnp.concatenate([v_ref[i, 0], v_ref[i + 4, 0]], axis=1)
 
 
+def join_kernel(first_ref, second_ref, out_ref):
+    out_ref[0:N, :] = first_ref[...]
+    out_ref[N : 2 * N, :] = second_ref[...]
+
+
 def triangle_kernel(s_ref, own_ref, near_ref, d1_ref, d2_ref, out_ref, both_ref, low, high):
     odd, core, upper = (s_ref[0] & 1) == 1, s_ref[1], s_ref[3]
     both_ref[0:N, :] = own_ref[...]
@@ -107,13 +112,13 @@
 
 
 def square_kernel(s_ref, *refs):
-    packs, (p1_ref, v_ref, vh_ref, vl_ref, pv_ref, tr_ref) = refs[:6], refs[6:12]
-    q_ref, r_ref, rh, rl = refs[12:]
+    packs, (p1_ref, v_ref, vh_ref, vl_ref, pv_ref, tr_ref) = refs[:4], refs[4:10]
+    q_ref, r_ref, rh, rl = refs[10:]
     yl, core, upper = s_ref[0], s_ref[1], s_ref[3]
     for k in range(4):
         for other in range(2):
             place = 2 * (yl ^ k) + (core ^ other)
-            part = packs[2 * k - 2 + other][...] if k > 1 else packs[other][k * N : (k + 1) * N, :]
+            part = packs[k // 2 * 2 + other][k % 2 * N : (k % 2 + 1) * N, :]
             q_ref[:, pl.ds(pl.multiple_of(place * 128, 128), 128)] = part
     total = jnp.zeros((1, 2 * N), F32)
     for i in range(H):
@@ -343,6 +348,7 @@
     d2 = lax.ppermute(diag, "col", [(4, 0)])
     later, d1 = lax.optimization_barrier((packed, d1))
     cross = lax.ppermute(later, "col", [(c, c ^ 4) for c in range(8)])
+    far = lax.ppermute(later, "col", [(c, c ^ 6) for c in range(8)])
     triangle, joined = call(
         triangle_kernel,
         out_shape=[shape(576, 128), shape(2 * N, 128)],
@@ -353,12 +359,12 @@
     )(scalars, packed, near, d1, d2)
     pairs = [(index(r, c + 4), index(r + 1, c)) for r, c in ends]
     ta = lax.ppermute(triangle, both, pairs + [(b, a) for a, b in pairs])
-    cross, joined, triangle = lax.optimization_barrier((cross, joined, triangle))
-    forward = lax.ppermute(cross, "col", [(c, c ^ 2) for c in range(8)])
-    joined2, cross2 = swap(joined), swap(cross)
-    forward, cross2 = lax.optimization_barrier((forward, cross2))
-    forward2 = swap(forward)
-    ta, forward = lax.optimization_barrier((ta, forward))
+    joined2 = swap(joined)
+    distant = call(
+        join_kernel, out_shape=shape(2 * N, 128), in_specs=[VMEM] * 2, out_specs=VMEM,
+        mib=8, name="join",
+    )(cross, far)
+    distant2 = swap(distant)
     tb = swap(ta)
 
     *old, trace = call(
@@ -367,7 +373,7 @@
             shape(N, N), shape(N, N), jax.ShapeDtypeStruct((N, N), BF16),
             jax.ShapeDtypeStruct((N, N), BF16), shape(N, N), shape(1, 128),
         ],
-        in_specs=[SMEM] + [VMEM] * 6,
+        in_specs=[SMEM] + [VMEM] * 4,
         out_specs=[VMEM] * 6,
         scratch_shapes=[
             pltpu.VMEM((N, 2 * N), F32),
@@ -376,7 +382,7 @@
             pltpu.VMEM((N, W), BF16),
         ],
         mib=24, name="square",
-    )(scalars, joined, joined2, cross, cross2, forward, forward2)
+    )(scalars, joined, joined2, distant, distant2)
 
     own, far, near, sums = call(
         second_kernel,

time: 101 us -> 97.8 us (0.968)
  waiting for transfers between devices: 6.16 us -> 0.03 us
  blocking collectives: 35.9 us -> 38.8 us
    ppermute x1, waiting for transfers between devices: 4.64 us -> 0.01 us  [per_device(): cross = lax.ppermute(later, 'col', [(c, c ^ 4) for c in range(8)])]
    ppermute x1, starting transfers between devices: 5.97 us -> 2.23 us  [per_device(): near = lax.ppermute(near, 'col', [(c, 7 - c) for c in range(8)])]
    all_to_all x1, blocking collectives: 35.9 us -> 38.8 us  [per_device(): sums = lax.all_to_all(sums, 'row', 0, 0, tiled=True)]
    ppermute x4 -> x3, starting transfers between devices: 23 us -> 25.9 us  [swap(): return lax.ppermute(x, 'col', [(c, c ^ 1) for c in range(8)])]
    ppermute x4 -> x3, waiting for transfers between devices: 1.51 us -> 0.01 us  [swap(): return lax.ppermute(x, 'col', [(c, c ^ 1) for c in range(8)])]
  transfers between devices with their start and end apart: 12 -> 11, of which waited for: 2 -> 0; matrix products, arithmetic and copies ran while one was open for 0% -> 0% of each run, Pallas kernels for 5% -> 5%
where the time goes in v8:
time: 97.8 us; the launch traced here: 96.3 us
  starting transfers between devices  41 us (42%)
  blocking collectives  38.8 us (40%)
  Pallas kernels  12.9 us (13%)
  local copies, waits for them, and re-layouts  2.62 us (3%)
    all_to_all x1, blocking collectives, per_device(): sums = lax.all_to_all(sums, 'row', 0, 0, tiled=True)  38.8 us
    ppermute x3, starting transfers between devices, swap(): return lax.ppermute(x, 'col', [(c, c ^ 1) for c in range(8)])  25.9 us
    pallas_call x1, Pallas kernels, per_device(): call(second_kernel, out_shape=[shape(2, N, 128), shape(N, 128), shape(N,...  6.63 us
    ppermute x1, starting transfers between devices, per_device(): cross = lax.ppermute(later, 'col', [(c, c ^ 4) for c in range(8)])  4.21 us
    ppermute x1, starting transfers between devices, per_device(): near = lax.ppermute(packed, 'col', [(c, c ^ 2) for c in range(8)])  4.03 us
    pallas_call x1, Pallas kernels, per_device(): call(square_kernel, out_shape=[shape(N, N), shape(N, N), jax.ShapeDtypeSt...  3.94 us
    unnamed x6, local copies, waits for them, and re-layouts  2.38 us
    ppermute x1, starting transfers between devices, per_device(): near = lax.ppermute(near, 'col', [(c, 7 - c) for c in range(8)])  2.23 us
  transfers between devices with their start and end apart: 11, of which 0 were waited for; matrix products, arithmetic and copies ran while one was open for 0% of the time, Pallas kernels for 5%

profile of v8, /device:TPU:1, one launch (start us, length us, event | category | flops | bytes accessed | tf_op | source)
XLA Modules:
  0.0 96.3 jit_solution(18395034660635695018)
XLA Ops:
  0.6 1.0 %copy-done = f32[8,2,64,64]{3,2,1,0:T(8,128)S(1)} copy-done((f32[8,2,64,64]{3,2,1,0:T(8,128)S(1)}, f32[8,2,64,64]{3,2,1,0:T(8,128)}, u32[]{:S(2)}) %copy-start) | copy-done | bytes 262168
  1.7 0.2 pack.1
  1.8 0.7 collective-permute-start.1
  2.5 0.7 collective-permute-start.2
  3.2 4.0 %collective-permute-start = (f32[512,128]{1,0:T(8,128)S(1)}, f32[512,128]{1,0:T(8,128)S(1)}, u32[]{:S(2)}, u32[]{:S(2)}) collective-permute-start(f32[512,128]{1,0:T(8,128)S(1)} %get-tuple-element.22.own_ref), channel_id=1, source_target_pairs={{0,2},{1,3},{2,0},{3,1},{4,6},{5,7},{6,4},{7,5},{8,10},{9,11},{10,... | collective-permute-start | bytes 786440 | tf_op jit(solution)/shard_map/ppermute | solution.py:346
  7.3 0.7 copy-done.1
  7.9 0.1 pad_dynamic-slice_fusion
  8.0 4.2 %collective-permute-start.4 = (f32[512,128]{1,0:T(8,128)S(1)}, f32[512,128]{1,0:T(8,128)S(1)}, u32[]{:S(2)}, u32[]{:S(2)}) collective-permute-start(f32[512,128]{1,0:T(8,128)S(1)} %get-tuple-element.22.own_ref), channel_id=1, source_target_pairs={{0,4},{1,5},{2,6},{3,7},{4,0},{5,1},{6,2},{7,3},{8,12},{9,13},{10,... | collective-permute-start | bytes 786440 | tf_op jit(solution)/shard_map/ppermute | solution.py:350
  12.2 1.9 %collective-permute-start.5 = (f32[512,128]{1,0:T(8,128)S(1)}, f32[512,128]{1,0:T(8,128)S(1)}, u32[]{:S(2)}, u32[]{:S(2)}) collective-permute-start(f32[512,128]{1,0:T(8,128)S(1)} %get-tuple-element.22.own_ref), channel_id=1, source_target_pairs={{0,6},{1,7},{2,4},{3,5},{4,2},{5,3},{6,0},{7,1},{8,14},{9,15},{10,... | collective-permute-start | bytes 786440 | tf_op jit(solution)/shard_map/ppermute | solution.py:351
  14.2 0.0 copy-start.2
  14.2 0.7 copy-done.2
  14.9 0.1 pad_dynamic-slice_fusion.1
  15.0 0.1 concatenate.3.s_ref
  15.1 0.6 triangle.1
  15.7 0.7 collective-permute-start.7
  16.4 16.6 %collective-permute-start.3 = (f32[1024,128]{1,0:T(8,128)S(1)}, f32[1024,128]{1,0:T(8,128)S(1)}, u32[]{:S(2)}, u32[]{:S(2)}) collective-permute-start(f32[1024,128]{1,0:T(8,128)S(1)} %get-tuple-element.21.refs_0_), channel_id=1, source_target_pairs={{0,1},{1,0},{2,3},{3,2},{4,5},{5,4},{6,7},{7,6},{8,9},{9,8},{10,11... | collective-permute-start | bytes 1572872 | tf_op jit(solution)/shard_map/ppermute | solution.py:332
  33.1 7.4 %collective-permute-start.6 = (f32[1024,128]{1,0:T(8,128)S(1)}, f32[1024,128]{1,0:T(8,128)S(1)}, u32[]{:S(2)}, u32[]{:S(2)}) collective-permute-start(f32[1024,128]{1,0:T(8,128)S(1)} %join.1.refs_2_), channel_id=1, source_target_pairs={{0,1},{1,0},{2,3},{3,2},{4,5},{5,4},{6,7},{7,6},{8,9},{9,8},{10,11... | collective-permute-start | bytes 1572872 | tf_op jit(solution)/shard_map/ppermute | solution.py:332
  40.5 1.9 %collective-permute-start.8 = (f32[576,128]{1,0:T(8,128)S(1)}, f32[576,128]{1,0:T(8,128)S(1)}, u32[]{:S(2)}, u32[]{:S(2)}) collective-permute-start(f32[576,128]{1,0:T(8,128)S(1)} %collective-permute-done.7.ta), channel_id=1, source_target_pairs={{0,1},{1,0},{2,3},{3,2},{4,5},{5,4},{6,7},{7,6},{8,9},{9,8},{10,11... | collective-permute-start | bytes 884744 | tf_op jit(solution)/shard_map/ppermute | solution.py:332
  42.4 3.9 %square.1 = (f32[512,512]{1,0:T(8,128)S(1)}, f32[512,512]{1,0:T(8,128)S(1)}, bf16[512,512]{1,0:T(8,128)(2,1)S(1)}, bf16[512,512]{1,0:T(8,128)(2,1)S(1)}, f32[512,512]{1,0:T(8,128)S(1)}, /*index=5*/f32[1,128]{1,0:T(1,128)S(1)}) custom-call(s32[76]{0:T(128)S(1)} %concatenate.3.s_ref, f32[1024,128]{1,0:T(8,128)S(1)} %get-tuple-element.21.refs_0_, ...), custom_call_target="tpu_custom_call" | custom-call | tf_op jit(solution)/shard_map/square/pallas_call | solution.py:370
  46.4 6.6 %second.1 = (f32[2,512,128]{2,1,0:T(8,128)S(1)}, f32[512,128]{1,0:T(8,128)S(1)}, f32[512,128]{1,0:T(8,128)S(1)}, f32[96,128]{1,0:T(8,128)S(1)}) custom-call(s32[76]{0:T(128)S(1)} %concatenate.3.s_ref, f32[512,512]{1,0:T(8,128)S(1)} %get-tuple-element.23.p1_ref, f32[512,512]{1,0:T(8,128)S(1)} %get-tuple-element.24.v_ref, ...), custom_call_target="tpu_custom_call" | custom-call | tf_op jit(solution)/shard_map/second/pallas_call | solution.py:387
  53.0 2.2 %collective-permute-start.10 = (f32[512,128]{1,0:T(8,128)S(1)}, f32[512,128]{1,0:T(8,128)S(1)}, u32[]{:S(2)}, u32[]{:S(2)}) collective-permute-start(f32[512,128]{1,0:T(8,128)S(1)} %get-tuple-element.32), channel_id=1, source_target_pairs={{0,7},{1,6},{2,5},{3,4},{4,3},{5,2},{6,1},{7,0},{8,15},{9,14},{10,... | collective-permute-start | bytes 786440 | tf_op jit(solution)/shard_map/ppermute | solution.py:403
  55.3 0.7 collective-permute-start.9
  56.0 38.8 %all_to_all.11 = f32[96,1,128]{2,1,0:T(1,128)S(1)} all-to-all(f32[96,1,128]{2,1,0:T(1,128)S(1)} %bitcast.13), channel_id=1, replica_groups=mesh['row'=96,'col'=8] {'row'}, dimensions={0} | all-to-all | bytes 98304 | tf_op jit(solution)/shard_map/all_to_all | solution.py:404
  94.8 1.5 %last.1 = (f32[8,2,64,64]{3,2,1,0:T(8,128)}, f32[2]{0:T(128)}) custom-call(s32[76]{0:T(128)S(1)} %concatenate.3.s_ref, f32[2,512,128]{2,1,0:T(8,128)S(1)} %get-tuple-element.30.own_ref, f32[512,128]{1,0:T(8,128)S(1)} %collective-permute-done.9.far_ref, f32[512,128]{1,0:T(8,128)S(1)} %collective-permute-done.10.near_ref, f32[96,128]{1,0:T(8,128)S(1)} %bitcast.12), custom_call_target="tpu_custom_call" | custom-call | tf_op jit(solution)/shard_map/last/pallas_call | solution.py:405
  (15 shorter events, 0.1 us)
Async XLA Ops:
  0.6 1.0 %copy-start = (f32[8,2,64,64]{3,2,1,0:T(8,128)S(1)}, f32[8,2,64,64]{3,2,1,0:T(8,128)}, u32[]{:S(2)}) copy-start(f32[8,2,64,64]{3,2,1,0:T(8,128)} %v_ref.1) | copy-start | bytes 786436
  1.8 6.2 %collective-permute-start.1 = (f32[256,128]{1,0:T(8,128)S(1)}, f32[256,128]{1,0:T(8,128)S(1)}, u32[]{:S(2)}, u32[]{:S(2)}) collective-permute-start(f32[256,128]{1,0:T(8,128)S(1)} %get-tuple-element.19), channel_id=1, source_target_pairs={{4,2},{12,10},{20,18},{28,26},{36,34},{44,42},{52,50},{60,58},{68,... | collective-permute-start | bytes 393224 | tf_op jit(solution)/shard_map/ppermute | solution.py:347
  2.5 12.5 %collective-permute-start.2 = (f32[256,128]{1,0:T(8,128)S(1)}, f32[256,128]{1,0:T(8,128)S(1)}, u32[]{:S(2)}, u32[]{:S(2)}) collective-permute-start(f32[256,128]{1,0:T(8,128)S(1)} %get-tuple-element.19), channel_id=1, source_target_pairs={{4,0},{12,8},{20,16},{28,24},{36,32},{44,40},{52,48},{60,56},{68,6... | collective-permute-start | bytes 393224 | tf_op jit(solution)/shard_map/ppermute | solution.py:348
  3.2 11.9 %collective-permute-start = (f32[512,128]{1,0:T(8,128)S(1)}, f32[512,128]{1,0:T(8,128)S(1)}, u32[]{:S(2)}, u32[]{:S(2)}) collective-permute-start(f32[512,128]{1,0:T(8,128)S(1)} %get-tuple-element.22.own_ref), channel_id=1, source_target_pairs={{0,2},{1,3},{2,0},{3,1},{4,6},{5,7},{6,4},{7,5},{8,10},{9,11},{10,... | collective-permute-start | bytes 786440 | tf_op jit(solution)/shard_map/ppermute | solution.py:346
  7.2 0.7 copy-start.1
  8.0 25.0 %collective-permute-start.4 = (f32[512,128]{1,0:T(8,128)S(1)}, f32[512,128]{1,0:T(8,128)S(1)}, u32[]{:S(2)}, u32[]{:S(2)}) collective-permute-start(f32[512,128]{1,0:T(8,128)S(1)} %get-tuple-element.22.own_ref), channel_id=1, source_target_pairs={{0,4},{1,5},{2,6},{3,7},{4,0},{5,1},{6,2},{7,3},{8,12},{9,13},{10,... | collective-permute-start | bytes 786440 | tf_op jit(solution)/shard_map/ppermute | solution.py:350
  12.2 20.8 %collective-permute-start.5 = (f32[512,128]{1,0:T(8,128)S(1)}, f32[512,128]{1,0:T(8,128)S(1)}, u32[]{:S(2)}, u32[]{:S(2)}) collective-permute-start(f32[512,128]{1,0:T(8,128)S(1)} %get-tuple-element.22.own_ref), channel_id=1, source_target_pairs={{0,6},{1,7},{2,4},{3,5},{4,2},{5,3},{6,0},{7,1},{8,14},{9,15},{10,... | collective-permute-start | bytes 786440 | tf_op jit(solution)/shard_map/ppermute | solution.py:351
  14.2 0.7 copy-start.2
  15.7 24.8 %collective-permute-start.7 = (f32[576,128]{1,0:T(8,128)S(1)}, f32[576,128]{1,0:T(8,128)S(1)}, u32[]{:S(2)}, u32[]{:S(2)}) collective-permute-start(f32[576,128]{1,0:T(8,128)S(1)} %get-tuple-element.29), channel_id=1, source_target_pairs={{4,8},{5,9},{6,10},{7,11},{12,16},{13,17},{14,18},{15,19},{20,24},... | collective-permute-start | bytes 884744 | tf_op jit(solution)/shard_map/ppermute | solution.py:361
  16.4 26.0 %collective-permute-start.3 = (f32[1024,128]{1,0:T(8,128)S(1)}, f32[1024,128]{1,0:T(8,128)S(1)}, u32[]{:S(2)}, u32[]{:S(2)}) collective-permute-start(f32[1024,128]{1,0:T(8,128)S(1)} %get-tuple-element.21.refs_0_), channel_id=1, source_target_pairs={{0,1},{1,0},{2,3},{3,2},{4,5},{5,4},{6,7},{7,6},{8,9},{9,8},{10,11... | collective-permute-start | bytes 1572872 | tf_op jit(solution)/shard_map/ppermute | solution.py:332
  33.1 9.3 %collective-permute-start.6 = (f32[1024,128]{1,0:T(8,128)S(1)}, f32[1024,128]{1,0:T(8,128)S(1)}, u32[]{:S(2)}, u32[]{:S(2)}) collective-permute-start(f32[1024,128]{1,0:T(8,128)S(1)} %join.1.refs_2_), channel_id=1, source_target_pairs={{0,1},{1,0},{2,3},{3,2},{4,5},{5,4},{6,7},{7,6},{8,9},{9,8},{10,11... | collective-permute-start | bytes 1572872 | tf_op jit(solution)/shard_map/ppermute | solution.py:332
  40.5 5.9 %collective-permute-start.8 = (f32[576,128]{1,0:T(8,128)S(1)}, f32[576,128]{1,0:T(8,128)S(1)}, u32[]{:S(2)}, u32[]{:S(2)}) collective-permute-start(f32[576,128]{1,0:T(8,128)S(1)} %collective-permute-done.7.ta), channel_id=1, source_target_pairs={{0,1},{1,0},{2,3},{3,2},{4,5},{5,4},{6,7},{7,6},{8,9},{9,8},{10,11... | collective-permute-start | bytes 884744 | tf_op jit(solution)/shard_map/ppermute | solution.py:332
  53.0 41.8 %collective-permute-start.10 = (f32[512,128]{1,0:T(8,128)S(1)}, f32[512,128]{1,0:T(8,128)S(1)}, u32[]{:S(2)}, u32[]{:S(2)}) collective-permute-start(f32[512,128]{1,0:T(8,128)S(1)} %get-tuple-element.32), channel_id=1, source_target_pairs={{0,7},{1,6},{2,5},{3,4},{4,3},{5,2},{6,1},{7,0},{8,15},{9,14},{10,... | collective-permute-start | bytes 786440 | tf_op jit(solution)/shard_map/ppermute | solution.py:403
  55.3 39.5 %collective-permute-start.9 = (f32[512,128]{1,0:T(8,128)S(1)}, f32[512,128]{1,0:T(8,128)S(1)}, u32[]{:S(2)}, u32[]{:S(2)}) collective-permute-start(f32[512,128]{1,0:T(8,128)S(1)} %get-tuple-element.31), channel_id=1, source_target_pairs={{7,8},{6,9},{5,10},{4,11},{15,16},{14,17},{13,18},{12,19},{23,24},... | collective-permute-start | bytes 786440 | tf_op jit(solution)/shard_map/ppermute | solution.py:402

commit v9 on v8

--- a/solution.py
+++ b/solution.py
@@ -37,6 +37,17 @@
         return lax.dot_general(x, y, (dims, ((), ())), preferred_element_type=F32)
 
     return one(ah, bh) + (one(ah, bl) + one(al, bh))
+
+
+def dot3_stacked(a, b):
+    (ah, al), (bh, bl) = a, b
+    size = ah.shape[0]
+
+    def one(x, y):
+        return lax.dot_general(x, y, (NT, ((), ())), preferred_element_type=F32)
+
+    both = one(jnp.concatenate([ah, al], axis=0), bh)
+    return both[:size] + (one(ah, bl) + both[size:])
 
 
 NN = ((1,), (0,))
@@ -162,7 +173,7 @@
 
 
 def second_kernel(s_ref, p1_ref, v_ref, vh_ref, vl_ref, pv_ref, tr_ref, ta, tb,
-                  own_ref, far_ref, near_ref, sums_ref, t_ref, w_ref, mh, ml):
+                  own_ref, share_ref, sums_ref, t_ref, w_ref, mh, ml):
     core, col, upper = s_ref[1], s_ref[2], s_ref[3]
     lane = lax.broadcasted_iota(jnp.int32, (B, N), 1)
     zero = jnp.zeros((B, 128), F32)
@@ -254,27 +265,24 @@
     both = jnp.where(spot == 2, jnp.sum(outer, axis=1, keepdims=True), both)
     sums_ref[...] = jnp.broadcast_to(both, sums_ref.shape)
 
-    wide = (lax.broadcasted_iota(jnp.int32, (B, 128), 1) >= B).astype(jnp.int32)
     shift = 6 - 2 * col
 
-    def share(i, rows, panel):
-        block = rows + i + shift
-        pair = row(jnp.clip(block, -1, 2 * H - 1), 128)
-        span = lanes(panel)
-        product = dot3(
-            (mh[row(rows + i), span], ml[row(rows + i), span]),
-            (mh[pair, span], ml[pair, span]), NT,
+    def share(i, rows, block, panel):
+        pair, span = row(block, 128), lanes(panel)
+        return dot3_stacked(
+            (mh[row(rows + i), span], ml[row(rows + i), span]), (mh[pair, span], ml[pair, span])
         )
-        index = block + wide - base
-        return jnp.where((index >= 0) & (index < H), product, 0.0)
-
-    for i in range(H):
-        far_ref[strip(i), :] = share(i, other, base)
-        near_ref[strip(i), :] = share(i, base, other)
+
+    for i in range(H):
+        far = (upper == 0) & (shift + i >= H) | (upper == 1) & (shift + i < 0)
+        rows = jnp.where(far, other, base)
+        share_ref[strip(i), :] = share(i, rows, rows + i + shift, jnp.where(far, base, other))
         here = row(base + i)
         block = base + i + 2 * col - H
         pair = row(block, 128)
-        own_ref[0, strip(i), :] = dot3((mh[here, :], ml[here, :]), (mh[pair, :], ml[pair, :]), NT)
+        own_ref[0, strip(i), :] = dot3_stacked(
+            (mh[here, :], ml[here, :]), (mh[pair, :], ml[pair, :])
+        )
         if i % 2:
             span = pl.ds(pl.multiple_of((block - 1) * B, 128), 256)
             held = mh[here, span].astype(F32) + ml[here, span].astype(F32)
@@ -283,13 +291,20 @@
             span = pl.ds(pl.multiple_of(block * B, 128), 128)
             held = mh[here, span].astype(F32) + ml[here, span].astype(F32)
         own_ref[1, strip(i), :] = held
+    i = 2 * (col & 3) + 1
+    here = at(i, B)
+    wide = lax.broadcasted_iota(jnp.int32, (B, 128), 1) >= B
+    share_ref[here, :] = jnp.where(wide, share(i, 0, 7 - 8 * upper, H), share_ref[here, :])
 
 
 def last_kernel(s_ref, own_ref, far_ref, near_ref, sums_ref, out_ref, traces_ref):
     col, upper = s_ref[2], s_ref[3]
     wide = lax.broadcasted_iota(jnp.int32, (B, 128), 1) >= B
     for i in range(H):
-        squared = own_ref[0, strip(i), :] + (far_ref[strip(i), :] + near_ref[strip(i), :])
+        index = i + 2 * col - H + wide.astype(jnp.int32)
+        inside = (index >= 0) & (index < H)
+        share = jnp.where(inside, near_ref[strip(i), :], far_ref[strip(i), :])
+        squared = own_ref[0, strip(i), :] + share
         keep, pick = [], []
         for h in range(2):
             far = jnp.abs(2 * col + h - H)
@@ -384,11 +399,11 @@
         mib=24, name="square",
     )(scalars, joined, joined2, distant, distant2)
 
-    own, far, near, sums = call(
+    own, share, sums = call(
         second_kernel,
-        out_shape=[shape(2, N, 128), shape(N, 128), shape(N, 128), shape(rows, 128)],
+        out_shape=[shape(2, N, 128), shape(N, 128), shape(rows, 128)],
         in_specs=[SMEM] + [VMEM] * 8,
-        out_specs=[VMEM] * 4,
+        out_specs=[VMEM] * 3,
         scratch_shapes=[
             pltpu.VMEM((2, 576, 128), F32),
             pltpu.VMEM((N, N), F32),
@@ -399,8 +414,8 @@
     )(scalars, *old, trace, ta, tb)
 
     pairs = [(index(r, 7 - c), index(r + 1, c)) for r, c in ends]
-    far = lax.ppermute(far, both, pairs + [(b, a) for a, b in pairs])
-    near = lax.ppermute(near, "col", [(c, 7 - c) for c in range(8)])
+    far = lax.ppermute(share, both, pairs + [(b, a) for a, b in pairs])
+    near = lax.ppermute(share, "col", [(c, 7 - c) for c in range(8)])
     sums = lax.all_to_all(sums, "row", 0, 0, tiled=True)
     return call(
         last_kernel,

time: 97.8 us -> 96.1 us (0.983)
  Pallas kernels: 12.9 us -> 11.2 us
    pallas_call x1, Pallas kernels: 6.63 us -> 4.91 us  [per_device(): call(second_kernel, out_shape=[shape(2, N, 128), shape(N, 128), shape(row...]
where the time goes in v9:
time: 96.1 us; the launch traced here: 94.6 us
  starting transfers between devices  41 us (43%)
  blocking collectives  38.8 us (40%)
  Pallas kernels  11.2 us (12%)
  local copies, waits for them, and re-layouts  2.62 us (3%)
    all_to_all x1, blocking collectives, per_device(): sums = lax.all_to_all(sums, 'row', 0, 0, tiled=True)  38.8 us
    ppermute x3, starting transfers between devices, swap(): return lax.ppermute(x, 'col', [(c, c ^ 1) for c in range(8)])  25.9 us
    pallas_call x1, Pallas kernels, per_device(): call(second_kernel, out_shape=[shape(2, N, 128), shape(N, 128), shape(row...  4.91 us
    ppermute x1, starting transfers between devices, per_device(): cross = lax.ppermute(later, 'col', [(c, c ^ 4) for c in range(8)])  4.21 us
    ppermute x1, starting transfers between devices, per_device(): near = lax.ppermute(packed, 'col', [(c, c ^ 2) for c in range(8)])  4.03 us
    pallas_call x1, Pallas kernels, per_device(): call(square_kernel, out_shape=[shape(N, N), shape(N, N), jax.ShapeDtypeSt...  3.94 us
    unnamed x6, local copies, waits for them, and re-layouts  2.38 us
    ppermute x1, starting transfers between devices, per_device(): near = lax.ppermute(share, 'col', [(c, 7 - c) for c in range(8)])  2.23 us
  transfers between devices with their start and end apart: 11, of which 0 were waited for; matrix products, arithmetic and copies ran while one was open for 0% of the time, Pallas kernels for 5%

profile of v9, /device:TPU:1, one launch (start us, length us, event | category | flops | bytes accessed | tf_op | source)
XLA Modules:
  0.0 94.6 jit_solution(9072273624235082519)
XLA Ops:
  0.6 1.0 %copy-done = f32[8,2,64,64]{3,2,1,0:T(8,128)S(1)} copy-done((f32[8,2,64,64]{3,2,1,0:T(8,128)S(1)}, f32[8,2,64,64]{3,2,1,0:T(8,128)}, u32[]{:S(2)}) %copy-start) | copy-done | bytes 262168
  1.7 0.2 pack.1
  1.8 0.7 collective-permute-start.1
  2.5 0.7 collective-permute-start.2
  3.2 4.0 %collective-permute-start = (f32[512,128]{1,0:T(8,128)S(1)}, f32[512,128]{1,0:T(8,128)S(1)}, u32[]{:S(2)}, u32[]{:S(2)}) collective-permute-start(f32[512,128]{1,0:T(8,128)S(1)} %get-tuple-element.21.own_ref), channel_id=1, source_target_pairs={{0,2},{1,3},{2,0},{3,1},{4,6},{5,7},{6,4},{7,5},{8,10},{9,11},{10,... | collective-permute-start | bytes 786440 | tf_op jit(solution)/shard_map/ppermute | solution.py:361
  7.3 0.7 copy-done.1
  7.9 0.1 pad_dynamic-slice_fusion
  8.0 4.2 %collective-permute-start.4 = (f32[512,128]{1,0:T(8,128)S(1)}, f32[512,128]{1,0:T(8,128)S(1)}, u32[]{:S(2)}, u32[]{:S(2)}) collective-permute-start(f32[512,128]{1,0:T(8,128)S(1)} %get-tuple-element.21.own_ref), channel_id=1, source_target_pairs={{0,4},{1,5},{2,6},{3,7},{4,0},{5,1},{6,2},{7,3},{8,12},{9,13},{10,... | collective-permute-start | bytes 786440 | tf_op jit(solution)/shard_map/ppermute | solution.py:365
  12.2 1.9 %collective-permute-start.5 = (f32[512,128]{1,0:T(8,128)S(1)}, f32[512,128]{1,0:T(8,128)S(1)}, u32[]{:S(2)}, u32[]{:S(2)}) collective-permute-start(f32[512,128]{1,0:T(8,128)S(1)} %get-tuple-element.21.own_ref), channel_id=1, source_target_pairs={{0,6},{1,7},{2,4},{3,5},{4,2},{5,3},{6,0},{7,1},{8,14},{9,15},{10,... | collective-permute-start | bytes 786440 | tf_op jit(solution)/shard_map/ppermute | solution.py:366
  14.2 0.0 copy-start.2
  14.2 0.7 copy-done.2
  14.9 0.1 pad_dynamic-slice_fusion.1
  15.0 0.1 concatenate.3.s_ref
  15.1 0.6 triangle.1
  15.7 0.7 collective-permute-start.7
  16.4 16.6 %collective-permute-start.3 = (f32[1024,128]{1,0:T(8,128)S(1)}, f32[1024,128]{1,0:T(8,128)S(1)}, u32[]{:S(2)}, u32[]{:S(2)}) collective-permute-start(f32[1024,128]{1,0:T(8,128)S(1)} %get-tuple-element.20.refs_0_), channel_id=1, source_target_pairs={{0,1},{1,0},{2,3},{3,2},{4,5},{5,4},{6,7},{7,6},{8,9},{9,8},{10,11... | collective-permute-start | bytes 1572872 | tf_op jit(solution)/shard_map/ppermute | solution.py:347
  33.1 7.4 %collective-permute-start.6 = (f32[1024,128]{1,0:T(8,128)S(1)}, f32[1024,128]{1,0:T(8,128)S(1)}, u32[]{:S(2)}, u32[]{:S(2)}) collective-permute-start(f32[1024,128]{1,0:T(8,128)S(1)} %join.1.refs_2_), channel_id=1, source_target_pairs={{0,1},{1,0},{2,3},{3,2},{4,5},{5,4},{6,7},{7,6},{8,9},{9,8},{10,11... | collective-permute-start | bytes 1572872 | tf_op jit(solution)/shard_map/ppermute | solution.py:347
  40.5 1.9 %collective-permute-start.8 = (f32[576,128]{1,0:T(8,128)S(1)}, f32[576,128]{1,0:T(8,128)S(1)}, u32[]{:S(2)}, u32[]{:S(2)}) collective-permute-start(f32[576,128]{1,0:T(8,128)S(1)} %collective-permute-done.7.ta), channel_id=1, source_target_pairs={{0,1},{1,0},{2,3},{3,2},{4,5},{5,4},{6,7},{7,6},{8,9},{9,8},{10,11... | collective-permute-start | bytes 884744 | tf_op jit(solution)/shard_map/ppermute | solution.py:347
  42.4 3.9 %square.1 = (f32[512,512]{1,0:T(8,128)S(1)}, f32[512,512]{1,0:T(8,128)S(1)}, bf16[512,512]{1,0:T(8,128)(2,1)S(1)}, bf16[512,512]{1,0:T(8,128)(2,1)S(1)}, f32[512,512]{1,0:T(8,128)S(1)}, /*index=5*/f32[1,128]{1,0:T(1,128)S(1)}) custom-call(s32[76]{0:T(128)S(1)} %concatenate.3.s_ref, f32[1024,128]{1,0:T(8,128)S(1)} %get-tuple-element.20.refs_0_, ...), custom_call_target="tpu_custom_call" | custom-call | tf_op jit(solution)/shard_map/square/pallas_call | solution.py:385
  46.4 4.9 %second.1 = (f32[2,512,128]{2,1,0:T(8,128)S(1)}, f32[512,128]{1,0:T(8,128)S(1)}, f32[96,128]{1,0:T(8,128)S(1)}) custom-call(s32[76]{0:T(128)S(1)} %concatenate.3.s_ref, f32[512,512]{1,0:T(8,128)S(1)} %get-tuple-element.22.p1_ref, f32[512,512]{1,0:T(8,128)S(1)} %get-tuple-element.23.v_ref, bf16[512,512]{1,0:T(8,128)(2,1)S(1)} %get-tuple-element.24.vh_ref, ...), custom_call_target="tpu_custom_call" | custom-call | tf_op jit(solution)/shard_map/second/pallas_call | solution.py:402
  51.3 2.2 %collective-permute-start.10 = (f32[512,128]{1,0:T(8,128)S(1)}, f32[512,128]{1,0:T(8,128)S(1)}, u32[]{:S(2)}, u32[]{:S(2)}) collective-permute-start(f32[512,128]{1,0:T(8,128)S(1)} %get-tuple-element.30), channel_id=1, source_target_pairs={{0,7},{1,6},{2,5},{3,4},{4,3},{5,2},{6,1},{7,0},{8,15},{9,14},{10,... | collective-permute-start | bytes 786440 | tf_op jit(solution)/shard_map/ppermute | solution.py:418
  53.5 0.7 collective-permute-start.9
  54.2 38.8 %all_to_all.11 = f32[96,1,128]{2,1,0:T(1,128)S(1)} all-to-all(f32[96,1,128]{2,1,0:T(1,128)S(1)} %bitcast.13), channel_id=1, replica_groups=mesh['row'=96,'col'=8] {'row'}, dimensions={0} | all-to-all | bytes 98304 | tf_op jit(solution)/shard_map/all_to_all | solution.py:419
  93.1 1.5 %last.1 = (f32[8,2,64,64]{3,2,1,0:T(8,128)}, f32[2]{0:T(128)}) custom-call(s32[76]{0:T(128)S(1)} %concatenate.3.s_ref, f32[2,512,128]{2,1,0:T(8,128)S(1)} %get-tuple-element.29.own_ref, f32[512,128]{1,0:T(8,128)S(1)} %collective-permute-done.9.far_ref, f32[512,128]{1,0:T(8,128)S(1)} %collective-permute-done.10.near_ref, f32[96,128]{1,0:T(8,128)S(1)} %bitcast.12), custom_call_target="tpu_custom_call" | custom-call | tf_op jit(solution)/shard_map/last/pallas_call | solution.py:420
  (15 shorter events, 0.1 us)
Async XLA Ops:
  0.6 1.0 %copy-start = (f32[8,2,64,64]{3,2,1,0:T(8,128)S(1)}, f32[8,2,64,64]{3,2,1,0:T(8,128)}, u32[]{:S(2)}) copy-start(f32[8,2,64,64]{3,2,1,0:T(8,128)} %v_ref.1) | copy-start | bytes 786436
  1.8 6.2 %collective-permute-start.1 = (f32[256,128]{1,0:T(8,128)S(1)}, f32[256,128]{1,0:T(8,128)S(1)}, u32[]{:S(2)}, u32[]{:S(2)}) collective-permute-start(f32[256,128]{1,0:T(8,128)S(1)} %get-tuple-element.18), channel_id=1, source_target_pairs={{4,2},{12,10},{20,18},{28,26},{36,34},{44,42},{52,50},{60,58},{68,... | collective-permute-start | bytes 393224 | tf_op jit(solution)/shard_map/ppermute | solution.py:362
  2.5 12.5 %collective-permute-start.2 = (f32[256,128]{1,0:T(8,128)S(1)}, f32[256,128]{1,0:T(8,128)S(1)}, u32[]{:S(2)}, u32[]{:S(2)}) collective-permute-start(f32[256,128]{1,0:T(8,128)S(1)} %get-tuple-element.18), channel_id=1, source_target_pairs={{4,0},{12,8},{20,16},{28,24},{36,32},{44,40},{52,48},{60,56},{68,6... | collective-permute-start | bytes 393224 | tf_op jit(solution)/shard_map/ppermute | solution.py:363
  3.2 11.9 %collective-permute-start = (f32[512,128]{1,0:T(8,128)S(1)}, f32[512,128]{1,0:T(8,128)S(1)}, u32[]{:S(2)}, u32[]{:S(2)}) collective-permute-start(f32[512,128]{1,0:T(8,128)S(1)} %get-tuple-element.21.own_ref), channel_id=1, source_target_pairs={{0,2},{1,3},{2,0},{3,1},{4,6},{5,7},{6,4},{7,5},{8,10},{9,11},{10,... | collective-permute-start | bytes 786440 | tf_op jit(solution)/shard_map/ppermute | solution.py:361
  7.2 0.7 copy-start.1
  8.0 25.0 %collective-permute-start.4 = (f32[512,128]{1,0:T(8,128)S(1)}, f32[512,128]{1,0:T(8,128)S(1)}, u32[]{:S(2)}, u32[]{:S(2)}) collective-permute-start(f32[512,128]{1,0:T(8,128)S(1)} %get-tuple-element.21.own_ref), channel_id=1, source_target_pairs={{0,4},{1,5},{2,6},{3,7},{4,0},{5,1},{6,2},{7,3},{8,12},{9,13},{10,... | collective-permute-start | bytes 786440 | tf_op jit(solution)/shard_map/ppermute | solution.py:365
  12.2 20.8 %collective-permute-start.5 = (f32[512,128]{1,0:T(8,128)S(1)}, f32[512,128]{1,0:T(8,128)S(1)}, u32[]{:S(2)}, u32[]{:S(2)}) collective-permute-start(f32[512,128]{1,0:T(8,128)S(1)} %get-tuple-element.21.own_ref), channel_id=1, source_target_pairs={{0,6},{1,7},{2,4},{3,5},{4,2},{5,3},{6,0},{7,1},{8,14},{9,15},{10,... | collective-permute-start | bytes 786440 | tf_op jit(solution)/shard_map/ppermute | solution.py:366
  14.2 0.7 copy-start.2
  15.7 24.8 %collective-permute-start.7 = (f32[576,128]{1,0:T(8,128)S(1)}, f32[576,128]{1,0:T(8,128)S(1)}, u32[]{:S(2)}, u32[]{:S(2)}) collective-permute-start(f32[576,128]{1,0:T(8,128)S(1)} %get-tuple-element.28), channel_id=1, source_target_pairs={{4,8},{5,9},{6,10},{7,11},{12,16},{13,17},{14,18},{15,19},{20,24},... | collective-permute-start | bytes 884744 | tf_op jit(solution)/shard_map/ppermute | solution.py:376
  16.4 26.0 %collective-permute-start.3 = (f32[1024,128]{1,0:T(8,128)S(1)}, f32[1024,128]{1,0:T(8,128)S(1)}, u32[]{:S(2)}, u32[]{:S(2)}) collective-permute-start(f32[1024,128]{1,0:T(8,128)S(1)} %get-tuple-element.20.refs_0_), channel_id=1, source_target_pairs={{0,1},{1,0},{2,3},{3,2},{4,5},{5,4},{6,7},{7,6},{8,9},{9,8},{10,11... | collective-permute-start | bytes 1572872 | tf_op jit(solution)/shard_map/ppermute | solution.py:347
  33.1 9.3 %collective-permute-start.6 = (f32[1024,128]{1,0:T(8,128)S(1)}, f32[1024,128]{1,0:T(8,128)S(1)}, u32[]{:S(2)}, u32[]{:S(2)}) collective-permute-start(f32[1024,128]{1,0:T(8,128)S(1)} %join.1.refs_2_), channel_id=1, source_target_pairs={{0,1},{1,0},{2,3},{3,2},{4,5},{5,4},{6,7},{7,6},{8,9},{9,8},{10,11... | collective-permute-start | bytes 1572872 | tf_op jit(solution)/shard_map/ppermute | solution.py:347
  40.5 5.9 %collective-permute-start.8 = (f32[576,128]{1,0:T(8,128)S(1)}, f32[576,128]{1,0:T(8,128)S(1)}, u32[]{:S(2)}, u32[]{:S(2)}) collective-permute-start(f32[576,128]{1,0:T(8,128)S(1)} %collective-permute-done.7.ta), channel_id=1, source_target_pairs={{0,1},{1,0},{2,3},{3,2},{4,5},{5,4},{6,7},{7,6},{8,9},{9,8},{10,11... | collective-permute-start | bytes 884744 | tf_op jit(solution)/shard_map/ppermute | solution.py:347
  51.3 41.8 %collective-permute-start.10 = (f32[512,128]{1,0:T(8,128)S(1)}, f32[512,128]{1,0:T(8,128)S(1)}, u32[]{:S(2)}, u32[]{:S(2)}) collective-permute-start(f32[512,128]{1,0:T(8,128)S(1)} %get-tuple-element.30), channel_id=1, source_target_pairs={{0,7},{1,6},{2,5},{3,4},{4,3},{5,2},{6,1},{7,0},{8,15},{9,14},{10,... | collective-permute-start | bytes 786440 | tf_op jit(solution)/shard_map/ppermute | solution.py:418
  53.5 39.5 %collective-permute-start.9 = (f32[512,128]{1,0:T(8,128)S(1)}, f32[512,128]{1,0:T(8,128)S(1)}, u32[]{:S(2)}, u32[]{:S(2)}) collective-permute-start(f32[512,128]{1,0:T(8,128)S(1)} %get-tuple-element.30), channel_id=1, source_target_pairs={{7,8},{6,9},{5,10},{4,11},{15,16},{14,17},{13,18},{12,19},{23,24},... | collective-permute-start | bytes 786440 | tf_op jit(solution)/shard_map/ppermute | solution.py:417

commit v10 on v9

--- a/solution.py
+++ b/solution.py
@@ -74,16 +74,29 @@
         return keep, self.flags * self.s_ref[self.start + self.rows + i] == 1
 
 
-def pack_kernel(v_ref, out_ref, diag_ref):
+def pack_kernel(v_ref, out_ref, diag_ref, cut_ref):
     for i in range(H):
         out_ref[strip(i), :] = jnp.concatenate([v_ref[i, 0], v_ref[i, 1]], axis=1)
     for i in range(4):
         diag_ref[strip(i), :] = jnp.concatenate([v_ref[i, 0], v_ref[i + 4, 0]], axis=1)
+    col = lax.axis_index("col")
+
+    @pl.when(col < 4)
+    def _():
+        cut_ref[...] = out_ref[0 : N - B, :]
+
+    @pl.when(col >= 4)
+    def _():
+        cut_ref[...] = out_ref[B:N, :]
+
+    @pl.when(col == 4)
+    def _():
+        cut_ref[0:B, :] = jnp.concatenate([v_ref[1, 0], v_ref[0, 0]], axis=1)
 
 
 def join_kernel(first_ref, second_ref, out_ref):
-    out_ref[0:N, :] = first_ref[...]
-    out_ref[N : 2 * N, :] = second_ref[...]
+    out_ref[0 : N - B, :] = first_ref[...]
+    out_ref[N - B : 2 * (N - B), :] = second_ref[...]
 
 
 def triangle_kernel(s_ref, own_ref, near_ref, d1_ref, d2_ref, out_ref, both_ref, low, high):
@@ -126,15 +139,35 @@
     packs, (p1_ref, v_ref, vh_ref, vl_ref, pv_ref, tr_ref) = refs[:4], refs[4:10]
     q_ref, r_ref, rh, rl = refs[10:]
     yl, core, upper = s_ref[0], s_ref[1], s_ref[3]
-    for k in range(4):
+    def place(k, other):
+        return pl.ds(pl.multiple_of(128 * (2 * (yl ^ k) + (core ^ other)), 128), 128)
+
+    for other in range(2):
+        for k in range(2):
+            q_ref[:, place(k, other)] = packs[other][k * N : (k + 1) * N, :]
+
+    def cut(k, other):
+        return packs[2 + other][(k - 2) * (N - B) : (k - 1) * (N - B), :]
+
+    @pl.when(upper == 0)
+    def _():
         for other in range(2):
-            place = 2 * (yl ^ k) + (core ^ other)
-            part = packs[k // 2 * 2 + other][k % 2 * N : (k % 2 + 1) * N, :]
-            q_ref[:, pl.ds(pl.multiple_of(place * 128, 128), 128)] = part
-    total = jnp.zeros((1, 2 * N), F32)
+            for k in range(2, 4):
+                q_ref[B:N, place(k, other)] = cut(k, other)
+        first = pltpu.roll(q_ref[B : 2 * B, N : N + 128], B, 1)
+        lane = lax.broadcasted_iota(jnp.int32, (B, 128), 1)
+        q_ref[0:B, N : N + 128] = jnp.where(lane < B, first, 0.0)
+        q_ref[0:B, N + 128 : 2 * N] = jnp.zeros((B, N - 128), F32)
+
+    @pl.when(upper == 1)
+    def _():
+        for other in range(2):
+            for k in range(2, 4):
+                q_ref[0 : N - B, place(k, other)] = cut(k, other)
+        q_ref[N - B : N, 0:N] = jnp.zeros((B, N), F32)
+
     for i in range(H):
         own = q_ref[strip(i), :]
-        total += jnp.sum(own * own, axis=0, keepdims=True)
         at = i * B
         if i % 2:
             own = pltpu.roll(jnp.concatenate([own, jnp.zeros((B, 128), F32)], axis=1), B, 1)
@@ -145,8 +178,16 @@
         left = W - at - own.shape[1]
         if left:
             parts.append(jnp.zeros((B, left), F32))
-        full = jnp.concatenate(parts, axis=1)
-        r_ref[strip(i), :] = full
+        r_ref[strip(i), :] = jnp.concatenate(parts, axis=1)
+    inner = r_ref[:, N : 2 * N]
+    above = lax.shift_right_logical(lax.broadcasted_iota(jnp.int32, (N, N), 0), 6)
+    along = lax.shift_right_logical(lax.broadcasted_iota(jnp.int32, (N, N), 1), 6)
+    half = jnp.where((above - along) * (1 - 2 * upper) > 0, inner, 0.0)
+    r_ref[:, N : 2 * N] = jnp.where(above == along, inner, half + half.T)
+    total = jnp.zeros((1, W), F32)
+    for i in range(H):
+        full = r_ref[strip(i), :]
+        total += jnp.sum(full * full, axis=0, keepdims=True)
         rh[strip(i), :], rl[strip(i), :] = halves(full)
     tr_ref[...] = jnp.broadcast_to(jnp.sum(total, axis=1, keepdims=True), tr_ref.shape)
 
@@ -354,16 +395,16 @@
 
     ends = [(r, c) for r in range(rows - 1) for c in range(4)]
 
-    packed, diag = call(
-        pack_kernel, out_shape=[shape(N, 128), shape(256, 128)], in_specs=[VMEM],
-        out_specs=[VMEM] * 2, mib=8, name="pack",
+    packed, diag, cut = call(
+        pack_kernel, out_shape=[shape(N, 128), shape(256, 128), shape(N - B, 128)],
+        in_specs=[VMEM], out_specs=[VMEM] * 3, mib=8, name="pack",
     )(values)
     near = lax.ppermute(packed, "col", [(c, c ^ 2) for c in range(8)])
     d1 = lax.ppermute(diag, "col", [(4, 2)])
     d2 = lax.ppermute(diag, "col", [(4, 0)])
-    later, d1 = lax.optimization_barrier((packed, d1))
-    cross = lax.ppermute(later, "col", [(c, c ^ 4) for c in range(8)])
-    far = lax.ppermute(later, "col", [(c, c ^ 6) for c in range(8)])
+    cut, d1 = lax.optimization_barrier((cut, d1))
+    cross = lax.ppermute(cut, "col", [(c, c ^ 4) for c in range(8)])
+    far = lax.ppermute(cut, "col", [(c, c ^ 6) for c in range(8)])
     triangle, joined = call(
         triangle_kernel,
         out_shape=[shape(576, 128), shape(2 * N, 128)],
@@ -376,7 +417,7 @@
     ta = lax.ppermute(triangle, both, pairs + [(b, a) for a, b in pairs])
     joined2 = swap(joined)
     distant = call(
-        join_kernel, out_shape=shape(2 * N, 128), in_specs=[VMEM] * 2, out_specs=VMEM,
+        join_kernel, out_shape=shape(2 * (N - B), 128), in_specs=[VMEM] * 2, out_specs=VMEM,
         mib=8, name="join",
     )(cross, far)
     distant2 = swap(distant)

time: 96.1 us -> 94.7 us (0.985); the launches traced: 94.6 us -> 94.2 us
  blocking collectives: 38.8 us -> 35.9 us
  starting transfers between devices: 41 us -> 43.7 us
    ppermute x3, starting transfers between devices: 25.9 us -> 28.9 us  [swap(): return lax.ppermute(x, 'col', [(c, c ^ 1) for c in range(8)])]
    all_to_all x1, blocking collectives: 38.8 us -> 35.9 us  [per_device(): sums = lax.all_to_all(sums, 'row', 0, 0, tiled=True)]
where the time goes in v10:
time: 94.7 us; the launch traced here: 94.2 us
  starting transfers between devices  43.7 us (46%)
  blocking collectives  35.9 us (38%)
  Pallas kernels  11.8 us (12%)
  local copies, waits for them, and re-layouts  1.96 us (2%)
    all_to_all x1, blocking collectives, per_device(): sums = lax.all_to_all(sums, 'row', 0, 0, tiled=True)  35.9 us
    ppermute x3, starting transfers between devices, swap(): return lax.ppermute(x, 'col', [(c, c ^ 1) for c in range(8)])  28.9 us
    pallas_call x1, Pallas kernels, per_device(): call(second_kernel, out_shape=[shape(2, N, 128), shape(N, 128), shape(row...  4.91 us
    pallas_call x1, Pallas kernels, per_device(): call(square_kernel, out_shape=[shape(N, N), shape(N, N), jax.ShapeDtypeSt...  4.47 us
    ppermute x1, starting transfers between devices, per_device(): cross = lax.ppermute(cut, 'col', [(c, c ^ 4) for c in range(8)])  4.23 us
    ppermute x1, starting transfers between devices, per_device(): near = lax.ppermute(packed, 'col', [(c, c ^ 2) for c in range(8)])  4.03 us
    ppermute x1, starting transfers between devices, per_device(): far = lax.ppermute(cut, 'col', [(c, c ^ 6) for c in range(8)])  1.92 us
    ppermute x1, starting transfers between devices, per_device(): near = lax.ppermute(share, 'col', [(c, 7 - c) for c in range(8)])  1.92 us
  transfers between devices with their start and end apart: 11, of which 0 were waited for; matrix products, arithmetic and copies ran while one was open for 0% of the time, Pallas kernels for 5%

profile of v10, /device:TPU:1, one launch (start us, length us, event | category | flops | bytes accessed | tf_op | source)
XLA Modules:
  0.0 94.2 jit_solution(12055017515215185527)
XLA Ops:
  0.6 1.0 %copy-done = f32[8,2,64,64]{3,2,1,0:T(8,128)S(1)} copy-done((f32[8,2,64,64]{3,2,1,0:T(8,128)S(1)}, f32[8,2,64,64]{3,2,1,0:T(8,128)}, u32[]{:S(2)}) %copy-start) | copy-done | bytes 262168
  1.7 0.2 pack.1
  1.9 0.7 collective-permute-start.1
  2.5 0.7 collective-permute-start.2
  3.2 4.0 %collective-permute-start = (f32[512,128]{1,0:T(8,128)S(1)}, f32[512,128]{1,0:T(8,128)S(1)}, u32[]{:S(2)}, u32[]{:S(2)}) collective-permute-start(f32[512,128]{1,0:T(8,128)S(1)} %get-tuple-element.18.own_ref), channel_id=1, source_target_pairs={{0,2},{1,3},{2,0},{3,1},{4,6},{5,7},{6,4},{7,5},{8,10},{9,11},{10,... | collective-permute-start | bytes 786440 | tf_op jit(solution)/shard_map/ppermute | solution.py:402
  7.3 0.0 copy-start.1
  7.3 0.7 copy-done.1
  8.0 0.1 pad_dynamic-slice_fusion
  8.0 4.2 %collective-permute-start.4 = (f32[448,128]{1,0:T(8,128)S(1)}, f32[448,128]{1,0:T(8,128)S(1)}, u32[]{:S(2)}, u32[]{:S(2)}) collective-permute-start(f32[448,128]{1,0:T(8,128)S(1)} %get-tuple-element.23), channel_id=1, source_target_pairs={{0,4},{1,5},{2,6},{3,7},{4,0},{5,1},{6,2},{7,3},{8,12},{9,13},{10,... | collective-permute-start | bytes 688136 | tf_op jit(solution)/shard_map/ppermute | solution.py:406
  12.3 1.9 %collective-permute-start.5 = (f32[448,128]{1,0:T(8,128)S(1)}, f32[448,128]{1,0:T(8,128)S(1)}, u32[]{:S(2)}, u32[]{:S(2)}) collective-permute-start(f32[448,128]{1,0:T(8,128)S(1)} %get-tuple-element.23), channel_id=1, source_target_pairs={{0,6},{1,7},{2,4},{3,5},{4,2},{5,3},{6,0},{7,1},{8,14},{9,15},{10,... | collective-permute-start | bytes 688136 | tf_op jit(solution)/shard_map/ppermute | solution.py:407
  14.2 0.1 pad_dynamic-slice_fusion.1
  14.3 0.1 concatenate.3.s_ref
  14.4 0.0 collective-permute-done.near_ref
  14.4 0.6 triangle.1
  15.0 0.7 collective-permute-start.7
  15.7 24.6 %collective-permute-start.3 = (f32[1024,128]{1,0:T(8,128)S(1)}, f32[1024,128]{1,0:T(8,128)S(1)}, u32[]{:S(2)}, u32[]{:S(2)}) collective-permute-start(f32[1024,128]{1,0:T(8,128)S(1)} %get-tuple-element.22.refs_0_), channel_id=1, source_target_pairs={{0,1},{1,0},{2,3},{3,2},{4,5},{5,4},{6,7},{7,6},{8,9},{9,8},{10,11... | collective-permute-start | bytes 1572872 | tf_op jit(solution)/shard_map/ppermute | solution.py:388
  40.4 1.9 %collective-permute-start.6 = (f32[896,128]{1,0:T(8,128)S(1)}, f32[896,128]{1,0:T(8,128)S(1)}, u32[]{:S(2)}, u32[]{:S(2)}) collective-permute-start(f32[896,128]{1,0:T(8,128)S(1)} %join.1.refs_2_), channel_id=1, source_target_pairs={{0,1},{1,0},{2,3},{3,2},{4,5},{5,4},{6,7},{7,6},{8,9},{9,8},{10,11... | collective-permute-start | bytes 1376264 | tf_op jit(solution)/shard_map/ppermute | solution.py:388
  42.3 2.4 %collective-permute-start.8 = (f32[576,128]{1,0:T(8,128)S(1)}, f32[576,128]{1,0:T(8,128)S(1)}, u32[]{:S(2)}, u32[]{:S(2)}) collective-permute-start(f32[576,128]{1,0:T(8,128)S(1)} %collective-permute-done.7.ta), channel_id=1, source_target_pairs={{0,1},{1,0},{2,3},{3,2},{4,5},{5,4},{6,7},{7,6},{8,9},{9,8},{10,11... | collective-permute-start | bytes 884744 | tf_op jit(solution)/shard_map/ppermute | solution.py:388
  44.8 4.5 %square.1 = (f32[512,512]{1,0:T(8,128)S(1)}, f32[512,512]{1,0:T(8,128)S(1)}, bf16[512,512]{1,0:T(8,128)(2,1)S(1)}, bf16[512,512]{1,0:T(8,128)(2,1)S(1)}, f32[512,512]{1,0:T(8,128)S(1)}, /*index=5*/f32[1,128]{1,0:T(1,128)S(1)}) custom-call(s32[76]{0:T(128)S(1)} %concatenate.3.s_ref, f32[1024,128]{1,0:T(8,128)S(1)} %get-tuple-element.22.refs_0_, ...), custom_call_target="tpu_custom_call" | custom-call | tf_op jit(solution)/shard_map/square/pallas_call | solution.py:426
  49.3 4.9 %second.1 = (f32[2,512,128]{2,1,0:T(8,128)S(1)}, f32[512,128]{1,0:T(8,128)S(1)}, f32[96,128]{1,0:T(8,128)S(1)}) custom-call(s32[76]{0:T(128)S(1)} %concatenate.3.s_ref, f32[512,512]{1,0:T(8,128)S(1)} %get-tuple-element.24.p1_ref, f32[512,512]{1,0:T(8,128)S(1)} %get-tuple-element.25.v_ref, bf16[512,512]{1,0:T(8,128)(2,1)S(1)} %get-tuple-element.26.vh_ref, ...), custom_call_target="tpu_custom_call" | custom-call | tf_op jit(solution)/shard_map/second/pallas_call | solution.py:443
  54.2 1.9 %collective-permute-start.10 = (f32[512,128]{1,0:T(8,128)S(1)}, f32[512,128]{1,0:T(8,128)S(1)}, u32[]{:S(2)}, u32[]{:S(2)}) collective-permute-start(f32[512,128]{1,0:T(8,128)S(1)} %get-tuple-element.32), channel_id=1, source_target_pairs={{0,7},{1,6},{2,5},{3,4},{4,3},{5,2},{6,1},{7,0},{8,15},{9,14},{10,... | collective-permute-start | bytes 786440 | tf_op jit(solution)/shard_map/ppermute | solution.py:459
  56.1 0.7 collective-permute-start.9
  56.8 35.9 %all_to_all.11 = f32[96,1,128]{2,1,0:T(1,128)S(1)} all-to-all(f32[96,1,128]{2,1,0:T(1,128)S(1)} %bitcast.13), channel_id=1, replica_groups=mesh['row'=96,'col'=8] {'row'}, dimensions={0} | all-to-all | bytes 98304 | tf_op jit(solution)/shard_map/all_to_all | solution.py:460
  92.7 1.5 %last.1 = (f32[8,2,64,64]{3,2,1,0:T(8,128)}, f32[2]{0:T(128)}) custom-call(s32[76]{0:T(128)S(1)} %concatenate.3.s_ref, f32[2,512,128]{2,1,0:T(8,128)S(1)} %get-tuple-element.31.own_ref, f32[512,128]{1,0:T(8,128)S(1)} %collective-permute-done.9.far_ref, f32[512,128]{1,0:T(8,128)S(1)} %collective-permute-done.10.near_ref, f32[96,128]{1,0:T(8,128)S(1)} %bitcast.12), custom_call_target="tpu_custom_call" | custom-call | tf_op jit(solution)/shard_map/last/pallas_call | solution.py:461
  (15 shorter events, 0.1 us)
Async XLA Ops:
  0.6 1.0 %copy-start = (f32[8,2,64,64]{3,2,1,0:T(8,128)S(1)}, f32[8,2,64,64]{3,2,1,0:T(8,128)}, u32[]{:S(2)}) copy-start(f32[8,2,64,64]{3,2,1,0:T(8,128)} %v_ref.1) | copy-start | bytes 786436
  1.9 6.2 %collective-permute-start.1 = (f32[256,128]{1,0:T(8,128)S(1)}, f32[256,128]{1,0:T(8,128)S(1)}, u32[]{:S(2)}, u32[]{:S(2)}) collective-permute-start(f32[256,128]{1,0:T(8,128)S(1)} %get-tuple-element.20), channel_id=1, source_target_pairs={{4,2},{12,10},{20,18},{28,26},{36,34},{44,42},{52,50},{60,58},{68,... | collective-permute-start | bytes 393224 | tf_op jit(solution)/shard_map/ppermute | solution.py:403
  2.5 11.8 %collective-permute-start.2 = (f32[256,128]{1,0:T(8,128)S(1)}, f32[256,128]{1,0:T(8,128)S(1)}, u32[]{:S(2)}, u32[]{:S(2)}) collective-permute-start(f32[256,128]{1,0:T(8,128)S(1)} %get-tuple-element.20), channel_id=1, source_target_pairs={{4,0},{12,8},{20,16},{28,24},{36,32},{44,40},{52,48},{60,56},{68,6... | collective-permute-start | bytes 393224 | tf_op jit(solution)/shard_map/ppermute | solution.py:404
  3.2 11.2 %collective-permute-start = (f32[512,128]{1,0:T(8,128)S(1)}, f32[512,128]{1,0:T(8,128)S(1)}, u32[]{:S(2)}, u32[]{:S(2)}) collective-permute-start(f32[512,128]{1,0:T(8,128)S(1)} %get-tuple-element.18.own_ref), channel_id=1, source_target_pairs={{0,2},{1,3},{2,0},{3,1},{4,6},{5,7},{6,4},{7,5},{8,10},{9,11},{10,... | collective-permute-start | bytes 786440 | tf_op jit(solution)/shard_map/ppermute | solution.py:402
  7.3 0.7 copy-start.1
  8.0 6.2 %copy-start.2 = (s32[768]{0:T(1024)S(1)}, s32[768]{0:T(1024)}, u32[]{:S(2)}) copy-start(s32[768]{0:T(1024)} %param.4) | copy-start | bytes 9220
  8.0 32.3 %collective-permute-start.4 = (f32[448,128]{1,0:T(8,128)S(1)}, f32[448,128]{1,0:T(8,128)S(1)}, u32[]{:S(2)}, u32[]{:S(2)}) collective-permute-start(f32[448,128]{1,0:T(8,128)S(1)} %get-tuple-element.23), channel_id=1, source_target_pairs={{0,4},{1,5},{2,6},{3,7},{4,0},{5,1},{6,2},{7,3},{8,12},{9,13},{10,... | collective-permute-start | bytes 688136 | tf_op jit(solution)/shard_map/ppermute | solution.py:406
  12.3 28.1 %collective-permute-start.5 = (f32[448,128]{1,0:T(8,128)S(1)}, f32[448,128]{1,0:T(8,128)S(1)}, u32[]{:S(2)}, u32[]{:S(2)}) collective-permute-start(f32[448,128]{1,0:T(8,128)S(1)} %get-tuple-element.23), channel_id=1, source_target_pairs={{0,6},{1,7},{2,4},{3,5},{4,2},{5,3},{6,0},{7,1},{8,14},{9,15},{10,... | collective-permute-start | bytes 688136 | tf_op jit(solution)/shard_map/ppermute | solution.py:407
  15.0 27.3 %collective-permute-start.7 = (f32[576,128]{1,0:T(8,128)S(1)}, f32[576,128]{1,0:T(8,128)S(1)}, u32[]{:S(2)}, u32[]{:S(2)}) collective-permute-start(f32[576,128]{1,0:T(8,128)S(1)} %get-tuple-element.30), channel_id=1, source_target_pairs={{4,8},{5,9},{6,10},{7,11},{12,16},{13,17},{14,18},{15,19},{20,24},... | collective-permute-start | bytes 884744 | tf_op jit(solution)/shard_map/ppermute | solution.py:417
  15.7 29.0 %collective-permute-start.3 = (f32[1024,128]{1,0:T(8,128)S(1)}, f32[1024,128]{1,0:T(8,128)S(1)}, u32[]{:S(2)}, u32[]{:S(2)}) collective-permute-start(f32[1024,128]{1,0:T(8,128)S(1)} %get-tuple-element.22.refs_0_), channel_id=1, source_target_pairs={{0,1},{1,0},{2,3},{3,2},{4,5},{5,4},{6,7},{7,6},{8,9},{9,8},{10,11... | collective-permute-start | bytes 1572872 | tf_op jit(solution)/shard_map/ppermute | solution.py:388
  40.4 4.4 %collective-permute-start.6 = (f32[896,128]{1,0:T(8,128)S(1)}, f32[896,128]{1,0:T(8,128)S(1)}, u32[]{:S(2)}, u32[]{:S(2)}) collective-permute-start(f32[896,128]{1,0:T(8,128)S(1)} %join.1.refs_2_), channel_id=1, source_target_pairs={{0,1},{1,0},{2,3},{3,2},{4,5},{5,4},{6,7},{7,6},{8,9},{9,8},{10,11... | collective-permute-start | bytes 1376264 | tf_op jit(solution)/shard_map/ppermute | solution.py:388
  42.3 6.9 %collective-permute-start.8 = (f32[576,128]{1,0:T(8,128)S(1)}, f32[576,128]{1,0:T(8,128)S(1)}, u32[]{:S(2)}, u32[]{:S(2)}) collective-permute-start(f32[576,128]{1,0:T(8,128)S(1)} %collective-permute-done.7.ta), channel_id=1, source_target_pairs={{0,1},{1,0},{2,3},{3,2},{4,5},{5,4},{6,7},{7,6},{8,9},{9,8},{10,11... | collective-permute-start | bytes 884744 | tf_op jit(solution)/shard_map/ppermute | solution.py:388
  54.2 38.5 %collective-permute-start.10 = (f32[512,128]{1,0:T(8,128)S(1)}, f32[512,128]{1,0:T(8,128)S(1)}, u32[]{:S(2)}, u32[]{:S(2)}) collective-permute-start(f32[512,128]{1,0:T(8,128)S(1)} %get-tuple-element.32), channel_id=1, source_target_pairs={{0,7},{1,6},{2,5},{3,4},{4,3},{5,2},{6,1},{7,0},{8,15},{9,14},{10,... | collective-permute-start | bytes 786440 | tf_op jit(solution)/shard_map/ppermute | solution.py:459
  56.1 36.6 %collective-permute-start.9 = (f32[512,128]{1,0:T(8,128)S(1)}, f32[512,128]{1,0:T(8,128)S(1)}, u32[]{:S(2)}, u32[]{:S(2)}) collective-permute-start(f32[512,128]{1,0:T(8,128)S(1)} %get-tuple-element.32), channel_id=1, source_target_pairs={{7,8},{6,9},{5,10},{4,11},{15,16},{14,17},{13,18},{12,19},{23,24},... | collective-permute-start | bytes 786440 | tf_op jit(solution)/shard_map/ppermute | solution.py:458

commit v11 on v10

--- a/solution.py
+++ b/solution.py
@@ -99,8 +99,9 @@
     out_ref[N - B : 2 * (N - B), :] = second_ref[...]
 
 
-def triangle_kernel(s_ref, own_ref, near_ref, d1_ref, d2_ref, out_ref, both_ref, low, high):
-    odd, core, upper = (s_ref[0] & 1) == 1, s_ref[1], s_ref[3]
+def triangle_kernel(own_ref, near_ref, d1_ref, d2_ref, out_ref, both_ref, low, high):
+    col = lax.axis_index("col")
+    odd, core, upper = (col & 2) == 2, col & 1, lax.shift_right_logical(col, 2)
     both_ref[0:N, :] = own_ref[...]
     both_ref[N : 2 * N, :] = near_ref[...]
     low[...] = jnp.where(odd, near_ref[...], own_ref[...])
@@ -194,18 +195,28 @@
     def part(rows, cols):
         return rh[rows, cols], rl[rows, cols]
 
+    def gram(rows, cols):
+        high, low = part(rows, cols)
+        mixed = lax.dot_general(high, low, (NT, ((), ())), preferred_element_type=F32)
+        square = lax.dot_general(high, high, (NT, ((), ())), preferred_element_type=F32)
+        return square + (mixed + mixed.T)
+
     lo, hi = slice(0, 256), slice(256, 512)
     mid = slice(N, 2 * N)
     side = pl.ds(pl.multiple_of(2 * N * upper, 128), N)
     v_ref[...] = r_ref[:, side]
     vh_ref[...], vl_ref[...] = rh[:, side], rl[:, side]
-    pv_ref[...] = dot3(part(slice(None), mid), (vh_ref[...], vl_ref[...]), NN)
+    full = pl.ds(pl.multiple_of(256 * (1 - upper), 128), 256)
+    pv_ref[:, full] = dot3(part(slice(None), mid), (vh_ref[:, full], vl_ref[:, full]), NN)
+    tile = pl.ds(pl.multiple_of(256 * upper, 128), 256)
+    near = pl.ds(pl.multiple_of(N + 256 * upper, 128), 256)
+    pv_ref[:, tile] = dot3(part(slice(None), near), (vh_ref[tile, tile], vl_ref[tile, tile]), NN)
 
     p01 = dot3(part(lo, slice(256, 1280)), part(hi, slice(256, 1280)), NT)
-    p1_ref[lo, lo] = dot3(part(lo, slice(0, 1280)), part(lo, slice(0, 1280)), NT)
+    p1_ref[lo, lo] = gram(lo, slice(0, 1280))
     p1_ref[lo, hi] = p01
     p1_ref[hi, lo] = p01.T
-    p1_ref[hi, hi] = dot3(part(hi, slice(256, W)), part(hi, slice(256, W)), NT)
+    p1_ref[hi, hi] = gram(hi, slice(256, W))
     rules = Rules(s_ref, BR[0], H, H)
     for i in range(H):
         keep, pick = rules.strip(i)
@@ -377,18 +388,9 @@
 def per_device(rows, values, radius, branch):
     both = ("row", "col")
     row, col = lax.axis_index("row"), lax.axis_index("col")
-    pad = ((H, H),)
-    radii = lax.dynamic_slice(jnp.pad(radius, pad, constant_values=-1), (H * row,), (3 * H,))
-    flags = lax.dynamic_slice(jnp.pad(branch, ((0, 0),) + pad), (0, H * row), (2, 3 * H))
-    scalars = jnp.concatenate(
-        [jnp.stack([col // 2, col % 2, col, col // 4]).astype(jnp.int32), radii, flags[0], flags[1]]
-    )
 
     def swap(x):
         return lax.ppermute(x, "col", [(c, c ^ 1) for c in range(8)])
-
-    def to_rows(x, pairs):
-        return lax.ppermute(x, both, pairs)
 
     def index(r, c):
         return r * 8 + c
@@ -402,19 +404,26 @@
     near = lax.ppermute(packed, "col", [(c, c ^ 2) for c in range(8)])
     d1 = lax.ppermute(diag, "col", [(4, 2)])
     d2 = lax.ppermute(diag, "col", [(4, 0)])
-    cut, d1 = lax.optimization_barrier((cut, d1))
     cross = lax.ppermute(cut, "col", [(c, c ^ 4) for c in range(8)])
     far = lax.ppermute(cut, "col", [(c, c ^ 6) for c in range(8)])
     triangle, joined = call(
         triangle_kernel,
         out_shape=[shape(576, 128), shape(2 * N, 128)],
-        in_specs=[SMEM] + [VMEM] * 4,
+        in_specs=[VMEM] * 4,
         out_specs=[VMEM] * 2,
         scratch_shapes=[pltpu.VMEM((N, 128), F32)] * 2,
         mib=8, name="triangle",
-    )(scalars, packed, near, d1, d2)
+    )(packed, near, d1, d2)
     pairs = [(index(r, c + 4), index(r + 1, c)) for r, c in ends]
     ta = lax.ppermute(triangle, both, pairs + [(b, a) for a, b in pairs])
+    radius, branch, joined = lax.optimization_barrier((radius, branch, joined))
+    pad = ((H, H),)
+    radii = lax.dynamic_slice(jnp.pad(radius, pad, constant_values=-1), (H * row,), (3 * H,))
+    flags = lax.dynamic_slice(jnp.pad(branch, ((0, 0),) + pad), (0, H * row), (2, 3 * H))
+    scalars = jnp.concatenate(
+        [jnp.stack([col // 2, col % 2, col, col // 4]).astype(jnp.int32), radii, flags[0], flags[1]]
+    )
+    cross, scalars = lax.optimization_barrier((cross, scalars))
     joined2 = swap(joined)
     distant = call(
         join_kernel, out_shape=shape(2 * (N - B), 128), in_specs=[VMEM] * 2, out_specs=VMEM,

time: 94.7 us -> 97.6 us (1.031)
  the two profiles are of different devices: /device:TPU:1 before, /device:TPU:16 now
where the time goes in v11:
time: 97.6 us; the launch traced here: 97.1 us
  starting transfers between devices  41.4 us (42%)
  blocking collectives  38.7 us (40%)
  Pallas kernels  10.8 us (11%)
  waiting for transfers between devices  4.08 us (4%)
  local copies, waits for them, and re-layouts  1.3 us (1%)
    all_to_all x1, blocking collectives, per_device(): sums = lax.all_to_all(sums, 'row', 0, 0, tiled=True)  38.7 us
    ppermute x1, starting transfers between devices, per_device(): d1 = lax.ppermute(diag, 'col', [(4, 2)])  10.2 us
    ppermute x1, starting transfers between devices, per_device(): ta = lax.ppermute(triangle, both, pairs + [(b, a) for a, b in pairs])  9.59 us
    ppermute x3, starting transfers between devices, swap(): return lax.ppermute(x, 'col', [(c, c ^ 1) for c in range(8)])  6.22 us
    pallas_call x1, Pallas kernels, per_device(): call(second_kernel, out_shape=[shape(2, N, 128), shape(N, 128), shape(row...  4.94 us
    ppermute x1, starting transfers between devices, per_device(): far = lax.ppermute(share, both, pairs + [(b, a) for a, b in pairs])  4.89 us
    pallas_call x1, Pallas kernels, per_device(): call(square_kernel, out_shape=[shape(N, N), shape(N, N), jax.ShapeDtypeSt...  3.87 us
    ppermute x1, starting transfers between devices, per_device(): near = lax.ppermute(packed, 'col', [(c, c ^ 2) for c in range(8)])  3.42 us
  transfers between devices with their start and end apart: 11, of which 2 were waited for; matrix products, arithmetic and copies ran while one was open for 0% of the time, Pallas kernels for 4%

profile of v11, /device:TPU:16, one launch (start us, length us, event | category | flops | bytes accessed | tf_op | source)
XLA Modules:
  0.0 97.1 jit_solution(10591550265112562067)
XLA Ops:
  0.6 1.0 %copy-done = f32[8,2,64,64]{3,2,1,0:T(8,128)S(1)} copy-done((f32[8,2,64,64]{3,2,1,0:T(8,128)S(1)}, f32[8,2,64,64]{3,2,1,0:T(8,128)}, u32[]{:S(2)}) %copy-start) | copy-done | bytes 262168
  1.7 0.3 pack.1
  1.9 3.4 %collective-permute-start.1 = (f32[512,128]{1,0:T(8,128)S(1)}, f32[512,128]{1,0:T(8,128)S(1)}, u32[]{:S(2)}, u32[]{:S(2)}) collective-permute-start(f32[512,128]{1,0:T(8,128)S(1)} %get-tuple-element.22.own_ref), channel_id=1, source_target_pairs={{0,2},{1,3},{2,0},{3,1},{4,6},{5,7},{6,4},{7,5},{8,10},{9,11},{10,... | collective-permute-start | bytes 786440 | tf_op jit(solution)/shard_map/ppermute | solution.py:404
  5.4 10.2 %collective-permute-start.2 = (f32[256,128]{1,0:T(8,128)S(1)}, f32[256,128]{1,0:T(8,128)S(1)}, u32[]{:S(2)}, u32[]{:S(2)}) collective-permute-start(f32[256,128]{1,0:T(8,128)S(1)} %get-tuple-element.23), channel_id=1, source_target_pairs={{4,2},{12,10},{20,18},{28,26},{36,34},{44,42},{52,50},{60,58},{68,... | collective-permute-start | bytes 393224 | tf_op jit(solution)/shard_map/ppermute | solution.py:405
  15.6 1.3 %collective-permute-start.3 = (f32[256,128]{1,0:T(8,128)S(1)}, f32[256,128]{1,0:T(8,128)S(1)}, u32[]{:S(2)}, u32[]{:S(2)}) collective-permute-start(f32[256,128]{1,0:T(8,128)S(1)} %get-tuple-element.23), channel_id=1, source_target_pairs={{4,0},{12,8},{20,16},{28,24},{36,32},{44,40},{52,48},{60,56},{68,6... | collective-permute-start | bytes 393224 | tf_op jit(solution)/shard_map/ppermute | solution.py:406
  16.9 1.9 %collective-permute-start = (f32[448,128]{1,0:T(8,128)S(1)}, f32[448,128]{1,0:T(8,128)S(1)}, u32[]{:S(2)}, u32[]{:S(2)}) collective-permute-start(f32[448,128]{1,0:T(8,128)S(1)} %get-tuple-element.21), channel_id=1, source_target_pairs={{0,4},{1,5},{2,6},{3,7},{4,0},{5,1},{6,2},{7,3},{8,12},{9,13},{10,... | collective-permute-start | bytes 688136 | tf_op jit(solution)/shard_map/ppermute | solution.py:407
  18.8 1.9 %collective-permute-start.5 = (f32[448,128]{1,0:T(8,128)S(1)}, f32[448,128]{1,0:T(8,128)S(1)}, u32[]{:S(2)}, u32[]{:S(2)}) collective-permute-start(f32[448,128]{1,0:T(8,128)S(1)} %get-tuple-element.21), channel_id=1, source_target_pairs={{0,6},{1,7},{2,4},{3,5},{4,2},{5,3},{6,0},{7,1},{8,14},{9,15},{10,... | collective-permute-start | bytes 688136 | tf_op jit(solution)/shard_map/ppermute | solution.py:408
  20.8 1.4 %collective-permute-done.3.d2_ref = f32[256,128]{1,0:T(8,128)S(1)} collective-permute-done((f32[256,128]{1,0:T(8,128)S(1)}, f32[256,128]{1,0:T(8,128)S(1)}, u32[]{:S(2)}, u32[]{:S(2)}) %collective-permute-start.3) | collective-permute-done | bytes 131104 | tf_op jit(solution)/shard_map/ppermute | solution.py:406
  22.2 0.1 triangle.1
  22.3 9.6 %collective-permute-start.7 = (f32[576,128]{1,0:T(8,128)S(1)}, f32[576,128]{1,0:T(8,128)S(1)}, u32[]{:S(2)}, u32[]{:S(2)}) collective-permute-start(f32[576,128]{1,0:T(8,128)S(1)} %get-tuple-element.36), channel_id=1, source_target_pairs={{4,8},{5,9},{6,10},{7,11},{12,16},{13,17},{14,18},{15,19},{20,24},... | collective-permute-start | bytes 884744 | tf_op jit(solution)/shard_map/ppermute | solution.py:418
  31.9 0.1 pad_dynamic-slice_fusion
  32.0 1.9 %collective-permute-start.4 = (f32[1024,128]{1,0:T(8,128)S(1)}, f32[1024,128]{1,0:T(8,128)S(1)}, u32[]{:S(2)}, u32[]{:S(2)}) collective-permute-start(f32[1024,128]{1,0:T(8,128)S(1)} %get-tuple-element.28.refs_0_), channel_id=1, source_target_pairs={{0,1},{1,0},{2,3},{3,2},{4,5},{5,4},{6,7},{7,6},{8,9},{9,8},{10,11... | collective-permute-start | bytes 1572872 | tf_op jit(solution)/shard_map/ppermute | solution.py:393
  34.0 0.1 pad_dynamic-slice_fusion.1
  34.0 0.1 concatenate.3.s_ref
  34.1 0.0 collective-permute-done.5.second_ref
  34.2 2.4 %collective-permute-start.6 = (f32[896,128]{1,0:T(8,128)S(1)}, f32[896,128]{1,0:T(8,128)S(1)}, u32[]{:S(2)}, u32[]{:S(2)}) collective-permute-start(f32[896,128]{1,0:T(8,128)S(1)} %join.1.refs_2_), channel_id=1, source_target_pairs={{0,1},{1,0},{2,3},{3,2},{4,5},{5,4},{6,7},{7,6},{8,9},{9,8},{10,11... | collective-permute-start | bytes 1376264 | tf_op jit(solution)/shard_map/ppermute | solution.py:393
  36.6 2.7 %collective-permute-done.7.ta = f32[576,128]{1,0:T(8,128)S(1)} collective-permute-done((f32[576,128]{1,0:T(8,128)S(1)}, f32[576,128]{1,0:T(8,128)S(1)}, u32[]{:S(2)}, u32[]{:S(2)}) %collective-permute-start.7) | collective-permute-done | bytes 294944 | tf_op jit(solution)/shard_map/ppermute | solution.py:418
  39.3 1.9 %collective-permute-start.8 = (f32[576,128]{1,0:T(8,128)S(1)}, f32[576,128]{1,0:T(8,128)S(1)}, u32[]{:S(2)}, u32[]{:S(2)}) collective-permute-start(f32[576,128]{1,0:T(8,128)S(1)} %collective-permute-done.7.ta), channel_id=1, source_target_pairs={{0,1},{1,0},{2,3},{3,2},{4,5},{5,4},{6,7},{7,6},{8,9},{9,8},{10,11... | collective-permute-start | bytes 884744 | tf_op jit(solution)/shard_map/ppermute | solution.py:393
  41.2 3.9 %square.1 = (f32[512,512]{1,0:T(8,128)S(1)}, f32[512,512]{1,0:T(8,128)S(1)}, bf16[512,512]{1,0:T(8,128)(2,1)S(1)}, bf16[512,512]{1,0:T(8,128)(2,1)S(1)}, f32[512,512]{1,0:T(8,128)S(1)}, /*index=5*/f32[1,128]{1,0:T(1,128)S(1)}) custom-call(s32[76]{0:T(128)S(1)} %concatenate.3.s_ref, f32[1024,128]{1,0:T(8,128)S(1)} %get-tuple-element.28.refs_0_, ...), custom_call_target="tpu_custom_call" | custom-call | tf_op jit(solution)/shard_map/square/pallas_call | solution.py:435
  45.1 4.9 %second.1 = (f32[2,512,128]{2,1,0:T(8,128)S(1)}, f32[512,128]{1,0:T(8,128)S(1)}, f32[96,128]{1,0:T(8,128)S(1)}) custom-call(s32[76]{0:T(128)S(1)} %concatenate.3.s_ref, f32[512,512]{1,0:T(8,128)S(1)} %get-tuple-element.30.p1_ref, f32[512,512]{1,0:T(8,128)S(1)} %get-tuple-element.31.v_ref, bf16[512,512]{1,0:T(8,128)(2,1)S(1)} %get-tuple-element.32.vh_ref, ...), custom_call_target="tpu_custom_call" | custom-call | tf_op jit(solution)/shard_map/second/pallas_call | solution.py:452
  50.1 1.9 %collective-permute-start.10 = (f32[512,128]{1,0:T(8,128)S(1)}, f32[512,128]{1,0:T(8,128)S(1)}, u32[]{:S(2)}, u32[]{:S(2)}) collective-permute-start(f32[512,128]{1,0:T(8,128)S(1)} %get-tuple-element.38), channel_id=1, source_target_pairs={{0,7},{1,6},{2,5},{3,4},{4,3},{5,2},{6,1},{7,0},{8,15},{9,14},{10,... | collective-permute-start | bytes 786440 | tf_op jit(solution)/shard_map/ppermute | solution.py:468
  52.0 4.9 %collective-permute-start.9 = (f32[512,128]{1,0:T(8,128)S(1)}, f32[512,128]{1,0:T(8,128)S(1)}, u32[]{:S(2)}, u32[]{:S(2)}) collective-permute-start(f32[512,128]{1,0:T(8,128)S(1)} %get-tuple-element.38), channel_id=1, source_target_pairs={{7,8},{6,9},{5,10},{4,11},{15,16},{14,17},{13,18},{12,19},{23,24},... | collective-permute-start | bytes 786440 | tf_op jit(solution)/shard_map/ppermute | solution.py:467
  56.9 38.7 %all_to_all.11 = f32[96,1,128]{2,1,0:T(1,128)S(1)} all-to-all(f32[96,1,128]{2,1,0:T(1,128)S(1)} %bitcast.13), channel_id=1, replica_groups=mesh['row'=96,'col'=8] {'row'}, dimensions={0} | all-to-all | bytes 98304 | tf_op jit(solution)/shard_map/all_to_all | solution.py:469
  95.6 1.5 %last.1 = (f32[8,2,64,64]{3,2,1,0:T(8,128)}, f32[2]{0:T(128)}) custom-call(s32[76]{0:T(128)S(1)} %concatenate.3.s_ref, f32[2,512,128]{2,1,0:T(8,128)S(1)} %get-tuple-element.37.own_ref, f32[512,128]{1,0:T(8,128)S(1)} %collective-permute-done.9.far_ref, f32[512,128]{1,0:T(8,128)S(1)} %collective-permute-done.10.near_ref, f32[96,128]{1,0:T(8,128)S(1)} %bitcast.12), custom_call_target="tpu_custom_call" | custom-call | tf_op jit(solution)/shard_map/last/pallas_call | solution.py:470
  (15 shorter events, 0.1 us)
Async XLA Ops:
  0.6 1.0 %copy-start = (f32[8,2,64,64]{3,2,1,0:T(8,128)S(1)}, f32[8,2,64,64]{3,2,1,0:T(8,128)}, u32[]{:S(2)}) copy-start(f32[8,2,64,64]{3,2,1,0:T(8,128)} %v_ref.1) | copy-start | bytes 786436
  1.9 20.3 %collective-permute-start.1 = (f32[512,128]{1,0:T(8,128)S(1)}, f32[512,128]{1,0:T(8,128)S(1)}, u32[]{:S(2)}, u32[]{:S(2)}) collective-permute-start(f32[512,128]{1,0:T(8,128)S(1)} %get-tuple-element.22.own_ref), channel_id=1, source_target_pairs={{0,2},{1,3},{2,0},{3,1},{4,6},{5,7},{6,4},{7,5},{8,10},{9,11},{10,... | collective-permute-start | bytes 786440 | tf_op jit(solution)/shard_map/ppermute | solution.py:404
  5.4 15.4 %collective-permute-start.2 = (f32[256,128]{1,0:T(8,128)S(1)}, f32[256,128]{1,0:T(8,128)S(1)}, u32[]{:S(2)}, u32[]{:S(2)}) collective-permute-start(f32[256,128]{1,0:T(8,128)S(1)} %get-tuple-element.23), channel_id=1, source_target_pairs={{4,2},{12,10},{20,18},{28,26},{36,34},{44,42},{52,50},{60,58},{68,... | collective-permute-start | bytes 393224 | tf_op jit(solution)/shard_map/ppermute | solution.py:405
  15.6 6.6 %collective-permute-start.3 = (f32[256,128]{1,0:T(8,128)S(1)}, f32[256,128]{1,0:T(8,128)S(1)}, u32[]{:S(2)}, u32[]{:S(2)}) collective-permute-start(f32[256,128]{1,0:T(8,128)S(1)} %get-tuple-element.23), channel_id=1, source_target_pairs={{4,0},{12,8},{20,16},{28,24},{36,32},{44,40},{52,48},{60,56},{68,6... | collective-permute-start | bytes 393224 | tf_op jit(solution)/shard_map/ppermute | solution.py:406
  16.9 17.2 %collective-permute-start = (f32[448,128]{1,0:T(8,128)S(1)}, f32[448,128]{1,0:T(8,128)S(1)}, u32[]{:S(2)}, u32[]{:S(2)}) collective-permute-start(f32[448,128]{1,0:T(8,128)S(1)} %get-tuple-element.21), channel_id=1, source_target_pairs={{0,4},{1,5},{2,6},{3,7},{4,0},{5,1},{6,2},{7,3},{8,12},{9,13},{10,... | collective-permute-start | bytes 688136 | tf_op jit(solution)/shard_map/ppermute | solution.py:407
  18.8 15.3 %collective-permute-start.5 = (f32[448,128]{1,0:T(8,128)S(1)}, f32[448,128]{1,0:T(8,128)S(1)}, u32[]{:S(2)}, u32[]{:S(2)}) collective-permute-start(f32[448,128]{1,0:T(8,128)S(1)} %get-tuple-element.21), channel_id=1, source_target_pairs={{0,6},{1,7},{2,4},{3,5},{4,2},{5,3},{6,0},{7,1},{8,14},{9,15},{10,... | collective-permute-start | bytes 688136 | tf_op jit(solution)/shard_map/ppermute | solution.py:408
  22.2 9.7 %copy-start.1 = (s32[2,768]{1,0:T(2,128)S(1)}, s32[2,768]{1,0:T(2,128)}, u32[]{:S(2)}) copy-start(s32[2,768]{1,0:T(2,128)} %param.5) | copy-start | bytes 18436
  22.3 11.6 %copy-start.2 = (s32[768]{0:T(1024)S(1)}, s32[768]{0:T(1024)}, u32[]{:S(2)}) copy-start(s32[768]{0:T(1024)} %param.4) | copy-start | bytes 9220
  22.3 17.0 %collective-permute-start.7 = (f32[576,128]{1,0:T(8,128)S(1)}, f32[576,128]{1,0:T(8,128)S(1)}, u32[]{:S(2)}, u32[]{:S(2)}) collective-permute-start(f32[576,128]{1,0:T(8,128)S(1)} %get-tuple-element.36), channel_id=1, source_target_pairs={{4,8},{5,9},{6,10},{7,11},{12,16},{13,17},{14,18},{15,19},{20,24},... | collective-permute-start | bytes 884744 | tf_op jit(solution)/shard_map/ppermute | solution.py:418
  32.0 9.2 %collective-permute-start.4 = (f32[1024,128]{1,0:T(8,128)S(1)}, f32[1024,128]{1,0:T(8,128)S(1)}, u32[]{:S(2)}, u32[]{:S(2)}) collective-permute-start(f32[1024,128]{1,0:T(8,128)S(1)} %get-tuple-element.28.refs_0_), channel_id=1, source_target_pairs={{0,1},{1,0},{2,3},{3,2},{4,5},{5,4},{6,7},{7,6},{8,9},{9,8},{10,11... | collective-permute-start | bytes 1572872 | tf_op jit(solution)/shard_map/ppermute | solution.py:393
  34.2 7.0 %collective-permute-start.6 = (f32[896,128]{1,0:T(8,128)S(1)}, f32[896,128]{1,0:T(8,128)S(1)}, u32[]{:S(2)}, u32[]{:S(2)}) collective-permute-start(f32[896,128]{1,0:T(8,128)S(1)} %join.1.refs_2_), channel_id=1, source_target_pairs={{0,1},{1,0},{2,3},{3,2},{4,5},{5,4},{6,7},{7,6},{8,9},{9,8},{10,11... | collective-permute-start | bytes 1376264 | tf_op jit(solution)/shard_map/ppermute | solution.py:393
  39.3 5.8 %collective-permute-start.8 = (f32[576,128]{1,0:T(8,128)S(1)}, f32[576,128]{1,0:T(8,128)S(1)}, u32[]{:S(2)}, u32[]{:S(2)}) collective-permute-start(f32[576,128]{1,0:T(8,128)S(1)} %collective-permute-done.7.ta), channel_id=1, source_target_pairs={{0,1},{1,0},{2,3},{3,2},{4,5},{5,4},{6,7},{7,6},{8,9},{9,8},{10,11... | collective-permute-start | bytes 884744 | tf_op jit(solution)/shard_map/ppermute | solution.py:393
  50.1 45.5 %collective-permute-start.10 = (f32[512,128]{1,0:T(8,128)S(1)}, f32[512,128]{1,0:T(8,128)S(1)}, u32[]{:S(2)}, u32[]{:S(2)}) collective-permute-start(f32[512,128]{1,0:T(8,128)S(1)} %get-tuple-element.38), channel_id=1, source_target_pairs={{0,7},{1,6},{2,5},{3,4},{4,3},{5,2},{6,1},{7,0},{8,15},{9,14},{10,... | collective-permute-start | bytes 786440 | tf_op jit(solution)/shard_map/ppermute | solution.py:468
  52.0 43.6 %collective-permute-start.9 = (f32[512,128]{1,0:T(8,128)S(1)}, f32[512,128]{1,0:T(8,128)S(1)}, u32[]{:S(2)}, u32[]{:S(2)}) collective-permute-start(f32[512,128]{1,0:T(8,128)S(1)} %get-tuple-element.38), channel_id=1, source_target_pairs={{7,8},{6,9},{5,10},{4,11},{15,16},{14,17},{13,18},{12,19},{23,24},... | collective-permute-start | bytes 786440 | tf_op jit(solution)/shard_map/ppermute | solution.py:467

commit v12 on v10

--- a/solution.py
+++ b/solution.py
@@ -194,18 +194,28 @@
     def part(rows, cols):
         return rh[rows, cols], rl[rows, cols]
 
+    def gram(rows, cols):
+        high, low = part(rows, cols)
+        mixed = lax.dot_general(high, low, (NT, ((), ())), preferred_element_type=F32)
+        square = lax.dot_general(high, high, (NT, ((), ())), preferred_element_type=F32)
+        return square + (mixed + mixed.T)
+
     lo, hi = slice(0, 256), slice(256, 512)
     mid = slice(N, 2 * N)
     side = pl.ds(pl.multiple_of(2 * N * upper, 128), N)
     v_ref[...] = r_ref[:, side]
     vh_ref[...], vl_ref[...] = rh[:, side], rl[:, side]
-    pv_ref[...] = dot3(part(slice(None), mid), (vh_ref[...], vl_ref[...]), NN)
+    full = pl.ds(pl.multiple_of(256 * (1 - upper), 128), 256)
+    pv_ref[:, full] = dot3(part(slice(None), mid), (vh_ref[:, full], vl_ref[:, full]), NN)
+    tile = pl.ds(pl.multiple_of(256 * upper, 128), 256)
+    near = pl.ds(pl.multiple_of(N + 256 * upper, 128), 256)
+    pv_ref[:, tile] = dot3(part(slice(None), near), (vh_ref[tile, tile], vl_ref[tile, tile]), NN)
 
     p01 = dot3(part(lo, slice(256, 1280)), part(hi, slice(256, 1280)), NT)
-    p1_ref[lo, lo] = dot3(part(lo, slice(0, 1280)), part(lo, slice(0, 1280)), NT)
+    p1_ref[lo, lo] = gram(lo, slice(0, 1280))
     p1_ref[lo, hi] = p01
     p1_ref[hi, lo] = p01.T
-    p1_ref[hi, hi] = dot3(part(hi, slice(256, W)), part(hi, slice(256, W)), NT)
+    p1_ref[hi, hi] = gram(hi, slice(256, W))
     rules = Rules(s_ref, BR[0], H, H)
     for i in range(H):
         keep, pick = rules.strip(i)

time: 94.7 us -> 94.2 us (level)
  no operation moved by 1% of the time
where the time goes in v12:
time: 94.2 us; the launch traced here: 93.7 us
  starting transfers between devices  43.7 us (46%)
  blocking collectives  35.9 us (38%)
  Pallas kernels  11.2 us (12%)
  local copies, waits for them, and re-layouts  1.96 us (2%)
    all_to_all x1, blocking collectives, per_device(): sums = lax.all_to_all(sums, 'row', 0, 0, tiled=True)  35.9 us
    ppermute x3, starting transfers between devices, swap(): return lax.ppermute(x, 'col', [(c, c ^ 1) for c in range(8)])  28.9 us
    pallas_call x1, Pallas kernels, per_device(): call(second_kernel, out_shape=[shape(2, N, 128), shape(N, 128), shape(row...  4.92 us
    ppermute x1, starting transfers between devices, per_device(): cross = lax.ppermute(cut, 'col', [(c, c ^ 4) for c in range(8)])  4.23 us
    ppermute x1, starting transfers between devices, per_device(): near = lax.ppermute(packed, 'col', [(c, c ^ 2) for c in range(8)])  4.03 us
    pallas_call x1, Pallas kernels, per_device(): call(square_kernel, out_shape=[shape(N, N), shape(N, N), jax.ShapeDtypeSt...  3.93 us
    ppermute x1, starting transfers between devices, per_device(): far = lax.ppermute(cut, 'col', [(c, c ^ 6) for c in range(8)])  1.92 us
    ppermute x1, starting transfers between devices, per_device(): near = lax.ppermute(share, 'col', [(c, 7 - c) for c in range(8)])  1.92 us
  transfers between devices with their start and end apart: 11, of which 0 were waited for; matrix products, arithmetic and copies ran while one was open for 0% of the time, Pallas kernels for 5%

profile of v12, /device:TPU:1, one launch (start us, length us, event | category | flops | bytes accessed | tf_op | source)
XLA Modules:
  0.0 93.7 jit_solution(13288453442128971724)
XLA Ops:
  0.6 1.0 %copy-done = f32[8,2,64,64]{3,2,1,0:T(8,128)S(1)} copy-done((f32[8,2,64,64]{3,2,1,0:T(8,128)S(1)}, f32[8,2,64,64]{3,2,1,0:T(8,128)}, u32[]{:S(2)}) %copy-start) | copy-done | bytes 262168
  1.7 0.2 pack.1
  1.9 0.7 collective-permute-start.1
  2.5 0.7 collective-permute-start.2
  3.2 4.0 %collective-permute-start = (f32[512,128]{1,0:T(8,128)S(1)}, f32[512,128]{1,0:T(8,128)S(1)}, u32[]{:S(2)}, u32[]{:S(2)}) collective-permute-start(f32[512,128]{1,0:T(8,128)S(1)} %get-tuple-element.18.own_ref), channel_id=1, source_target_pairs={{0,2},{1,3},{2,0},{3,1},{4,6},{5,7},{6,4},{7,5},{8,10},{9,11},{10,... | collective-permute-start | bytes 786440 | tf_op jit(solution)/shard_map/ppermute | solution.py:412
  7.3 0.0 copy-start.1
  7.3 0.7 copy-done.1
  8.0 0.1 pad_dynamic-slice_fusion
  8.0 4.2 %collective-permute-start.4 = (f32[448,128]{1,0:T(8,128)S(1)}, f32[448,128]{1,0:T(8,128)S(1)}, u32[]{:S(2)}, u32[]{:S(2)}) collective-permute-start(f32[448,128]{1,0:T(8,128)S(1)} %get-tuple-element.23), channel_id=1, source_target_pairs={{0,4},{1,5},{2,6},{3,7},{4,0},{5,1},{6,2},{7,3},{8,12},{9,13},{10,... | collective-permute-start | bytes 688136 | tf_op jit(solution)/shard_map/ppermute | solution.py:416
  12.3 1.9 %collective-permute-start.5 = (f32[448,128]{1,0:T(8,128)S(1)}, f32[448,128]{1,0:T(8,128)S(1)}, u32[]{:S(2)}, u32[]{:S(2)}) collective-permute-start(f32[448,128]{1,0:T(8,128)S(1)} %get-tuple-element.23), channel_id=1, source_target_pairs={{0,6},{1,7},{2,4},{3,5},{4,2},{5,3},{6,0},{7,1},{8,14},{9,15},{10,... | collective-permute-start | bytes 688136 | tf_op jit(solution)/shard_map/ppermute | solution.py:417
  14.2 0.1 pad_dynamic-slice_fusion.1
  14.3 0.1 concatenate.3.s_ref
  14.4 0.0 collective-permute-done.near_ref
  14.4 0.6 triangle.1
  15.0 0.7 collective-permute-start.7
  15.7 24.6 %collective-permute-start.3 = (f32[1024,128]{1,0:T(8,128)S(1)}, f32[1024,128]{1,0:T(8,128)S(1)}, u32[]{:S(2)}, u32[]{:S(2)}) collective-permute-start(f32[1024,128]{1,0:T(8,128)S(1)} %get-tuple-element.22.refs_0_), channel_id=1, source_target_pairs={{0,1},{1,0},{2,3},{3,2},{4,5},{5,4},{6,7},{7,6},{8,9},{9,8},{10,11... | collective-permute-start | bytes 1572872 | tf_op jit(solution)/shard_map/ppermute | solution.py:398
  40.4 1.9 %collective-permute-start.6 = (f32[896,128]{1,0:T(8,128)S(1)}, f32[896,128]{1,0:T(8,128)S(1)}, u32[]{:S(2)}, u32[]{:S(2)}) collective-permute-start(f32[896,128]{1,0:T(8,128)S(1)} %join.1.refs_2_), channel_id=1, source_target_pairs={{0,1},{1,0},{2,3},{3,2},{4,5},{5,4},{6,7},{7,6},{8,9},{9,8},{10,11... | collective-permute-start | bytes 1376264 | tf_op jit(solution)/shard_map/ppermute | solution.py:398
  42.3 2.4 %collective-permute-start.8 = (f32[576,128]{1,0:T(8,128)S(1)}, f32[576,128]{1,0:T(8,128)S(1)}, u32[]{:S(2)}, u32[]{:S(2)}) collective-permute-start(f32[576,128]{1,0:T(8,128)S(1)} %collective-permute-done.7.ta), channel_id=1, source_target_pairs={{0,1},{1,0},{2,3},{3,2},{4,5},{5,4},{6,7},{7,6},{8,9},{9,8},{10,11... | collective-permute-start | bytes 884744 | tf_op jit(solution)/shard_map/ppermute | solution.py:398
  44.8 3.9 %square.1 = (f32[512,512]{1,0:T(8,128)S(1)}, f32[512,512]{1,0:T(8,128)S(1)}, bf16[512,512]{1,0:T(8,128)(2,1)S(1)}, bf16[512,512]{1,0:T(8,128)(2,1)S(1)}, f32[512,512]{1,0:T(8,128)S(1)}, /*index=5*/f32[1,128]{1,0:T(1,128)S(1)}) custom-call(s32[76]{0:T(128)S(1)} %concatenate.3.s_ref, f32[1024,128]{1,0:T(8,128)S(1)} %get-tuple-element.22.refs_0_, ...), custom_call_target="tpu_custom_call" | custom-call | tf_op jit(solution)/shard_map/square/pallas_call | solution.py:436
  48.7 4.9 %second.1 = (f32[2,512,128]{2,1,0:T(8,128)S(1)}, f32[512,128]{1,0:T(8,128)S(1)}, f32[96,128]{1,0:T(8,128)S(1)}) custom-call(s32[76]{0:T(128)S(1)} %concatenate.3.s_ref, f32[512,512]{1,0:T(8,128)S(1)} %get-tuple-element.24.p1_ref, f32[512,512]{1,0:T(8,128)S(1)} %get-tuple-element.25.v_ref, bf16[512,512]{1,0:T(8,128)(2,1)S(1)} %get-tuple-element.26.vh_ref, ...), custom_call_target="tpu_custom_call" | custom-call | tf_op jit(solution)/shard_map/second/pallas_call | solution.py:453
  53.6 1.9 %collective-permute-start.10 = (f32[512,128]{1,0:T(8,128)S(1)}, f32[512,128]{1,0:T(8,128)S(1)}, u32[]{:S(2)}, u32[]{:S(2)}) collective-permute-start(f32[512,128]{1,0:T(8,128)S(1)} %get-tuple-element.32), channel_id=1, source_target_pairs={{0,7},{1,6},{2,5},{3,4},{4,3},{5,2},{6,1},{7,0},{8,15},{9,14},{10,... | collective-permute-start | bytes 786440 | tf_op jit(solution)/shard_map/ppermute | solution.py:469
  55.6 0.7 collective-permute-start.9
  56.2 35.9 %all_to_all.11 = f32[96,1,128]{2,1,0:T(1,128)S(1)} all-to-all(f32[96,1,128]{2,1,0:T(1,128)S(1)} %bitcast.13), channel_id=1, replica_groups=mesh['row'=96,'col'=8] {'row'}, dimensions={0} | all-to-all | bytes 98304 | tf_op jit(solution)/shard_map/all_to_all | solution.py:470
  92.2 1.5 %last.1 = (f32[8,2,64,64]{3,2,1,0:T(8,128)}, f32[2]{0:T(128)}) custom-call(s32[76]{0:T(128)S(1)} %concatenate.3.s_ref, f32[2,512,128]{2,1,0:T(8,128)S(1)} %get-tuple-element.31.own_ref, f32[512,128]{1,0:T(8,128)S(1)} %collective-permute-done.9.far_ref, f32[512,128]{1,0:T(8,128)S(1)} %collective-permute-done.10.near_ref, f32[96,128]{1,0:T(8,128)S(1)} %bitcast.12), custom_call_target="tpu_custom_call" | custom-call | tf_op jit(solution)/shard_map/last/pallas_call | solution.py:471
  (15 shorter events, 0.1 us)
Async XLA Ops:
  0.6 1.0 %copy-start = (f32[8,2,64,64]{3,2,1,0:T(8,128)S(1)}, f32[8,2,64,64]{3,2,1,0:T(8,128)}, u32[]{:S(2)}) copy-start(f32[8,2,64,64]{3,2,1,0:T(8,128)} %v_ref.1) | copy-start | bytes 786436
  1.9 6.2 %collective-permute-start.1 = (f32[256,128]{1,0:T(8,128)S(1)}, f32[256,128]{1,0:T(8,128)S(1)}, u32[]{:S(2)}, u32[]{:S(2)}) collective-permute-start(f32[256,128]{1,0:T(8,128)S(1)} %get-tuple-element.20), channel_id=1, source_target_pairs={{4,2},{12,10},{20,18},{28,26},{36,34},{44,42},{52,50},{60,58},{68,... | collective-permute-start | bytes 393224 | tf_op jit(solution)/shard_map/ppermute | solution.py:413
  2.5 11.8 %collective-permute-start.2 = (f32[256,128]{1,0:T(8,128)S(1)}, f32[256,128]{1,0:T(8,128)S(1)}, u32[]{:S(2)}, u32[]{:S(2)}) collective-permute-start(f32[256,128]{1,0:T(8,128)S(1)} %get-tuple-element.20), channel_id=1, source_target_pairs={{4,0},{12,8},{20,16},{28,24},{36,32},{44,40},{52,48},{60,56},{68,6... | collective-permute-start | bytes 393224 | tf_op jit(solution)/shard_map/ppermute | solution.py:414
  3.2 11.2 %collective-permute-start = (f32[512,128]{1,0:T(8,128)S(1)}, f32[512,128]{1,0:T(8,128)S(1)}, u32[]{:S(2)}, u32[]{:S(2)}) collective-permute-start(f32[512,128]{1,0:T(8,128)S(1)} %get-tuple-element.18.own_ref), channel_id=1, source_target_pairs={{0,2},{1,3},{2,0},{3,1},{4,6},{5,7},{6,4},{7,5},{8,10},{9,11},{10,... | collective-permute-start | bytes 786440 | tf_op jit(solution)/shard_map/ppermute | solution.py:412
  7.3 0.7 copy-start.1
  8.0 6.2 %copy-start.2 = (s32[768]{0:T(1024)S(1)}, s32[768]{0:T(1024)}, u32[]{:S(2)}) copy-start(s32[768]{0:T(1024)} %param.4) | copy-start | bytes 9220
  8.0 32.3 %collective-permute-start.4 = (f32[448,128]{1,0:T(8,128)S(1)}, f32[448,128]{1,0:T(8,128)S(1)}, u32[]{:S(2)}, u32[]{:S(2)}) collective-permute-start(f32[448,128]{1,0:T(8,128)S(1)} %get-tuple-element.23), channel_id=1, source_target_pairs={{0,4},{1,5},{2,6},{3,7},{4,0},{5,1},{6,2},{7,3},{8,12},{9,13},{10,... | collective-permute-start | bytes 688136 | tf_op jit(solution)/shard_map/ppermute | solution.py:416
  12.3 28.1 %collective-permute-start.5 = (f32[448,128]{1,0:T(8,128)S(1)}, f32[448,128]{1,0:T(8,128)S(1)}, u32[]{:S(2)}, u32[]{:S(2)}) collective-permute-start(f32[448,128]{1,0:T(8,128)S(1)} %get-tuple-element.23), channel_id=1, source_target_pairs={{0,6},{1,7},{2,4},{3,5},{4,2},{5,3},{6,0},{7,1},{8,14},{9,15},{10,... | collective-permute-start | bytes 688136 | tf_op jit(solution)/shard_map/ppermute | solution.py:417
  15.0 27.3 %collective-permute-start.7 = (f32[576,128]{1,0:T(8,128)S(1)}, f32[576,128]{1,0:T(8,128)S(1)}, u32[]{:S(2)}, u32[]{:S(2)}) collective-permute-start(f32[576,128]{1,0:T(8,128)S(1)} %get-tuple-element.30), channel_id=1, source_target_pairs={{4,8},{5,9},{6,10},{7,11},{12,16},{13,17},{14,18},{15,19},{20,24},... | collective-permute-start | bytes 884744 | tf_op jit(solution)/shard_map/ppermute | solution.py:427
  15.7 29.0 %collective-permute-start.3 = (f32[1024,128]{1,0:T(8,128)S(1)}, f32[1024,128]{1,0:T(8,128)S(1)}, u32[]{:S(2)}, u32[]{:S(2)}) collective-permute-start(f32[1024,128]{1,0:T(8,128)S(1)} %get-tuple-element.22.refs_0_), channel_id=1, source_target_pairs={{0,1},{1,0},{2,3},{3,2},{4,5},{5,4},{6,7},{7,6},{8,9},{9,8},{10,11... | collective-permute-start | bytes 1572872 | tf_op jit(solution)/shard_map/ppermute | solution.py:398
  40.4 4.4 %collective-permute-start.6 = (f32[896,128]{1,0:T(8,128)S(1)}, f32[896,128]{1,0:T(8,128)S(1)}, u32[]{:S(2)}, u32[]{:S(2)}) collective-permute-start(f32[896,128]{1,0:T(8,128)S(1)} %join.1.refs_2_), channel_id=1, source_target_pairs={{0,1},{1,0},{2,3},{3,2},{4,5},{5,4},{6,7},{7,6},{8,9},{9,8},{10,11... | collective-permute-start | bytes 1376264 | tf_op jit(solution)/shard_map/ppermute | solution.py:398
  42.3 6.4 %collective-permute-start.8 = (f32[576,128]{1,0:T(8,128)S(1)}, f32[576,128]{1,0:T(8,128)S(1)}, u32[]{:S(2)}, u32[]{:S(2)}) collective-permute-start(f32[576,128]{1,0:T(8,128)S(1)} %collective-permute-done.7.ta), channel_id=1, source_target_pairs={{0,1},{1,0},{2,3},{3,2},{4,5},{5,4},{6,7},{7,6},{8,9},{9,8},{10,11... | collective-permute-start | bytes 884744 | tf_op jit(solution)/shard_map/ppermute | solution.py:398
  53.6 38.5 %collective-permute-start.10 = (f32[512,128]{1,0:T(8,128)S(1)}, f32[512,128]{1,0:T(8,128)S(1)}, u32[]{:S(2)}, u32[]{:S(2)}) collective-permute-start(f32[512,128]{1,0:T(8,128)S(1)} %get-tuple-element.32), channel_id=1, source_target_pairs={{0,7},{1,6},{2,5},{3,4},{4,3},{5,2},{6,1},{7,0},{8,15},{9,14},{10,... | collective-permute-start | bytes 786440 | tf_op jit(solution)/shard_map/ppermute | solution.py:469
  55.6 36.6 %collective-permute-start.9 = (f32[512,128]{1,0:T(8,128)S(1)}, f32[512,128]{1,0:T(8,128)S(1)}, u32[]{:S(2)}, u32[]{:S(2)}) collective-permute-start(f32[512,128]{1,0:T(8,128)S(1)} %get-tuple-element.32), channel_id=1, source_target_pairs={{7,8},{6,9},{5,10},{4,11},{15,16},{14,17},{13,18},{12,19},{23,24},... | collective-permute-start | bytes 786440 | tf_op jit(solution)/shard_map/ppermute | solution.py:468
